TPU v7x, 128 devices: a whole 4x4x4 slice. The times are simulated.
128 devices in a mesh: row: 8 (over y, z_lo), col: 16 (over x, z_hi, core).
Axes of the slice: x: 4, y: 4, z: 4 (z_hi: 2, z_lo: 2; z = z_hi * 2 + z_lo), core: 2. Of those that a mesh axis runs over, the one named last changes fastest.
Arguments:
- picture_embedding_matrix: bfloat16 [20480, 1152], P(('row', 'col')), may hold values from -0.1875 to 0.1875
- caption_embedding_matrix: bfloat16 [20480, 1152], P(('row', 'col')), may hold values from -0.1875 to 0.1875
- matching_caption_indices: int32 [20480], P(('row', 'col')), may hold values from 0 to 20479, each once
- sharpness_factor: float32 [1], replicated, may hold values from 5 to 20
- additive_shift_term: float32 [1], replicated, may hold values from -4 to -1
Outputs:
- image_grad: float32 [20480, 1152], P(('row', 'col'))
- text_grad: float32 [20480, 1152], P(('row', 'col'))
Inputs may be any that keep to these rules, and one draw needn't show every extreme that they name: `matching_caption_indices`: it is a permutation: every text row is the positive of exactly one image row.
All inputs are finite; a program needn't handle non-finite values.
Results may differ from a plain program's by a relative error of at most 0.0052.
Values may be sent and summed in bfloat16 or wider, within the bound.
No kernel may reach another device: no remote copies, remote signals or barrier semaphores. Data moves between devices by JAX's collectives and lax.ppermute only.
A program may use at most 128 MiB of HBM per device.

v0:
```python
import math

import jax
import jax.numpy as jnp
from jax import lax
from jax.sharding import PartitionSpec as P


def normalize(raw):
    values = raw.astype(jnp.float32)
    inverse = lax.rsqrt(jnp.sum(values * values, axis=1, keepdims=True) + 1e-06)
    return (values * inverse, inverse)


def backward(unit_grad, unit, inverse):
    along = jnp.sum(unit * unit_grad, axis=1, keepdims=True)
    return inverse * (unit_grad - unit * along)


def shards(
    picture_embedding_matrix,
    caption_embedding_matrix,
    matching_caption_indices,
    sharpness_factor,
    additive_shift_term,
):
    local_entry_span = picture_embedding_matrix.shape[0]
    feature_width = picture_embedding_matrix.shape[1]
    col_devices = lax.axis_size("col")
    col_index = lax.axis_index("col")
    image_unit, image_inverse_norm = normalize(picture_embedding_matrix)
    text_unit, text_inverse = normalize(caption_embedding_matrix)
    image_half = image_unit.astype(jnp.bfloat16)
    text_half = text_unit.astype(jnp.bfloat16)
    multiplier_factor = sharpness_factor[0]
    bias_value = additive_shift_term[0]
    texts = lax.all_gather(text_half, "row", axis=0, tiled=True)
    text_count = texts.shape[0]
    positions = jnp.arange(text_count, dtype=jnp.int32)
    text_ids = (
        positions // local_entry_span * col_devices + col_index
    ) * local_entry_span + positions % local_entry_span
    image_all, labels_all = (
        lax.all_gather(image_half, "col", axis=0, tiled=True),
        lax.all_gather(matching_caption_indices, "col", axis=0, tiled=True),
    )
    piece_rows = image_all.shape[0]
    rows_per_block = math.gcd(piece_rows, 512)
    block_count = piece_rows // rows_per_block

    def accumulate(running, block_inputs):
        image_block, block_labels = block_inputs
        logits = (
            multiplier_factor * jnp.dot(image_block, texts.T, preferred_element_type=jnp.float32)
            + bias_value
        )
        signs = jnp.where(block_labels[:, None] == text_ids[None, :], 1.0, -1.0).astype(jnp.float32)
        coefficient = (-signs * jax.nn.sigmoid(-signs * logits)).astype(jnp.bfloat16)
        text_part = lax.dot_general(
            coefficient, image_block, (((0,), (0,)), ((), ())), preferred_element_type=jnp.float32
        )
        return (running + text_part, coefficient)

    opening_total = jnp.zeros((text_count, feature_width), jnp.float32)
    text_sum, pair_coefficients = lax.scan(
        accumulate,
        opening_total,
        (
            image_all.reshape(block_count, rows_per_block, feature_width),
            labels_all.reshape(block_count, rows_per_block),
        ),
    )
    pair_coefficients, text_partial = (pair_coefficients.reshape(piece_rows, text_count), text_sum)
    image_partial = jnp.dot(pair_coefficients, texts, preferred_element_type=jnp.float32)
    image_total = lax.psum_scatter(image_partial, "col", scatter_dimension=0, tiled=True)
    unit_image_grad = multiplier_factor * image_total
    unit_text_grad = multiplier_factor * lax.psum_scatter(
        text_partial, "row", scatter_dimension=0, tiled=True
    )
    return (
        backward(unit_image_grad, image_unit, image_inverse_norm),
        backward(unit_text_grad, text_unit, text_inverse),
    )


def solution(mesh):
    return jax.shard_map(
        shards,
        mesh=mesh,
        in_specs=(P(("row", "col"), None), P(("row", "col"), None), P(("row", "col")), P(), P()),
        out_specs=(P(("row", "col"), None), P(("row", "col"), None)),
        check_vma=False,
    )
```

profile of v0, /device:TPU:1, one launch (start us, length us, event | category | flops | bytes accessed | tf_op | source)
XLA Modules:
  0.0 473.4 jit_solution(4315063598524369675)
XLA Ops:
  7.2 1.1 fusion.40
  8.4 1.9 fusion.29
  11.5 1.9 fusion.32
  15.0 67.2 %all-reduce = s32[2560]{0:T(1024)S(1)} all-reduce(s32[2560]{0:T(1024)S(1)} %dynamic-update-slice), channel_id=1, replica_groups=mesh['row'=8,'col'=16] {'col'}, use_global_device_ids=true, to_apply=%add | all-reduce | flops 2560 | bytes 20480
  82.3 66.4 %all-gather.3.cloned.1.call-done = bf16[2560,1152]{1,0:T(8,128)(2,1)} async-done(((bf16[160,1152]{1,0:T(8,128)(2,1)}), bf16[2560,1152]{1,0:T(8,128)(2,1)}) %all-gather.3.cloned.1.call-update) | async-done | bytes 5898256 | tf_op jit(solution)/shard_map/all_gather | solution.py:44
  148.7 70.7 %while.13 = (s32[]{:T(128)}, f32[1280,1152]{1,0:T(8,128)}, bf16[5,512,1280]{2,1,0:T(8,128)(2,1)}, s32[5,512]{1,0:T(8,128)S(1)}, f32[]{:T(128)}, /*index=5*/bf16[...) while((s32[]{:T(128)}, f32[1280,1152]{1,0:T(8,128)}, ...), condition=%wide.region_3.4_spmd.clone, body=%wide.region_2.3_spmd.clone.sunk | while | flops 3030077440 | bytes 21056128 | solution.py:65
  148.7 7.0 %bitcast_dynamic-update-slice_fusion.2 = (bf16[5,512,1280]{2,1,0:T(8,128)(2,1)}, bf16[512,1280]{1,0:T(8,128)(2,1)S(1)}) fusion(bf16[5,512,1280]{2,1,0:T(8,128)(2,1)} %get-tuple-element.177, s32[]{:T(128)} %get-tuple-element.175, f32[]{:T(128)} %get-tuple-element.193, bf16[1280,1152]{1,0:T(8,128)(2,1)} %get-tuple-element.192, ...), kind=kOutput, calls=%fused_computation.11.clone.1 | convolution fusion | flops 1517158400 | bytes 6759424 | tf_op jit(solution)/shard_map/while/body/eval_jaxpr/dot_general | solution.py:54
  155.7 5.7 %convolution_add_fusion.2 = f32[1280,1152]{1,0:T(8,128)} fusion(bf16[512,1280]{1,0:T(8,128)(2,1)S(1)} %get-tuple-element.162, f32[1280,1152]{1,0:T(8,128)} %get-tuple-element.176, pred[]{:T(512)S(6)} %compare.3, bf16[5,512,1152]{2,1,0:T(8,128)(2,1)} %get-tuple-element.191, s32[]{:T(128)} %get-tuple-element.175), kind=kOutput, calls=%fused_computation.1.clone.1 | convolution fusion | flops 1512898560 | bytes 14287361 | tf_op jit(solution)/shard_map/while/body/eval_jaxpr/dot_general | solution.py:59
  161.5 7.0 %bitcast_dynamic-update-slice_fusion.2 = (bf16[5,512,1280]{2,1,0:T(8,128)(2,1)}, bf16[512,1280]{1,0:T(8,128)(2,1)S(1)}) fusion(bf16[5,512,1280]{2,1,0:T(8,128)(2,1)} %get-tuple-element.177, s32[]{:T(128)} %get-tuple-element.175, f32[]{:T(128)} %get-tuple-element.193, bf16[1280,1152]{1,0:T(8,128)(2,1)} %get-tuple-element.192, ...), kind=kOutput, calls=%fused_computation.11.clone.1 | convolution fusion | flops 1517158400 | bytes 6759424 | tf_op jit(solution)/shard_map/while/body/eval_jaxpr/dot_general | solution.py:54
  168.5 7.5 %convolution_add_fusion.2 = f32[1280,1152]{1,0:T(8,128)} fusion(bf16[512,1280]{1,0:T(8,128)(2,1)S(1)} %get-tuple-element.162, f32[1280,1152]{1,0:T(8,128)} %get-tuple-element.176, pred[]{:T(512)S(6)} %compare.3, bf16[5,512,1152]{2,1,0:T(8,128)(2,1)} %get-tuple-element.191, s32[]{:T(128)} %get-tuple-element.175), kind=kOutput, calls=%fused_computation.1.clone.1 | convolution fusion | flops 1512898560 | bytes 14287361 | tf_op jit(solution)/shard_map/while/body/eval_jaxpr/dot_general | solution.py:59
  176.0 7.0 %bitcast_dynamic-update-slice_fusion.2 = (bf16[5,512,1280]{2,1,0:T(8,128)(2,1)}, bf16[512,1280]{1,0:T(8,128)(2,1)S(1)}) fusion(bf16[5,512,1280]{2,1,0:T(8,128)(2,1)} %get-tuple-element.177, s32[]{:T(128)} %get-tuple-element.175, f32[]{:T(128)} %get-tuple-element.193, bf16[1280,1152]{1,0:T(8,128)(2,1)} %get-tuple-element.192, ...), kind=kOutput, calls=%fused_computation.11.clone.1 | convolution fusion | flops 1517158400 | bytes 6759424 | tf_op jit(solution)/shard_map/while/body/eval_jaxpr/dot_general | solution.py:54
  182.9 7.5 %convolution_add_fusion.2 = f32[1280,1152]{1,0:T(8,128)} fusion(bf16[512,1280]{1,0:T(8,128)(2,1)S(1)} %get-tuple-element.162, f32[1280,1152]{1,0:T(8,128)} %get-tuple-element.176, pred[]{:T(512)S(6)} %compare.3, bf16[5,512,1152]{2,1,0:T(8,128)(2,1)} %get-tuple-element.191, s32[]{:T(128)} %get-tuple-element.175), kind=kOutput, calls=%fused_computation.1.clone.1 | convolution fusion | flops 1512898560 | bytes 14287361 | tf_op jit(solution)/shard_map/while/body/eval_jaxpr/dot_general | solution.py:59
  190.4 7.0 %bitcast_dynamic-update-slice_fusion.2 = (bf16[5,512,1280]{2,1,0:T(8,128)(2,1)}, bf16[512,1280]{1,0:T(8,128)(2,1)S(1)}) fusion(bf16[5,512,1280]{2,1,0:T(8,128)(2,1)} %get-tuple-element.177, s32[]{:T(128)} %get-tuple-element.175, f32[]{:T(128)} %get-tuple-element.193, bf16[1280,1152]{1,0:T(8,128)(2,1)} %get-tuple-element.192, ...), kind=kOutput, calls=%fused_computation.11.clone.1 | convolution fusion | flops 1517158400 | bytes 6759424 | tf_op jit(solution)/shard_map/while/body/eval_jaxpr/dot_general | solution.py:54
  197.4 7.5 %convolution_add_fusion.2 = f32[1280,1152]{1,0:T(8,128)} fusion(bf16[512,1280]{1,0:T(8,128)(2,1)S(1)} %get-tuple-element.162, f32[1280,1152]{1,0:T(8,128)} %get-tuple-element.176, pred[]{:T(512)S(6)} %compare.3, bf16[5,512,1152]{2,1,0:T(8,128)(2,1)} %get-tuple-element.191, s32[]{:T(128)} %get-tuple-element.175), kind=kOutput, calls=%fused_computation.1.clone.1 | convolution fusion | flops 1512898560 | bytes 14287361 | tf_op jit(solution)/shard_map/while/body/eval_jaxpr/dot_general | solution.py:59
  204.9 7.0 %bitcast_dynamic-update-slice_fusion.2 = (bf16[5,512,1280]{2,1,0:T(8,128)(2,1)}, bf16[512,1280]{1,0:T(8,128)(2,1)S(1)}) fusion(bf16[5,512,1280]{2,1,0:T(8,128)(2,1)} %get-tuple-element.177, s32[]{:T(128)} %get-tuple-element.175, f32[]{:T(128)} %get-tuple-element.193, bf16[1280,1152]{1,0:T(8,128)(2,1)} %get-tuple-element.192, ...), kind=kOutput, calls=%fused_computation.11.clone.1 | convolution fusion | flops 1517158400 | bytes 6759424 | tf_op jit(solution)/shard_map/while/body/eval_jaxpr/dot_general | solution.py:54
  211.9 7.5 %convolution_add_fusion.2 = f32[1280,1152]{1,0:T(8,128)} fusion(bf16[512,1280]{1,0:T(8,128)(2,1)S(1)} %get-tuple-element.162, f32[1280,1152]{1,0:T(8,128)} %get-tuple-element.176, pred[]{:T(512)S(6)} %compare.3, bf16[5,512,1152]{2,1,0:T(8,128)(2,1)} %get-tuple-element.191, s32[]{:T(128)} %get-tuple-element.175), kind=kOutput, calls=%fused_computation.1.clone.1 | convolution fusion | flops 1512898560 | bytes 14287361 | tf_op jit(solution)/shard_map/while/body/eval_jaxpr/dot_general | solution.py:59
  219.5 1.8 copy-done.3
  221.2 13.5 %fusion.41 = f32[2560,1152]{1,0:T(8,128)} fusion(bf16[2560,1280]{1,0:T(8,128)(2,1)} %bitcast.37, bf16[1280,1152]{1,0:T(8,128)(2,1)S(1)} %copy-done.3), kind=kOutput, calls=%fused_computation.54 | convolution fusion | flops 7549747200 | bytes 21299200 | tf_op jit(solution)/shard_map/dot_general | solution.py:74
  235.4 104.6 %reduce-scatter.5.cloned.1.call-done = f32[160,1152]{1,0:T(8,128)} async-done(((f32[1280,1152]{1,0:T(8,128)}), f32[160,1152]{1,0:T(8,128)}) %reduce-scatter.5.cloned.1.call-update) | async-done | bytes 737296 | tf_op jit(solution)/shard_map/reduce_scatter | solution.py:77
  340.1 1.4 fusion.37
  341.4 2.2 fusion.39
  343.7 119.6 %reduce-scatter.3.cloned.1.call-done = f32[160,1152]{1,0:T(8,128)} async-done(((f32[2560,1152]{1,0:T(8,128)}), f32[160,1152]{1,0:T(8,128)}) %reduce-scatter.3.cloned.1.call-update) | async-done | bytes 737296 | tf_op jit(solution)/shard_map/reduce_scatter | solution.py:75
  463.3 1.4 fusion.33
  464.7 2.2 fusion.35
  (37 shorter events, 2.4 us)
Async XLA Ops:
  7.2 6.3 %copy-start.4 = (u32[128]{0:T(128)S(1)}, u32[128]{0:T(128)}, u32[]{:S(2)}) copy-start(u32[128]{0:T(128)} %constant.56) | copy-start | bytes 1540
  7.2 7.6 %copy-start.2 = (s32[160]{0:T(256)S(1)}, s32[160]{0:T(256)}, u32[]{:S(2)}) copy-start(s32[160]{0:T(256)} %param.9) | copy-start | bytes 1924
  7.2 75.1 %all-gather.5.cloned.1.call-start = ((), (), s32[]{:S(2)}) async-start(), calls=%async_computation.3 | async-start | bytes 3317760 | tf_op jit(solution)/shard_map/all_gather | solution.py:37
  10.3 138.4 %all-gather.3.cloned.1.call-start = ((), (), s32[]{:S(2)}) async-start(), calls=%async_computation.2 | async-start | bytes 6266880 | tf_op jit(solution)/shard_map/all_gather | solution.py:44
  13.4 326.7 %reduce-scatter.5.cloned.1.call-start = ((), (), s32[]{:S(2)}) async-start(), calls=%async_computation.5 | async-start | bytes 6635520 | tf_op jit(solution)/shard_map/reduce_scatter | solution.py:77
  219.4 1.8 copy-start.3
  219.4 243.9 %reduce-scatter.3.cloned.1.call-start = ((), (), s32[]{:S(2)}) async-start(), calls=%async_computation.4 | async-start | bytes 12533760 | tf_op jit(solution)/shard_map/reduce_scatter | solution.py:75
  234.7 105.4 %copy-start = (bf16[160,1152]{1,0:T(8,128)(2,1)S(1)}, bf16[160,1152]{1,0:T(8,128)(2,1)}, u32[]{:S(2)}) copy-start(bf16[160,1152]{1,0:T(8,128)(2,1)} %param.8) | copy-start | bytes 1105924
  234.7 228.6 %copy-start.1 = (bf16[160,1152]{1,0:T(8,128)(2,1)S(1)}, bf16[160,1152]{1,0:T(8,128)(2,1)}, u32[]{:S(2)}) copy-start(bf16[160,1152]{1,0:T(8,128)(2,1)} %param.7) | copy-start | bytes 1105924
Sparse Core Ops, SparseCore 0:
  10.4 70.8 all-gather.4
  84.2 64.3 all-gather.2
  219.5 120.4 reduce-scatter.4
  345.0 118.2 reduce-scatter.2
where the time goes:
time: 474 us; the launch traced here: 473 us
  waiting for transfers between devices  291 us (61%)
  matrix products  84.1 us (18%)
  blocking collectives  67.2 us (14%)
  between operations  15.2 us (3%)
  other arithmetic  13.3 us (3%)
    reduce_scatter x1, waiting for transfers between devices, shards(): lax.psum_scatter(image_partial, 'col', scatter_dimension=0, tiled=True)  120 us
    reduce_scatter x1, waiting for transfers between devices, shards(): lax.psum_scatter(text_partial, 'row', scatter_dimension=0, tiled=True)  105 us
    unnamed x1, blocking collectives  67.2 us
    all_gather x1, waiting for transfers between devices, shards(): lax.all_gather(image_half, 'col', axis=0, tiled=True)  66.4 us
    dot_general x5, matrix products, accumulate(): lax.dot_general(coefficient, image_block, (((0,), (0,)), ((), ())), prefe...  35.6 us
    dot_general x5, matrix products, accumulate(): jnp.dot(image_block, texts.T, preferred_element_type=jnp.float32)  35 us
    dot_general x1, matrix products, shards(): jnp.dot(pair_coefficients, texts, preferred_element_type=jnp.float32)  13.5 us
  transfers between devices with their start and end apart: 4, of which 3 were waited for; matrix products, arithmetic and copies ran while one was open for 4% of the time, Pallas kernels for 0%

commit v1 on v0

v1 whole, which is shorter than its diff:
```python
import jax
import jax.numpy as jnp
from jax import lax
from jax.experimental import pallas as pl
from jax.experimental.pallas import tpu as pltpu
from jax.sharding import PartitionSpec as P

AXES = ("row", "col")
VMEM = pl.BlockSpec(memory_space=pltpu.VMEM)
SMEM = pl.BlockSpec(memory_space=pltpu.SMEM)
ANY = pl.BlockSpec(memory_space=pl.ANY)
BIG = pltpu.CompilerParams(vmem_limit_bytes=56 * 2**20)
F32 = jnp.float32
BF16 = jnp.bfloat16
BLOCK = 256


def device(x, y, z, k):
    return (y % 4 * 2 + z % 2) * 16 + x % 4 * 4 + z % 4 // 2 * 2 + k


def z_mate(z, k):
    return z + 1 if (z + k) % 2 == 0 else z - 1


def pairs(move):
    out = []
    for x in range(4):
        for y in range(4):
            for z in range(4):
                for k in range(2):
                    out.append((device(x, y, z, k), device(*move(x, y, z, k))))
    return out


def ring(step):
    return pairs(lambda x, y, z, k: (x + step, y, z, k) if k == 0 else (x, y + step, z, k))


CORES = pairs(lambda x, y, z, k: (x, y, z, 1 - k))
MATES = pairs(lambda x, y, z, k: (x, y, z_mate(z, k), k))
STEPS = (0, 1, -1, 2)


def send(value, perm):
    return lax.ppermute(value, AXES, perm)


def normalize(raw):
    values = raw.astype(F32)
    inverse = lax.rsqrt(jnp.sum(values * values, axis=1, keepdims=True) + 1e-06)
    return values * inverse, inverse


def prepare_kernel(place, image, text, labels, keep, away):
    core = place[0]
    rows = image.shape[0]
    image_half = normalize(image[...])[0].astype(BF16)
    text_half = normalize(text[...])[0].astype(BF16)
    label = labels[...]
    high = lax.shift_right_logical(label, 8).astype(F32)
    low = jnp.bitwise_and(label, 255).astype(F32)
    line = lax.broadcasted_iota(jnp.int32, (16, label.shape[1]), 0)
    digits = jnp.where(line == 2 * core, high, jnp.where(line == 2 * core + 1, low, 0.0)).astype(BF16)
    tail = jnp.zeros((16, image.shape[1]), BF16)
    for out in (keep, away):
        out[rows:, :] = tail
        out[rows:, : label.shape[1]] = digits

    @pl.when(core == 0)
    def _():
        keep[:rows, :] = image_half
        away[:rows, :] = text_half

    @pl.when(core == 1)
    def _():
        keep[:rows, :] = text_half
        away[:rows, :] = image_half


def prepare(place, image, text, labels):
    rows, width = image.shape
    shape = jax.ShapeDtypeStruct((rows + 16, width), BF16)
    padded = jnp.pad(labels, (0, 256 - rows)).reshape(1, 256)
    return pl.pallas_call(
        prepare_kernel,
        out_shape=(shape, shape),
        in_specs=[SMEM, VMEM, VMEM, VMEM],
        out_specs=(VMEM, VMEM),
        compiler_params=BIG,
        name="prepare",
    )(place, image, text, padded)


def pair_kernel(pieces, scale, place, *refs):
    mine, other = refs[:pieces], refs[pieces : 2 * pieces]
    keep, away = refs[2 * pieces], refs[2 * pieces + 1]
    images, digits, texts, labels, coefficient, image_out, text_sum, text_out, load_sem, out_sem = refs[
        2 * pieces + 2 :
    ]
    core = place[0]
    rows = mine[0].shape[0] - 16
    half = rows // 2
    block_count = pieces * rows // BLOCK
    text_rows = pieces * half

    def loads(image_from, text_from, offset):
        copies = []
        for p in range(pieces):
            copies.append(
                pltpu.make_async_copy(
                    text_from[p].at[pl.ds(offset, half)], texts.at[pl.ds(p * half, half)], load_sem.at[3 * p]
                )
            )
            copies.append(
                pltpu.make_async_copy(
                    image_from[p].at[pl.ds(0, rows)], images.at[pl.ds(p * rows, rows)], load_sem.at[3 * p + 1]
                )
            )
            copies.append(
                pltpu.make_async_copy(image_from[p].at[pl.ds(rows, 16)], digits.at[p], load_sem.at[3 * p + 2])
            )
        return copies

    @pl.when(core == 0)
    def _():
        for copy in loads(mine, other, half):
            copy.start()
        for copy in loads(mine, other, half):
            copy.wait()

    @pl.when(core == 1)
    def _():
        for copy in loads(other, mine, 0):
            copy.start()
        for copy in loads(other, mine, 0):
            copy.wait()

    text_sum[...] = jnp.zeros_like(text_sum)
    for p in range(pieces):
        digit = digits[p].astype(F32)
        for k in range(2):
            number = digit[2 * k : 2 * k + 1, :half] * 256.0 + digit[2 * k + 1 : 2 * k + 2, :half]
            start = p * rows + k * half
            labels[:, start : start + half] = jnp.broadcast_to(number, (8, half))
    a, b = 0.5 * scale[0], 0.5 * scale[1]
    position = lax.broadcasted_iota(jnp.int32, (half, BLOCK), 0).astype(F32)

    def block(i, _):
        begin = pl.multiple_of(i * BLOCK, BLOCK)
        image = images[pl.ds(begin, BLOCK), :]
        label = labels[0:1, pl.ds(begin, BLOCK)]
        for p in range(pieces):
            logits = lax.dot_general(
                texts[p * half : (p + 1) * half, :], image, (((1,), (1,)), ((), ())), preferred_element_type=F32
            )
            first = place[1 + p].astype(F32)
            shift = jnp.where(position == label - first, -0.5, 0.5)
            coefficient[p * half : (p + 1) * half, :] = (0.5 * jnp.tanh(logits * a + b) + shift).astype(BF16)
        for p in range(text_rows // BLOCK):
            rows_p = slice(p * BLOCK, (p + 1) * BLOCK)
            text_sum[rows_p, :] += jnp.dot(coefficient[rows_p, :], image, preferred_element_type=F32)
        image_out[pl.ds(begin, BLOCK), :] = lax.dot_general(
            coefficient[...], texts[...], (((0,), (0,)), ((), ())), preferred_element_type=F32
        ).astype(BF16)
        return 0

    lax.fori_loop(0, block_count, block, 0)
    text_out[...] = text_sum[...].astype(BF16)

    def flush(image_to, text_to):
        one = pltpu.make_async_copy(image_out, image_to, out_sem.at[0])
        two = pltpu.make_async_copy(text_out, text_to.at[pl.ds(0, text_rows)], out_sem.at[1])
        one.start()
        two.start()
        one.wait()
        two.wait()

    @pl.when(core == 0)
    def _():
        flush(keep, away)

    @pl.when(core == 1)
    def _():
        flush(away, keep)


def pair_sums(scale, place, mine, other):
    pieces = len(mine)
    rows, width = mine[0].shape[0] - 16, mine[0].shape[1]
    total = pieces * rows
    shape = jax.ShapeDtypeStruct((total, width), BF16)
    flops = 6 * total * total // 2 * width
    return pl.pallas_call(
        lambda *refs: pair_kernel(pieces, *refs),
        out_shape=(shape, shape),
        in_specs=[SMEM, SMEM] + [ANY] * (2 * pieces),
        out_specs=(ANY, ANY),
        scratch_shapes=[
            pltpu.VMEM((total, width), BF16),
            pltpu.VMEM((pieces, 16, width), BF16),
            pltpu.VMEM((total // 2, width), BF16),
            pltpu.VMEM((8, total), F32),
            pltpu.VMEM((total // 2, BLOCK), BF16),
            pltpu.VMEM((total, width), BF16),
            pltpu.VMEM((total // 2, width), F32),
            pltpu.VMEM((total // 2, width), BF16),
            pltpu.SemaphoreType.DMA((3 * pieces,)),
            pltpu.SemaphoreType.DMA((2,)),
        ],
        compiler_params=BIG,
        cost_estimate=pl.CostEstimate(flops=flops, bytes_accessed=10 * total * width, transcendentals=total * total // 2),
        name="pair_sums",
    )(scale, place, *mine, *other)


def join_kernel(place, keep, got, *outs):
    core = place[0]
    rows = outs[0].shape[0]
    half = rows // 2

    @pl.when(core == 0)
    def _():
        for p, out in enumerate(outs):
            part = slice(p * rows, (p + 1) * rows)
            out[...] = (keep[part, :].astype(F32) + got[part, :].astype(F32)).astype(BF16)

    @pl.when(core == 1)
    def _():
        for p, out in enumerate(outs):
            part = slice(p * half, (p + 1) * half)
            out[:half, :] = keep[part, :]
            out[half:, :] = got[part, :]


def join(place, keep, got, pieces):
    rows, width = keep.shape[0] // pieces, keep.shape[1]
    shape = jax.ShapeDtypeStruct((rows, width), BF16)
    return pl.pallas_call(
        join_kernel,
        out_shape=(shape,) * pieces,
        in_specs=[SMEM, VMEM, VMEM],
        out_specs=(VMEM,) * pieces,
        compiler_params=BIG,
        name="join",
    )(place, keep, got)


def add_kernel(*refs):
    total = refs[0][...].astype(F32)
    for ref in refs[1:-1]:
        total = total + ref[...].astype(F32)
    refs[-1][...] = total.astype(refs[-1].dtype)


def add(values, dtype):
    return pl.pallas_call(
        add_kernel,
        out_shape=jax.ShapeDtypeStruct(values[0].shape, dtype),
        in_specs=[VMEM] * len(values),
        out_specs=VMEM,
        compiler_params=BIG,
        name="add",
    )(*values)


def finish_kernel(place, scale, image, text, total, got, image_grad, text_grad):
    core = place[0]
    half = got.shape[0]

    def backward(raw, unit_grad):
        unit, inverse = normalize(raw[...])
        unit_grad = scale[0] * unit_grad
        along = jnp.sum(unit * unit_grad, axis=1, keepdims=True)
        return inverse * (unit_grad - unit * along)

    @pl.when(core == 0)
    def _():
        image_grad[...] = backward(image, total[:half, :])
        text_grad[...] = backward(text, got[...])

    @pl.when(core == 1)
    def _():
        image_grad[...] = backward(image, got[...])
        text_grad[...] = backward(text, total[:half, :])


def finish(place, scale, image, text, total, got):
    shape = jax.ShapeDtypeStruct(image.shape, F32)
    return pl.pallas_call(
        finish_kernel,
        out_shape=(shape, shape),
        in_specs=[SMEM, SMEM] + [VMEM] * 4,
        out_specs=(VMEM, VMEM),
        compiler_params=BIG,
        name="finish",
    )(place, scale, image, text, total, got)


def shards(image, text, labels, sharpness, shift):
    rows = image.shape[0]
    row, col = lax.axis_index("row"), lax.axis_index("col")
    x, core = col // 4, col % 2
    y, z = row // 2, col // 2 % 2 * 2 + row % 2
    mate = jnp.where(z % 2 == 1, z + 1, z + 3) % 4
    bases = [device_at(x, y + d, level, core) * rows for level in (z, mate) for d in STEPS]
    place = jnp.stack([core] + bases).astype(jnp.int32)
    scale = jnp.concatenate([sharpness, shift])

    keep, away = prepare(place, image, text, labels)
    got = send(away, CORES)
    own = jnp.concatenate([keep[:rows], got[:rows], keep[rows:] + got[rows:]], axis=0)
    mate_own = send(own, MATES)
    mine = [own] + [send(own, ring(-d)) for d in STEPS[1:]]
    mine += [mate_own] + [send(mate_own, ring(-d)) for d in STEPS[1:]]
    other = [send(piece, CORES) for piece in mine]
    keep, away = pair_sums(scale, place, mine, other)
    got = send(away, CORES)
    parts = join(place, keep, got, 8)
    mate_parts = [parts[4]] + [send(part, ring(d)) for part, d in zip(parts[5:], STEPS[1:])]
    mate_total = send(add(mate_parts, BF16), MATES)
    own_parts = [parts[0]] + [send(part, ring(d)) for part, d in zip(parts[1:4], STEPS[1:])]
    total = add(own_parts + [mate_total], F32)
    got = send(total[rows:], CORES)
    return finish(place, scale, image, text, total, got)


def device_at(x, y, z, k):
    return (y % 4 * 2 + z % 2) * 16 + x % 4 * 4 + z % 4 // 2 * 2 + k


def solution(mesh):
    spec = P(AXES, None)
    return jax.shard_map(
        shards,
        mesh=mesh,
        in_specs=(spec, spec, P(AXES), P(), P()),
        out_specs=(spec, spec),
        check_vma=False,
    )
```

time: 474 us -> 171 us (0.36)
  waiting for transfers between devices: 291 us -> 53 us
  matrix products: 84.1 us -> 0 us
  blocking collectives: 67.2 us -> 0 us
  Pallas kernels: 0 us -> 62.5 us
  starting transfers between devices: 0.16 us -> 38.3 us
  between operations: 15.2 us -> 2.41 us
  other arithmetic: 13.3 us -> 1.39 us
  local copies, waits for them, and re-layouts: 2.75 us -> 12.7 us
    reduce_scatter x2 -> x0, waiting for transfers between devices: 224 us -> none  [the longest x1 120 us: shards(): lax.psum_scatter(image_partial, 'col', scatter_dimension=0, tiled=True)]
    dot_general x11 -> x0, matrix products: 84.1 us -> none  [the longest x5 35.6 us: accumulate(): lax.dot_general(coefficient, image_block, (((0,), (0,)), ((), ())), prefe...]
    unnamed x1 -> x0, blocking collectives: 67.2 us -> none
    all_gather x2 -> x0, waiting for transfers between devices: 66.4 us -> none  [the longest x1 66.4 us: shards(): lax.all_gather(image_half, 'col', axis=0, tiled=True)]
    pallas_call x0 -> x6, Pallas kernels: none -> 62.5 us  [the longest x1 42.8 us: pair_sums(): pl.pallas_call(lambda *refs: pair_kernel(pieces, *refs), out_shape=(shape...]
    ppermute x0 -> x25, waiting for transfers between devices: none -> 53 us  [send(): return lax.ppermute(value, AXES, perm)]
    ppermute x0 -> x25, starting transfers between devices: none -> 38.3 us  [send(): return lax.ppermute(value, AXES, perm)]
    unnamed x13 -> x48, local copies, waits for them, and re-layouts: 2.71 us -> 8.6 us
  transfers between devices with their start and end apart: 4 -> 25, of which waited for: 3 -> 13; matrix products, arithmetic and copies ran while one was open for 4% -> 1% of each run, Pallas kernels for 0% -> 2%
where the time goes in v1:
time: 171 us; the launch traced here: 170 us
  Pallas kernels  62.5 us (37%)
  waiting for transfers between devices  53 us (31%)
  starting transfers between devices  38.3 us (22%)
  local copies, waits for them, and re-layouts  12.7 us (7%)
  between operations  2.41 us (1%)
    ppermute x25, waiting for transfers between devices, send(): return lax.ppermute(value, AXES, perm)  53 us
    pallas_call x1, Pallas kernels, pair_sums(): pl.pallas_call(lambda *refs: pair_kernel(pieces, *refs), out_shape=(shape...  42.8 us
    ppermute x25, starting transfers between devices, send(): return lax.ppermute(value, AXES, perm)  38.3 us
    unnamed x48, local copies, waits for them, and re-layouts  8.6 us
    pallas_call x1, Pallas kernels, join(): pl.pallas_call(join_kernel, out_shape=(shape,) * pieces, in_specs=[SMEM,...  7.38 us
    pallas_call x2, Pallas kernels, add(): pl.pallas_call(add_kernel, out_shape=jax.ShapeDtypeStruct(values[0].shape...  6.6 us
    pallas_call x1, Pallas kernels, finish(): pl.pallas_call(finish_kernel, out_shape=(shape, shape), in_specs=[SMEM, S...  3.45 us
  transfers between devices with their start and end apart: 25, of which 13 were waited for; matrix products, arithmetic and copies ran while one was open for 1% of the time, Pallas kernels for 2%

profile of v1, /device:TPU:1, one launch (start us, length us, event | category | flops | bytes accessed | tf_op | source)
XLA Modules:
  0.0 170.4 jit_solution(4762590490797984314)
XLA Ops:
  2.8 2.3 %prepare.1 = (bf16[176,1152]{1,0:T(8,128)(2,1)}, bf16[176,1152]{1,0:T(8,128)(2,1)}) custom-call(s32[9]{0:T(128)} %stack.39.place.refs_1_, bf16[160,1152]{1,0:T(8,128)(2,1)} %image.3, bf16[160,1152]{1,0:T(8,128)(2,1)} %text.3, s32[1,256]{1,0:T(1,128)} %bitcast.10), custom_call_target="tpu_custom_call" | custom-call | tf_op jit(solution)/shard_map/prepare/pallas_call | solution.py:85
  9.0 3.9 %collective-permute-start.4 = (bf16[336,1152]{1,0:T(8,128)(2,1)S(1)}, bf16[336,1152]{1,0:T(8,128)(2,1)S(1)}, u32[]{:S(2)}, u32[]{:S(2)}) collective-permute-start(bf16[336,1152]{1,0:T(8,128)(2,1)S(1)} %pad_maximum_fusion.refs_2_), channel_id=1, source_target_pairs={{0,16},{1,19},{16,0},{17,3},{2,18},{3,17},{18,2},{19,1},{32,48},{3... | collective-permute-start | bytes 2322440 | tf_op jit(solution)/shard_map/ppermute | solution.py:46
  12.9 2.9 %collective-permute-start.3 = (bf16[336,1152]{1,0:T(8,128)(2,1)S(1)}, bf16[336,1152]{1,0:T(8,128)(2,1)S(1)}, u32[]{:S(2)}, u32[]{:S(2)}) collective-permute-start(bf16[336,1152]{1,0:T(8,128)(2,1)S(1)} %pad_maximum_fusion.refs_2_), channel_id=1, source_target_pairs={{0,8},{1,65},{16,24},{17,81},{2,10},{3,67},{18,26},{19,83},{32,40}... | collective-permute-start | bytes 2322440 | tf_op jit(solution)/shard_map/ppermute | solution.py:46
  16.2 2.3 %collective-permute-start.1 = (bf16[336,1152]{1,0:T(8,128)(2,1)S(1)}, bf16[336,1152]{1,0:T(8,128)(2,1)S(1)}, u32[]{:S(2)}, u32[]{:S(2)}) collective-permute-start(bf16[336,1152]{1,0:T(8,128)(2,1)S(1)} %pad_maximum_fusion.refs_2_), channel_id=1, source_target_pairs={{0,12},{1,97},{16,28},{17,113},{2,14},{3,99},{18,30},{19,115},{32,... | collective-permute-start | bytes 2322440 | tf_op jit(solution)/shard_map/ppermute | solution.py:46
  18.5 3.9 %collective-permute-done.4.refs_6_ = bf16[336,1152]{1,0:T(8,128)(2,1)S(1)} collective-permute-done((bf16[336,1152]{1,0:T(8,128)(2,1)S(1)}, bf16[336,1152]{1,0:T(8,128)(2,1)S(1)}, u32[]{:S(2)}, u32[]{:S(2)}) %collective-permute-start.4) | collective-permute-done | bytes 774176 | tf_op jit(solution)/shard_map/ppermute | solution.py:46
  22.5 3.0 %collective-permute-start.7 = (bf16[336,1152]{1,0:T(8,128)(2,1)S(1)}, bf16[336,1152]{1,0:T(8,128)(2,1)S(1)}, u32[]{:S(2)}, u32[]{:S(2)}) collective-permute-start(bf16[336,1152]{1,0:T(8,128)(2,1)S(1)} %collective-permute-done.4.refs_6_), channel_id=1, source_target_pairs={{0,8},{1,65},{16,24},{17,81},{2,10},{3,67},{18,26},{19,83},{32,40}... | collective-permute-start | bytes 2322440 | tf_op jit(solution)/shard_map/ppermute | solution.py:46
  26.8 7.0 %collective-permute-done.2.refs_4_ = bf16[336,1152]{1,0:T(8,128)(2,1)S(1)} collective-permute-done((bf16[336,1152]{1,0:T(8,128)(2,1)S(1)}, bf16[336,1152]{1,0:T(8,128)(2,1)S(1)}, u32[]{:S(2)}, u32[]{:S(2)}) %collective-permute-start.2) | collective-permute-done | bytes 774176 | tf_op jit(solution)/shard_map/ppermute | solution.py:46
  34.1 1.6 collective-permute-start.11
  35.8 6.3 %collective-permute-done.7.refs_9_ = bf16[336,1152]{1,0:T(8,128)(2,1)S(1)} collective-permute-done((bf16[336,1152]{1,0:T(8,128)(2,1)S(1)}, bf16[336,1152]{1,0:T(8,128)(2,1)S(1)}, u32[]{:S(2)}, u32[]{:S(2)}) %collective-permute-start.7) | collective-permute-done | bytes 774176 | tf_op jit(solution)/shard_map/ppermute | solution.py:46
  43.5 6.8 %collective-permute-done.6.refs_8_ = bf16[336,1152]{1,0:T(8,128)(2,1)S(1)} collective-permute-done((bf16[336,1152]{1,0:T(8,128)(2,1)S(1)}, bf16[336,1152]{1,0:T(8,128)(2,1)S(1)}, u32[]{:S(2)}, u32[]{:S(2)}) %collective-permute-start.6) | collective-permute-done | bytes 774176 | tf_op jit(solution)/shard_map/ppermute | solution.py:46
  57.3 42.8 %pair_sums.1 = (bf16[2560,1152]{1,0:T(8,128)(2,1)}, bf16[2560,1152]{1,0:T(8,128)(2,1)}) custom-call(f32[2]{0:T(128)} %pad_maximum_fusion.1.refs_0_.scale, s32[9]{0:T(128)} %stack.39.place.refs_1_, bf16[336,1152]{1,0:T(8,128)(2,1)} %copy-done.1, bf16[336,1152]{1,0:T(8,128)(2,1)} %copy-done.14, bf16[336,1152]{1,0:T(8,128)(2,1)} %copy-done.13, ...), custom_call_target="tpu_custom_call" | custom-call | flops 22649241600 | bytes 29491200 | tf_op jit(solution)/shard_map/pair_sums/pallas_call | solution.py:194
  100.3 9.8 %collective-permute-done.16.got = bf16[2560,1152]{1,0:T(8,128)(2,1)S(1)} collective-permute-done((bf16[2560,1152]{1,0:T(8,128)(2,1)}, bf16[2560,1152]{1,0:T(8,128)(2,1)S(1)}, u32[]{:S(2)}, u32[]{:S(2)}) %collective-permute-start.16) | collective-permute-done | bytes 5898272 | tf_op jit(solution)/shard_map/ppermute | solution.py:46
  110.0 2.5 %copy-done = bf16[2560,1152]{1,0:T(8,128)(2,1)} copy-done((bf16[2560,1152]{1,0:T(8,128)(2,1)}, bf16[2560,1152]{1,0:T(8,128)(2,1)S(1)}, u32[]{:S(2)}) %copy-start) | copy-done | bytes 5898264
  112.5 7.4 %join.1 = (bf16[320,1152]{1,0:T(8,128)(2,1)}, bf16[320,1152]{1,0:T(8,128)(2,1)}, bf16[320,1152]{1,0:T(8,128)(2,1)}, bf16[320,1152]{1,0:T(8,128)(2,1)}, bf16[320,...) custom-call(s32[9]{0:T(128)} %stack.39.place.refs_1_, ...), custom_call_target="tpu_custom_call" | custom-call | tf_op jit(solution)/shard_map/join/pallas_call | solution.py:239
  122.7 1.6 collective-permute-start.22
  124.7 2.3 %collective-permute-start.18 = (bf16[320,1152]{1,0:T(8,128)(2,1)}, bf16[320,1152]{1,0:T(8,128)(2,1)S(1)}, u32[]{:S(2)}, u32[]{:S(2)}) collective-permute-start(bf16[320,1152]{1,0:T(8,128)(2,1)} %get-tuple-element.20), channel_id=1, source_target_pairs={{0,12},{1,97},{16,28},{17,113},{2,14},{3,99},{18,30},{19,115},{32,... | collective-permute-start | bytes 2211848 | tf_op jit(solution)/shard_map/ppermute | solution.py:46
  127.0 5.0 %collective-permute-done.20.refs_1_ = bf16[320,1152]{1,0:T(8,128)(2,1)S(1)} collective-permute-done((bf16[320,1152]{1,0:T(8,128)(2,1)}, bf16[320,1152]{1,0:T(8,128)(2,1)S(1)}, u32[]{:S(2)}, u32[]{:S(2)}) %collective-permute-start.20) | collective-permute-done | bytes 737312 | tf_op jit(solution)/shard_map/ppermute | solution.py:46
  132.0 9.5 %collective-permute-start.19 = (bf16[320,1152]{1,0:T(8,128)(2,1)}, bf16[320,1152]{1,0:T(8,128)(2,1)S(1)}, u32[]{:S(2)}, u32[]{:S(2)}) collective-permute-start(bf16[320,1152]{1,0:T(8,128)(2,1)} %get-tuple-element.21), channel_id=1, source_target_pairs={{0,8},{1,65},{16,24},{17,81},{2,10},{3,67},{18,26},{19,83},{32,40}... | collective-permute-start | bytes 2211848 | tf_op jit(solution)/shard_map/ppermute | solution.py:46
  142.7 3.0 %add.246 = bf16[320,1152]{1,0:T(8,128)(2,1)} custom-call(bf16[320,1152]{1,0:T(8,128)(2,1)} %get-tuple-element.22.refs_0_, bf16[320,1152]{1,0:T(8,128)(2,1)} %copy-done.6, bf16[320,1152]{1,0:T(8,128)(2,1)} %copy-done.7, bf16[320,1152]{1,0:T(8,128)(2,1)} %copy-done.8), custom_call_target="tpu_custom_call" | custom-call | tf_op jit(solution)/shard_map/add/pallas_call | solution.py:257
  146.0 1.8 %collective-permute-done.17.refs_1_ = bf16[320,1152]{1,0:T(8,128)(2,1)S(1)} collective-permute-done((bf16[320,1152]{1,0:T(8,128)(2,1)}, bf16[320,1152]{1,0:T(8,128)(2,1)S(1)}, u32[]{:S(2)}, u32[]{:S(2)}) %collective-permute-start.17) | collective-permute-done | bytes 737312 | tf_op jit(solution)/shard_map/ppermute | solution.py:46
  147.9 9.1 %collective-permute-done.19.refs_3_ = bf16[320,1152]{1,0:T(8,128)(2,1)S(1)} collective-permute-done((bf16[320,1152]{1,0:T(8,128)(2,1)}, bf16[320,1152]{1,0:T(8,128)(2,1)S(1)}, u32[]{:S(2)}, u32[]{:S(2)}) %collective-permute-start.19) | collective-permute-done | bytes 737312 | tf_op jit(solution)/shard_map/ppermute | solution.py:46
  158.6 3.6 %add.247.total = f32[320,1152]{1,0:T(8,128)} custom-call(bf16[320,1152]{1,0:T(8,128)(2,1)} %get-tuple-element.18.refs_0_, bf16[320,1152]{1,0:T(8,128)(2,1)} %copy-done.2, bf16[320,1152]{1,0:T(8,128)(2,1)} %copy-done.3, bf16[320,1152]{1,0:T(8,128)(2,1)} %copy-done.4, bf16[320,1152]{1,0:T(8,128)(2,1)} %copy-done.5), custom_call_target="tpu_custom_call" | custom-call | tf_op jit(solution)/shard_map/add/pallas_call | solution.py:257
  164.2 1.8 %collective-permute-done.24.got = f32[160,1152]{1,0:T(8,128)S(1)} collective-permute-done((f32[160,1152]{1,0:T(8,128)S(1)}, f32[160,1152]{1,0:T(8,128)S(1)}, u32[]{:S(2)}, u32[]{:S(2)}) %collective-permute-start.24) | collective-permute-done | bytes 737312 | tf_op jit(solution)/shard_map/ppermute | solution.py:46
  166.9 3.5 %finish.1 = (f32[160,1152]{1,0:T(8,128)}, f32[160,1152]{1,0:T(8,128)}) custom-call(s32[9]{0:T(128)} %stack.39.place.refs_1_, f32[2]{0:T(128)} %pad_maximum_fusion.1.refs_0_.scale, bf16[160,1152]{1,0:T(8,128)(2,1)} %image.3, bf16[160,1152]{1,0:T(8,128)(2,1)} %text.3, f32[320,1152]{1,0:T(8,128)} %add.247.total, f32[160,1152]{1,0:T(8,128)} %copy-done.9), custom_call_target="tpu_custom_call" | custom-call | tf_op jit(solution)/shard_map/finish/pallas_call | solution.py:290
  (88 shorter events, 24.3 us)
Async XLA Ops:
  5.1 3.0 %collective-permute-start = (bf16[176,1152]{1,0:T(8,128)(2,1)}, bf16[176,1152]{1,0:T(8,128)(2,1)S(1)}, u32[]{:S(2)}, u32[]{:S(2)}) collective-permute-start(bf16[176,1152]{1,0:T(8,128)(2,1)} %get-tuple-element.15), channel_id=1, source_target_pairs={{0,1},{1,0},{16,17},{17,16},{2,3},{3,2},{18,19},{19,18},{32,33},{3... | collective-permute-start | bytes 1216520 | tf_op jit(solution)/shard_map/ppermute | solution.py:46
  9.0 13.5 %collective-permute-start.4 = (bf16[336,1152]{1,0:T(8,128)(2,1)S(1)}, bf16[336,1152]{1,0:T(8,128)(2,1)S(1)}, u32[]{:S(2)}, u32[]{:S(2)}) collective-permute-start(bf16[336,1152]{1,0:T(8,128)(2,1)S(1)} %pad_maximum_fusion.refs_2_), channel_id=1, source_target_pairs={{0,16},{1,19},{16,0},{17,3},{2,18},{3,17},{18,2},{19,1},{32,48},{3... | collective-permute-start | bytes 2322440 | tf_op jit(solution)/shard_map/ppermute | solution.py:46
  12.9 9.6 %collective-permute-start.8 = (bf16[336,1152]{1,0:T(8,128)(2,1)S(1)}, bf16[336,1152]{1,0:T(8,128)(2,1)S(1)}, u32[]{:S(2)}, u32[]{:S(2)}) collective-permute-start(bf16[336,1152]{1,0:T(8,128)(2,1)S(1)} %pad_maximum_fusion.refs_2_), channel_id=1, source_target_pairs={{0,1},{1,0},{16,17},{17,16},{2,3},{3,2},{18,19},{19,18},{32,33},{3... | collective-permute-start | bytes 2322440 | tf_op jit(solution)/shard_map/ppermute | solution.py:46
  12.9 12.6 %collective-permute-start.3 = (bf16[336,1152]{1,0:T(8,128)(2,1)S(1)}, bf16[336,1152]{1,0:T(8,128)(2,1)S(1)}, u32[]{:S(2)}, u32[]{:S(2)}) collective-permute-start(bf16[336,1152]{1,0:T(8,128)(2,1)S(1)} %pad_maximum_fusion.refs_2_), channel_id=1, source_target_pairs={{0,8},{1,65},{16,24},{17,81},{2,10},{3,67},{18,26},{19,83},{32,40}... | collective-permute-start | bytes 2322440 | tf_op jit(solution)/shard_map/ppermute | solution.py:46
  15.8 17.9 %collective-permute-start.2 = (bf16[336,1152]{1,0:T(8,128)(2,1)S(1)}, bf16[336,1152]{1,0:T(8,128)(2,1)S(1)}, u32[]{:S(2)}, u32[]{:S(2)}) collective-permute-start(bf16[336,1152]{1,0:T(8,128)(2,1)S(1)} %pad_maximum_fusion.refs_2_), channel_id=1, source_target_pairs={{0,4},{1,33},{16,20},{17,49},{2,6},{3,35},{18,22},{19,51},{32,36},... | collective-permute-start | bytes 2322440 | tf_op jit(solution)/shard_map/ppermute | solution.py:46
  16.2 17.9 %collective-permute-start.1 = (bf16[336,1152]{1,0:T(8,128)(2,1)S(1)}, bf16[336,1152]{1,0:T(8,128)(2,1)S(1)}, u32[]{:S(2)}, u32[]{:S(2)}) collective-permute-start(bf16[336,1152]{1,0:T(8,128)(2,1)S(1)} %pad_maximum_fusion.refs_2_), channel_id=1, source_target_pairs={{0,12},{1,97},{16,28},{17,113},{2,14},{3,99},{18,30},{19,115},{32,... | collective-permute-start | bytes 2322440 | tf_op jit(solution)/shard_map/ppermute | solution.py:46
  22.5 13.2 %collective-permute-start.12 = (bf16[336,1152]{1,0:T(8,128)(2,1)S(1)}, bf16[336,1152]{1,0:T(8,128)(2,1)S(1)}, u32[]{:S(2)}, u32[]{:S(2)}) collective-permute-start(bf16[336,1152]{1,0:T(8,128)(2,1)S(1)} %collective-permute-done.4.refs_6_), channel_id=1, source_target_pairs={{0,1},{1,0},{16,17},{17,16},{2,3},{3,2},{18,19},{19,18},{32,33},{3... | collective-permute-start | bytes 2322440 | tf_op jit(solution)/shard_map/ppermute | solution.py:46
  22.5 19.6 %collective-permute-start.7 = (bf16[336,1152]{1,0:T(8,128)(2,1)S(1)}, bf16[336,1152]{1,0:T(8,128)(2,1)S(1)}, u32[]{:S(2)}, u32[]{:S(2)}) collective-permute-start(bf16[336,1152]{1,0:T(8,128)(2,1)S(1)} %collective-permute-done.4.refs_6_), channel_id=1, source_target_pairs={{0,8},{1,65},{16,24},{17,81},{2,10},{3,67},{18,26},{19,83},{32,40}... | collective-permute-start | bytes 2322440 | tf_op jit(solution)/shard_map/ppermute | solution.py:46
  25.5 24.8 %collective-permute-start.6 = (bf16[336,1152]{1,0:T(8,128)(2,1)S(1)}, bf16[336,1152]{1,0:T(8,128)(2,1)S(1)}, u32[]{:S(2)}, u32[]{:S(2)}) collective-permute-start(bf16[336,1152]{1,0:T(8,128)(2,1)S(1)} %collective-permute-done.4.refs_6_), channel_id=1, source_target_pairs={{0,4},{1,33},{16,20},{17,49},{2,6},{3,35},{18,22},{19,51},{32,36},... | collective-permute-start | bytes 2322440 | tf_op jit(solution)/shard_map/ppermute | solution.py:46
  33.7 18.0 %collective-permute-start.5 = (bf16[336,1152]{1,0:T(8,128)(2,1)S(1)}, bf16[336,1152]{1,0:T(8,128)(2,1)S(1)}, u32[]{:S(2)}, u32[]{:S(2)}) collective-permute-start(bf16[336,1152]{1,0:T(8,128)(2,1)S(1)} %collective-permute-done.4.refs_6_), channel_id=1, source_target_pairs={{0,12},{1,97},{16,28},{17,113},{2,14},{3,99},{18,30},{19,115},{32,... | collective-permute-start | bytes 2322440 | tf_op jit(solution)/shard_map/ppermute | solution.py:46
  34.1 17.7 %collective-permute-start.11 = (bf16[336,1152]{1,0:T(8,128)(2,1)S(1)}, bf16[336,1152]{1,0:T(8,128)(2,1)S(1)}, u32[]{:S(2)}, u32[]{:S(2)}) collective-permute-start(bf16[336,1152]{1,0:T(8,128)(2,1)S(1)} %collective-permute-done.3.refs_5_), channel_id=1, source_target_pairs={{0,1},{1,0},{16,17},{17,16},{2,3},{3,2},{18,19},{19,18},{32,33},{3... | collective-permute-start | bytes 2322440 | tf_op jit(solution)/shard_map/ppermute | solution.py:46
  35.7 19.2 %collective-permute-start.10 = (bf16[336,1152]{1,0:T(8,128)(2,1)S(1)}, bf16[336,1152]{1,0:T(8,128)(2,1)S(1)}, u32[]{:S(2)}, u32[]{:S(2)}) collective-permute-start(bf16[336,1152]{1,0:T(8,128)(2,1)S(1)} %collective-permute-done.2.refs_4_), channel_id=1, source_target_pairs={{0,1},{1,0},{16,17},{17,16},{2,3},{3,2},{18,19},{19,18},{32,33},{3... | collective-permute-start | bytes 2322440 | tf_op jit(solution)/shard_map/ppermute | solution.py:46
  42.1 12.8 %collective-permute-start.9 = (bf16[336,1152]{1,0:T(8,128)(2,1)S(1)}, bf16[336,1152]{1,0:T(8,128)(2,1)S(1)}, u32[]{:S(2)}, u32[]{:S(2)}) collective-permute-start(bf16[336,1152]{1,0:T(8,128)(2,1)S(1)} %collective-permute-done.1.refs_3_), channel_id=1, source_target_pairs={{0,1},{1,0},{16,17},{17,16},{2,3},{3,2},{18,19},{19,18},{32,33},{3... | collective-permute-start | bytes 2322440 | tf_op jit(solution)/shard_map/ppermute | solution.py:46
  50.3 4.6 %collective-permute-start.15 = (bf16[336,1152]{1,0:T(8,128)(2,1)S(1)}, bf16[336,1152]{1,0:T(8,128)(2,1)S(1)}, u32[]{:S(2)}, u32[]{:S(2)}) collective-permute-start(bf16[336,1152]{1,0:T(8,128)(2,1)S(1)} %collective-permute-done.7.refs_9_), channel_id=1, source_target_pairs={{0,1},{1,0},{16,17},{17,16},{2,3},{3,2},{18,19},{19,18},{32,33},{3... | collective-permute-start | bytes 2322440 | tf_op jit(solution)/shard_map/ppermute | solution.py:46
  51.7 3.3 %collective-permute-start.14 = (bf16[336,1152]{1,0:T(8,128)(2,1)S(1)}, bf16[336,1152]{1,0:T(8,128)(2,1)S(1)}, u32[]{:S(2)}, u32[]{:S(2)}) collective-permute-start(bf16[336,1152]{1,0:T(8,128)(2,1)S(1)} %collective-permute-done.6.refs_8_), channel_id=1, source_target_pairs={{0,1},{1,0},{16,17},{17,16},{2,3},{3,2},{18,19},{19,18},{32,33},{3... | collective-permute-start | bytes 2322440 | tf_op jit(solution)/shard_map/ppermute | solution.py:46
  52.8 4.4 %collective-permute-start.13 = (bf16[336,1152]{1,0:T(8,128)(2,1)S(1)}, bf16[336,1152]{1,0:T(8,128)(2,1)}, u32[]{:S(2)}, u32[]{:S(2)}) collective-permute-start(bf16[336,1152]{1,0:T(8,128)(2,1)S(1)} %collective-permute-done.5.refs_7_), channel_id=1, source_target_pairs={{0,1},{1,0},{16,17},{17,16},{2,3},{3,2},{18,19},{19,18},{32,33},{3... | collective-permute-start | bytes 2322440 | tf_op jit(solution)/shard_map/ppermute | solution.py:46
  100.1 9.9 %collective-permute-start.16 = (bf16[2560,1152]{1,0:T(8,128)(2,1)}, bf16[2560,1152]{1,0:T(8,128)(2,1)S(1)}, u32[]{:S(2)}, u32[]{:S(2)}) collective-permute-start(bf16[2560,1152]{1,0:T(8,128)(2,1)} %get-tuple-element.17), channel_id=1, source_target_pairs={{0,1},{1,0},{16,17},{17,16},{2,3},{3,2},{18,19},{19,18},{32,33},{3... | collective-permute-start | bytes 17694728 | tf_op jit(solution)/shard_map/ppermute | solution.py:46
  119.9 12.1 %collective-permute-start.20 = (bf16[320,1152]{1,0:T(8,128)(2,1)}, bf16[320,1152]{1,0:T(8,128)(2,1)S(1)}, u32[]{:S(2)}, u32[]{:S(2)}) collective-permute-start(bf16[320,1152]{1,0:T(8,128)(2,1)} %get-tuple-element.23), channel_id=1, source_target_pairs={{0,4},{1,33},{16,20},{17,49},{2,6},{3,35},{18,22},{19,51},{32,36},... | collective-permute-start | bytes 2211848 | tf_op jit(solution)/shard_map/ppermute | solution.py:46
  121.2 20.3 %collective-permute-start.21 = (bf16[320,1152]{1,0:T(8,128)(2,1)}, bf16[320,1152]{1,0:T(8,128)(2,1)S(1)}, u32[]{:S(2)}, u32[]{:S(2)}) collective-permute-start(bf16[320,1152]{1,0:T(8,128)(2,1)} %get-tuple-element.24), channel_id=1, source_target_pairs={{0,12},{1,97},{16,28},{17,113},{2,14},{3,99},{18,30},{19,115},{32,... | collective-permute-start | bytes 2211848 | tf_op jit(solution)/shard_map/ppermute | solution.py:46
  122.7 18.9 %collective-permute-start.22 = (bf16[320,1152]{1,0:T(8,128)(2,1)}, bf16[320,1152]{1,0:T(8,128)(2,1)S(1)}, u32[]{:S(2)}, u32[]{:S(2)}) collective-permute-start(bf16[320,1152]{1,0:T(8,128)(2,1)} %get-tuple-element.25), channel_id=1, source_target_pairs={{0,8},{1,65},{16,24},{17,81},{2,10},{3,67},{18,26},{19,83},{32,40}... | collective-permute-start | bytes 2211848 | tf_op jit(solution)/shard_map/ppermute | solution.py:46
  124.3 23.5 %collective-permute-start.17 = (bf16[320,1152]{1,0:T(8,128)(2,1)}, bf16[320,1152]{1,0:T(8,128)(2,1)S(1)}, u32[]{:S(2)}, u32[]{:S(2)}) collective-permute-start(bf16[320,1152]{1,0:T(8,128)(2,1)} %get-tuple-element.19), channel_id=1, source_target_pairs={{0,4},{1,33},{16,20},{17,49},{2,6},{3,35},{18,22},{19,51},{32,36},... | collective-permute-start | bytes 2211848 | tf_op jit(solution)/shard_map/ppermute | solution.py:46
  124.7 23.2 %collective-permute-start.18 = (bf16[320,1152]{1,0:T(8,128)(2,1)}, bf16[320,1152]{1,0:T(8,128)(2,1)S(1)}, u32[]{:S(2)}, u32[]{:S(2)}) collective-permute-start(bf16[320,1152]{1,0:T(8,128)(2,1)} %get-tuple-element.20), channel_id=1, source_target_pairs={{0,12},{1,97},{16,28},{17,113},{2,14},{3,99},{18,30},{19,115},{32,... | collective-permute-start | bytes 2211848 | tf_op jit(solution)/shard_map/ppermute | solution.py:46
  132.0 24.9 %collective-permute-start.19 = (bf16[320,1152]{1,0:T(8,128)(2,1)}, bf16[320,1152]{1,0:T(8,128)(2,1)S(1)}, u32[]{:S(2)}, u32[]{:S(2)}) collective-permute-start(bf16[320,1152]{1,0:T(8,128)(2,1)} %get-tuple-element.21), channel_id=1, source_target_pairs={{0,8},{1,65},{16,24},{17,81},{2,10},{3,67},{18,26},{19,83},{32,40}... | collective-permute-start | bytes 2211848 | tf_op jit(solution)/shard_map/ppermute | solution.py:46
  145.7 12.0 %collective-permute-start.23 = (bf16[320,1152]{1,0:T(8,128)(2,1)}, bf16[320,1152]{1,0:T(8,128)(2,1)S(1)}, u32[]{:S(2)}, u32[]{:S(2)}) collective-permute-start(bf16[320,1152]{1,0:T(8,128)(2,1)} %add.246), channel_id=1, source_target_pairs={{0,16},{1,19},{16,0},{17,3},{2,18},{3,17},{18,2},{19,1},{32,48},{3... | collective-permute-start | bytes 2211848 | tf_op jit(solution)/shard_map/ppermute | solution.py:46
  (25 other events, 290.4 us)

commit v2 on v0

v2 whole, which is shorter than its diff:
```python
import jax
import jax.numpy as jnp
from jax import lax
from jax.experimental import pallas as pl
from jax.experimental.pallas import tpu as pltpu
from jax.sharding import PartitionSpec as P

AXES = ("row", "col")
VMEM = pl.BlockSpec(memory_space=pltpu.VMEM)
SMEM = pl.BlockSpec(memory_space=pltpu.SMEM)
HBM = pl.BlockSpec(memory_space=pltpu.HBM)
BIG = pltpu.CompilerParams(vmem_limit_bytes=64 * 2**20)
F32 = jnp.float32
BF16 = jnp.bfloat16


def device(x, y, z, k):
    return (y % 4 * 2 + z % 2) * 16 + x % 4 * 4 + z % 4 // 2 * 2 + k


def z_mate(z, k):
    return z + 1 if (z + k) % 2 == 0 else z - 1


def pairs(move):
    out = []
    for x in range(4):
        for y in range(4):
            for z in range(4):
                for k in range(2):
                    out.append((device(x, y, z, k), device(*move(x, y, z, k))))
    return out


def ring(step):
    return pairs(lambda x, y, z, k: (x + step, y, z, k) if k == 0 else (x, y + step, z, k))


CORES = pairs(lambda x, y, z, k: (x, y, z, 1 - k))
MATES = pairs(lambda x, y, z, k: (x, y, z_mate(z, k), k))
STEPS = (0, 1, -1, 2)


def send(value, perm):
    return lax.ppermute(value, AXES, perm)


def normalize(raw):
    values = raw.astype(F32)
    inverse = lax.rsqrt(jnp.sum(values * values, axis=1, keepdims=True) + 1e-06)
    return values * inverse, inverse


def whoami():
    row, col = lax.axis_index("row"), lax.axis_index("col")
    return col // 4, row // 2, col // 2 % 2 * 2 + row % 2, col % 2


def prepare_kernel(image, text, other_image, other_text, labels, other_labels, own):
    core = lax.axis_index("col") % 2
    rows = image.shape[0]

    def fill(mine, other):
        own[:rows, :] = normalize(mine[...])[0].astype(BF16)
        own[rows : 2 * rows, :] = normalize(other[...])[0].astype(BF16)

    @pl.when(core == 0)
    def _():
        fill(image, other_image)

    @pl.when(core == 1)
    def _():
        fill(text, other_text)

    line = lax.broadcasted_iota(jnp.int32, (16, rows), 0)
    digits = jnp.zeros((16, rows), F32)
    for k, label in enumerate((labels[...], other_labels[...])):
        high = lax.shift_right_logical(label, 8).astype(F32)
        low = jnp.bitwise_and(label, 255).astype(F32)
        digits = jnp.where(line == 2 * k, high, jnp.where(line == 2 * k + 1, low, digits))
    own[2 * rows :, :] = jnp.zeros((16, image.shape[1]), BF16)
    own[2 * rows :, :rows] = digits.astype(BF16)


def prepare(image, text, labels):
    rows, width = image.shape
    labels = labels.reshape(1, rows)
    return pl.pallas_call(
        prepare_kernel,
        out_shape=jax.ShapeDtypeStruct((2 * rows + 16, width), BF16),
        in_specs=[VMEM] * 6,
        out_specs=VMEM,
        compiler_params=BIG,
        name="prepare",
    )(image, text, send(image, CORES), send(text, CORES), labels, send(labels, CORES))


class Blocks:
    def __init__(self, mine, other, images, digits, texts, labels, sems):
        self.mine, self.other = mine, other
        self.images, self.digits, self.texts, self.labels, self.sems = images, digits, texts, labels, sems
        self.rows = mine[0].shape[0] - 16
        self.half = self.rows // 2
        self.pieces = len(mine)

    def copies(self, image_from, text_from, offset):
        rows, half = self.rows, self.half
        text, image = [], []
        for p in range(self.pieces):
            text.append((text_from[p].at[pl.ds(offset, half)], self.texts.at[pl.ds(p * half, half)]))
            image.append((image_from[p].at[pl.ds(0, rows)], self.images.at[pl.ds(p * rows, rows)]))
            image.append((image_from[p].at[pl.ds(rows, 16)], self.digits.at[p]))
        return [(a, b, self.sems.at[i]) for i, (a, b) in enumerate(text + image)]

    def each(self, core, wait, which):
        part = {"text": slice(0, self.pieces), "image": slice(self.pieces, None)}[which]

        def act(copies):
            for copy in copies[part]:
                copy = pltpu.make_async_copy(*copy)
                copy.wait() if wait else copy.start()

        @pl.when(core == 0)
        def _():
            act(self.copies(self.mine, self.other, self.half))

        @pl.when(core == 1)
        def _():
            act(self.copies(self.other, self.mine, 0))

    def set_labels(self):
        for p in range(self.pieces):
            digit = self.digits[p].astype(F32)
            for k in range(2):
                number = digit[2 * k : 2 * k + 1, : self.half] * 256.0 + digit[2 * k + 1 : 2 * k + 2, : self.half]
                start = p * self.rows + k * self.half
                self.labels[:, start : start + self.half] = jnp.broadcast_to(number, (8, self.half))


def set_coefficient(scale, mate, texts, images, labels, out):
    a, b = 0.5 * scale[0][0], 0.5 * scale[1][0]
    half = texts.shape[0] // 4
    x, y, z, core = whoami()
    level = jnp.where(mate, jnp.where(z % 2 == 1, z + 1, z + 3) % 4, z)
    logits = lax.dot_general(texts[...], images[...], (((1,), (1,)), ((), ())), preferred_element_type=F32)
    label = labels[0:1, :]
    position = lax.broadcasted_iota(jnp.int32, (half, label.shape[1]), 0).astype(F32)
    for p, step in enumerate(STEPS):
        first = (device_at(x, y + step + 4, level, core) * half).astype(F32)
        part = slice(p * half, (p + 1) * half)
        shift = jnp.where(position == label - first, -0.5, 0.5)
        out[part, :] = (0.5 * jnp.tanh(logits[part, :] * a + b) + shift).astype(BF16)


def device_at(x, y, z, k):
    return (y % 4 * 2 + z % 2) * 16 + x * 4 + z // 2 * 2 + k


def along_text(coefficient, images):
    return jnp.dot(coefficient[...], images[...], preferred_element_type=F32)


def along_image(coefficient, texts):
    return lax.dot_general(coefficient[...], texts[...], (((0,), (0,)), ((), ())), preferred_element_type=F32)


def own_kernel(sharpness, shift, *refs):
    mine, other = refs[:4], refs[4:8]
    image_sum, text_sum = refs[8:10]
    images, digits, labels, texts, coefficient, sems = refs[10:]
    core = lax.axis_index("col") % 2
    group = Blocks(mine, other, images, digits, texts, labels, sems)
    for wait in (False, True):
        group.each(core, wait, "text")
        group.each(core, wait, "image")
    group.set_labels()
    set_coefficient((sharpness, shift), False, texts, images, labels, coefficient)
    text_sum[...] = along_text(coefficient, images)
    image_sum[...] = along_image(coefficient, texts)


def group_scratch(rows, width):
    return [
        pltpu.VMEM((4 * rows, width), BF16),
        pltpu.VMEM((4, 16, width), BF16),
        pltpu.VMEM((8, 4 * rows), F32),
    ]


def cost(quads, rows, width):
    flops = quads * 6 * 8 * rows * rows * width
    return pl.CostEstimate(flops=flops, bytes_accessed=quads * 20 * rows * width, transcendentals=quads * 8 * rows * rows)


def own_sums(scale, mine, other):
    rows, width = mine[0].shape[0] - 16, mine[0].shape[1]
    return pl.pallas_call(
        own_kernel,
        out_shape=(jax.ShapeDtypeStruct((4 * rows, width), F32), jax.ShapeDtypeStruct((2 * rows, width), F32)),
        in_specs=[SMEM] * 2 + [HBM] * 8,
        out_specs=(VMEM, VMEM),
        scratch_shapes=group_scratch(rows, width)
        + [
            pltpu.VMEM((2 * rows, width), BF16),
            pltpu.VMEM((2 * rows, 4 * rows), BF16),
            pltpu.SemaphoreType.DMA((12,)),
        ],
        compiler_params=BIG,
        cost_estimate=cost(1, rows, width),
        name="own_sums",
    )(*scale, *mine, *other)


LEAVING = (((1, 1, 3),), ((0, 1, 2),), ((0, 0, 1), (0, 3, 1), (1, 0, 1)))


def rest_kernel(sharpness, shift, *refs):
    scale = (sharpness, shift)
    own_mine, mate_mine, own_other, mate_other = refs[:4], refs[4:8], refs[8:12], refs[12:16]
    image_before, text_before = refs[16:18]
    keeps, aways = refs[18:21], refs[21:24]
    images, digits, labels, texts, image_total, text_total, coefficient, image_out, text_out = refs[24:33]
    sems, before_sem, out_sem = refs[33:]
    core = lax.axis_index("col") % 2
    rows = own_mine[0].shape[0] - 16
    half = rows // 2
    own = Blocks(own_mine, own_other, images.at[0], digits.at[0], texts.at[0], labels.at[0], sems.at[0])
    mate = Blocks(mate_mine, mate_other, images.at[1], digits.at[1], texts.at[1], labels.at[1], sems.at[1])
    before = [
        pltpu.make_async_copy(image_before, image_total.at[0], before_sem.at[0]),
        pltpu.make_async_copy(text_before, text_total.at[0], before_sem.at[1]),
    ]
    mate.each(core, False, "text")
    own.each(core, False, "image")
    before[0].start()
    own.each(core, False, "text")
    mate.each(core, False, "image")
    before[1].start()
    image_total[1] = jnp.zeros_like(image_total[1])
    text_total[1] = jnp.zeros_like(text_total[1])

    def flush(wait, which):
        def act(image_to, text_to):
            sem = 0
            for g, spans in enumerate(LEAVING):
                at = 0
                for group, first, count in spans:
                    for kind, source, target, size in (
                        (0, image_out, image_to[g], rows),
                        (1, text_out, text_to[g], half),
                    ):
                        if (kind, group) not in which:
                            sem += 1
                            continue
                        copy = pltpu.make_async_copy(
                            source.at[group, pl.ds(first * size, count * size)],
                            target.at[pl.ds(at * size, count * size)],
                            out_sem.at[sem],
                        )
                        copy.wait() if wait else copy.start()
                        sem += 1
                    at += count

        @pl.when(core == 0)
        def _():
            act(keeps, aways)

        @pl.when(core == 1)
        def _():
            act(aways, keeps)

    def block(q, _):
        i = jnp.minimum(q, 1)
        t = 1 - q % 2

        @pl.when(q == 0)
        def _():
            mate.each(core, True, "text")
            own.each(core, True, "image")
            own.set_labels()

        @pl.when(q == 1)
        def _():
            own.each(core, True, "text")
            mate.each(core, True, "image")
            mate.set_labels()
            before[1].wait()
            image_out[0] = image_total[0].astype(BF16)
            flush(False, ((0, 0),))

        @pl.when(q == 2)
        def _():
            text_out[0] = text_total[0].astype(BF16)
            flush(False, ((1, 0),))

        set_coefficient(scale, t == 1, texts.at[t], images.at[i], labels.at[i], coefficient)
        text_total[t] += along_text(coefficient, images.at[i])

        @pl.when(q == 0)
        def _():
            before[0].wait()

        image_total[i] += along_image(coefficient, texts.at[t])
        return 0

    lax.fori_loop(0, 3, block, 0)
    image_out[1] = image_total[1].astype(BF16)
    flush(False, ((0, 1),))
    text_out[1] = text_total[1].astype(BF16)
    flush(False, ((1, 1),))
    flush(True, ((0, 0), (0, 1), (1, 0), (1, 1)))


def rest_sums(scale, mine, other, before):
    rows, width = mine[0].shape[0] - 16, mine[0].shape[1]
    shapes = [jax.ShapeDtypeStruct((sum(n for _, _, n in spans) * rows, width), BF16) for spans in LEAVING]
    outs = pl.pallas_call(
        rest_kernel,
        out_shape=tuple(shapes * 2),
        in_specs=[SMEM] * 2 + [HBM] * 18,
        out_specs=(HBM,) * 6,
        scratch_shapes=[
            pltpu.VMEM((2, 4 * rows, width), BF16),
            pltpu.VMEM((2, 4, 16, width), BF16),
            pltpu.VMEM((2, 8, 4 * rows), F32),
            pltpu.VMEM((2, 2 * rows, width), BF16),
            pltpu.VMEM((2, 4 * rows, width), F32),
            pltpu.VMEM((2, 2 * rows, width), F32),
            pltpu.VMEM((2 * rows, 4 * rows), BF16),
            pltpu.VMEM((2, 4 * rows, width), BF16),
            pltpu.VMEM((2, 2 * rows, width), BF16),
            pltpu.SemaphoreType.DMA((2, 12)),
            pltpu.SemaphoreType.DMA((2,)),
            pltpu.SemaphoreType.DMA((10,)),
        ],
        compiler_params=BIG,
        cost_estimate=cost(3, rows, width),
        name="rest_sums",
    )(*scale, *mine, *other, *before)
    return outs[:3], outs[3:]


def join_kernel(pieces, extras, keep, got, *refs):
    extra, outs = refs[:extras], refs[extras : extras + len(pieces)]
    kept, came, more, sent, sems, out_sems = refs[extras + len(pieces) :]
    core = lax.axis_index("col") % 2
    rows = outs[0].shape[0]
    half = rows // 2

    def loads(size):
        out = []
        for i, p in enumerate(pieces):
            for j, (a, b) in enumerate(((keep, kept), (got, came))):
                out.append(
                    pltpu.make_async_copy(
                        a.at[pl.ds(p * size, size)], b.at[pl.ds(i * rows, size)], sems.at[2 * i + j]
                    )
                )
        return out

    added = [pltpu.make_async_copy(extra[i], more.at[i], out_sems.at[len(pieces) + i]) for i in range(extras)]

    def run(size):
        copies = loads(size)
        for copy in copies + added:
            copy.start()
        stores = []
        for i, out in enumerate(outs):
            copies[2 * i].wait()
            copies[2 * i + 1].wait()
            part = slice(i * rows, (i + 1) * rows)
            first, second = slice(i * rows, i * rows + half), slice(i * rows + half, (i + 1) * rows)
            if i == len(outs) - 1:
                for copy in added:
                    copy.wait()
            if size == rows:
                total = kept[part, :].astype(F32) + came[part, :].astype(F32)
                if extras and i == len(outs) - 1:
                    total = total + more[0].astype(F32)
                sent[part, :] = total.astype(BF16)
            elif extras and i == len(outs) - 1:
                sent[first, :] = (kept[first, :].astype(F32) + more[0, :half, :].astype(F32)).astype(BF16)
                sent[second, :] = (came[first, :].astype(F32) + more[0, half:, :].astype(F32)).astype(BF16)
            else:
                sent[first, :] = kept[first, :]
                sent[second, :] = came[first, :]
            store = pltpu.make_async_copy(sent.at[pl.ds(i * rows, rows)], out, out_sems.at[i])
            store.start()
            stores.append(store)
        for store in stores:
            store.wait()

    @pl.when(core == 0)
    def _():
        run(rows)

    @pl.when(core == 1)
    def _():
        run(half)


def join(keep, got, rows, pieces, extra=()):
    width = keep.shape[1]
    count = len(pieces)
    shape = jax.ShapeDtypeStruct((rows, width), BF16)
    return pl.pallas_call(
        lambda *refs: join_kernel(pieces, len(extra), *refs),
        out_shape=(shape,) * count,
        in_specs=[HBM] * (2 + len(extra)),
        out_specs=(HBM,) * count,
        scratch_shapes=[
            pltpu.VMEM((count * rows, width), BF16),
            pltpu.VMEM((count * rows, width), BF16),
            pltpu.VMEM((1, rows, width), BF16),
            pltpu.VMEM((count * rows, width), BF16),
            pltpu.SemaphoreType.DMA((2 * count,)),
            pltpu.SemaphoreType.DMA((count + 1,)),
        ],
        compiler_params=BIG,
        name="join",
    )(keep, got, *extra)


def total_of(refs):
    total = refs[0][...].astype(F32)
    for ref in refs[1:]:
        total = total + ref[...].astype(F32)
    return total


def add_kernel(*refs):
    refs[-1][...] = total_of(refs[:-1]).astype(refs[-1].dtype)


def add(*values):
    return pl.pallas_call(
        add_kernel,
        out_shape=jax.ShapeDtypeStruct(values[0].shape, BF16),
        in_specs=[VMEM] * len(values),
        out_specs=VMEM,
        compiler_params=BIG,
        name="add",
    )(*values)


def split_kernel(*refs):
    total = total_of(refs[:-2])
    half = total.shape[0] // 2
    refs[-2][...] = total[:half, :]
    refs[-1][...] = total[half:, :]


def split_total(*values):
    shape = jax.ShapeDtypeStruct((values[0].shape[0] // 2, values[0].shape[1]), F32)
    return pl.pallas_call(
        split_kernel,
        out_shape=(shape, shape),
        in_specs=[VMEM] * len(values),
        out_specs=(VMEM, VMEM),
        compiler_params=BIG,
        name="split_total",
    )(*values)


def finish_kernel(scale, image, text, total, got, image_grad, text_grad):
    core = lax.axis_index("col") % 2

    def backward(raw, unit_grad):
        unit, inverse = normalize(raw[...])
        unit_grad = scale[0] * unit_grad[...]
        along = jnp.sum(unit * unit_grad, axis=1, keepdims=True)
        return inverse * (unit_grad - unit * along)

    @pl.when(core == 0)
    def _():
        image_grad[...] = backward(image, total)
        text_grad[...] = backward(text, got)

    @pl.when(core == 1)
    def _():
        image_grad[...] = backward(image, got)
        text_grad[...] = backward(text, total)


def finish(scale, image, text, total, got):
    shape = jax.ShapeDtypeStruct(image.shape, F32)
    return pl.pallas_call(
        finish_kernel,
        out_shape=(shape, shape),
        in_specs=[SMEM] + [VMEM] * 4,
        out_specs=(VMEM, VMEM),
        compiler_params=BIG,
        name="finish",
    )(scale, image, text, total, got)


def after(values, first):
    return lax.optimization_barrier((tuple(values), first))


def after(values, first):
    return list(lax.optimization_barrier((tuple(values), first))[0])


def shards(image, text, labels, sharpness, shift):
    scale = (sharpness, shift)
    rows = 2 * image.shape[0]
    own0 = prepare(image, text, labels)
    mate0 = send(own0, MATES)
    own = [own0] + [send(own0, ring(-d)) for d in STEPS[1:]]
    own = after(own, mate0)
    own_other = [send(piece, CORES) for piece in own]
    mate = [mate0] + [send(mate0, ring(-d)) for d in STEPS[1:3]] + [send(own[3], MATES)]
    before = own_sums(scale, own, own_other)
    mate = after(mate, before)
    mate_other = [send(piece, CORES) for piece in mate]
    keeps, aways = rest_sums(scale, own + mate, own_other + mate_other, before)

    gone = send(aways[0], CORES)
    mate_up, mate_down, far = join(keeps[0], gone, rows, (0, 1, 2))
    far = send(far, MATES)
    mate_up, mate_down = send(mate_up, ring(1)), send(mate_down, ring(-1))
    gone = send(after(aways[1:2], gone)[0], CORES)
    up, down = join(keeps[1], gone, rows, (0, 1))
    up, down = send(up, ring(1)), send(down, ring(-1))
    gone = send(after(aways[2:], gone)[0], CORES)
    own_part, mate_part = join(keeps[2], gone, rows, (0, 2))
    (far,) = join(keeps[2], gone, rows, (1,), (far,))
    far = send(far, ring(2))
    mate_total = send(add(mate_part, mate_up, mate_down), MATES)
    total, away = split_total(own_part, up, down, far, mate_total)
    return finish(sharpness, image, text, total, send(away, CORES))


def solution(mesh):
    spec = P(AXES, None)
    return jax.shard_map(
        shards,
        mesh=mesh,
        in_specs=(spec, spec, P(AXES), P(), P()),
        out_specs=(spec, spec),
        check_vma=False,
    )
```

time: 474 us -> 142 us (0.30)
  waiting for transfers between devices: 291 us -> 43.2 us
  matrix products: 84.1 us -> 0 us
  blocking collectives: 67.2 us -> 0 us
  Pallas kernels: 0 us -> 61.1 us
  starting transfers between devices: 0.16 us -> 33.4 us
  other arithmetic: 13.3 us -> 0 us
  between operations: 15.2 us -> 2.09 us
    reduce_scatter x2 -> x0, waiting for transfers between devices: 224 us -> none  [the longest x1 120 us: shards(): lax.psum_scatter(image_partial, 'col', scatter_dimension=0, tiled=True)]
    dot_general x11 -> x0, matrix products: 84.1 us -> none  [the longest x5 35.6 us: accumulate(): lax.dot_general(coefficient, image_block, (((0,), (0,)), ((), ())), prefe...]
    unnamed x1 -> x0, blocking collectives: 67.2 us -> none
    all_gather x2 -> x0, waiting for transfers between devices: 66.4 us -> none  [the longest x1 66.4 us: shards(): lax.all_gather(image_half, 'col', axis=0, tiled=True)]
    pallas_call x0 -> x10, Pallas kernels: none -> 61.1 us  [the longest x1 27.7 us: rest_sums(): pl.pallas_call(rest_kernel, out_shape=tuple(shapes * 2), in_specs=[SMEM]...]
    ppermute x0 -> x29, waiting for transfers between devices: none -> 43.2 us  [send(): return lax.ppermute(value, AXES, perm)]
    ppermute x0 -> x29, starting transfers between devices: none -> 33.4 us  [send(): return lax.ppermute(value, AXES, perm)]
    reduce_sum x4 -> x0, other arithmetic: 5.02 us -> none  [the longest x2 2.73 us: backward(): along = jnp.sum(unit * unit_grad, axis=1, keepdims=True)]
  transfers between devices with their start and end apart: 4 -> 29, of which waited for: 3 -> 15; matrix products, arithmetic and copies ran while one was open for 4% -> 0% of each run, Pallas kernels for 0% -> 17%
where the time goes in v2:
time: 142 us
  Pallas kernels  61.1 us (43%)
  waiting for transfers between devices  43.2 us (30%)
  starting transfers between devices  33.4 us (24%)
  local copies, waits for them, and re-layouts  2.17 us (2%)
  between operations  2.09 us (1%)
    ppermute x29, waiting for transfers between devices, send(): return lax.ppermute(value, AXES, perm)  43.2 us
    ppermute x29, starting transfers between devices, send(): return lax.ppermute(value, AXES, perm)  33.4 us
    pallas_call x1, Pallas kernels, rest_sums(): pl.pallas_call(rest_kernel, out_shape=tuple(shapes * 2), in_specs=[SMEM]...  27.7 us
    pallas_call x1, Pallas kernels, own_sums(): pl.pallas_call(own_kernel, out_shape=(jax.ShapeDtypeStruct((4 * rows, wid...  12 us
    pallas_call x4, Pallas kernels, join(): pl.pallas_call(lambda *refs: join_kernel(pieces, len(extra), *refs), out_...  9.63 us
    pallas_call x1, Pallas kernels, split_total(): pl.pallas_call(split_kernel, out_shape=(shape, shape), in_specs=[VMEM] *...  3.33 us
    pallas_call x1, Pallas kernels, finish(): pl.pallas_call(finish_kernel, out_shape=(shape, shape), in_specs=[SMEM] +...  3.21 us
  transfers between devices with their start and end apart: 29, of which 15 were waited for; matrix products, arithmetic and copies ran while one was open for 0% of the time, Pallas kernels for 17%

profile of v2, /device:TPU:1, one launch (start us, length us, event | category | flops | bytes accessed | tf_op | source)
XLA Modules:
  0.0 142.0 jit_solution(17753992574667491395)
XLA Ops:
  4.3 2.5 %prepare.1.refs_0_ = bf16[336,1152]{1,0:T(8,128)(2,1)} custom-call(bf16[160,1152]{1,0:T(8,128)(2,1)} %image.3, bf16[160,1152]{1,0:T(8,128)(2,1)} %text.3, bf16[160,1152]{1,0:T(8,128)(2,1)} %collective-permute-done.other_image, bf16[160,1152]{1,0:T(8,128)(2,1)} %collective-permute-done.1.other_text, s32[1,160]{1,0:T(1,128)} %bitcast.2, ...), custom_call_target="tpu_custom_call" | custom-call | tf_op jit(solution)/shard_map/prepare/pallas_call | solution.py:88
  6.8 3.8 %collective-permute-start.6 = (bf16[336,1152]{1,0:T(8,128)(2,1)}, bf16[336,1152]{1,0:T(8,128)(2,1)}, u32[]{:S(2)}, u32[]{:S(2)}) collective-permute-start(bf16[336,1152]{1,0:T(8,128)(2,1)} %prepare.1.refs_0_), channel_id=1, source_target_pairs={{0,16},{1,19},{16,0},{17,3},{2,18},{3,17},{18,2},{19,1},{32,48},{3... | collective-permute-start | bytes 2322440 | tf_op jit(solution)/shard_map/ppermute | solution.py:45
  10.6 2.9 %collective-permute-start.5 = (bf16[336,1152]{1,0:T(8,128)(2,1)}, bf16[336,1152]{1,0:T(8,128)(2,1)}, u32[]{:S(2)}, u32[]{:S(2)}) collective-permute-start(bf16[336,1152]{1,0:T(8,128)(2,1)} %prepare.1.refs_0_), channel_id=1, source_target_pairs={{0,8},{1,65},{16,24},{17,81},{2,10},{3,67},{18,26},{19,83},{32,40}... | collective-permute-start | bytes 2322440 | tf_op jit(solution)/shard_map/ppermute | solution.py:45
  16.2 4.3 %collective-permute-done.6.refs_4_ = bf16[336,1152]{1,0:T(8,128)(2,1)} collective-permute-done((bf16[336,1152]{1,0:T(8,128)(2,1)}, bf16[336,1152]{1,0:T(8,128)(2,1)}, u32[]{:S(2)}, u32[]{:S(2)}) %collective-permute-start.6) | collective-permute-done | bytes 774176 | tf_op jit(solution)/shard_map/ppermute | solution.py:45
  20.5 2.8 %collective-permute-done.5.refs_3_ = bf16[336,1152]{1,0:T(8,128)(2,1)} collective-permute-done((bf16[336,1152]{1,0:T(8,128)(2,1)}, bf16[336,1152]{1,0:T(8,128)(2,1)}, u32[]{:S(2)}, u32[]{:S(2)}) %collective-permute-start.5) | collective-permute-done | bytes 774176 | tf_op jit(solution)/shard_map/ppermute | solution.py:45
  23.3 8.1 %collective-permute-done.4.refs_2_ = bf16[336,1152]{1,0:T(8,128)(2,1)S(1)} collective-permute-done((bf16[336,1152]{1,0:T(8,128)(2,1)}, bf16[336,1152]{1,0:T(8,128)(2,1)S(1)}, u32[]{:S(2)}, u32[]{:S(2)}) %collective-permute-start.4) | collective-permute-done | bytes 774176 | tf_op jit(solution)/shard_map/ppermute | solution.py:45
  35.3 2.3 %collective-permute-start.7 = (bf16[336,1152]{1,0:T(8,128)(2,1)}, bf16[336,1152]{1,0:T(8,128)(2,1)}, u32[]{:S(2)}, u32[]{:S(2)}) collective-permute-start(bf16[336,1152]{1,0:T(8,128)(2,1)} %collective-permute-done.6.refs_4_), channel_id=1, source_target_pairs={{0,12},{1,97},{16,28},{17,113},{2,14},{3,99},{18,30},{19,115},{32,... | collective-permute-start | bytes 2322440 | tf_op jit(solution)/shard_map/ppermute | solution.py:45
  42.0 12.0 %own_sums.1 = (f32[1280,1152]{1,0:T(8,128)}, f32[640,1152]{1,0:T(8,128)}) custom-call(f32[1]{0:T(128)S(6)} %copy.7.sharpness.scale, f32[1]{0:T(128)S(6)} %copy.8.shift, bf16[336,1152]{1,0:T(8,128)(2,1)} %prepare.1.refs_0_, bf16[336,1152]{1,0:T(8,128)(2,1)} %copy-done.1, bf16[336,1152]{1,0:T(8,128)(2,1)} %copy-done, ...), custom_call_target="tpu_custom_call" | custom-call | flops 5662310400 | bytes 7372800 | tf_op jit(solution)/shard_map/own_sums/pallas_call | solution.py:197
  60.1 27.7 %rest_sums.1 = (bf16[960,1152]{1,0:T(8,128)(2,1)}, bf16[640,1152]{1,0:T(8,128)(2,1)}, bf16[960,1152]{1,0:T(8,128)(2,1)}, bf16[960,1152]{1,0:T(8,128)(2,1)}, bf16...) custom-call(f32[1]{0:T(128)S(6)} %copy.7.sharpness.scale, f32[1]{0:T(128)S(6)} %copy.8.shift, ...), custom_call_target="tpu_custom_call" | custom-call | flops 16986931200 | bytes 22118400 | tf_op jit(solution)/shard_map/rest_sums/pallas_call | solution.py:317
  88.0 4.6 %collective-permute-done.18.refs_1_ = bf16[960,1152]{1,0:T(8,128)(2,1)} collective-permute-done((bf16[960,1152]{1,0:T(8,128)(2,1)}, bf16[960,1152]{1,0:T(8,128)(2,1)}, u32[]{:S(2)}, u32[]{:S(2)}) %collective-permute-start.18) | collective-permute-done | bytes 2211872 | tf_op jit(solution)/shard_map/ppermute | solution.py:45
  92.7 3.5 %collective-permute-done.19.refs_1_ = bf16[640,1152]{1,0:T(8,128)(2,1)} collective-permute-done((bf16[640,1152]{1,0:T(8,128)(2,1)}, bf16[640,1152]{1,0:T(8,128)(2,1)}, u32[]{:S(2)}, u32[]{:S(2)}) %collective-permute-start.19) | collective-permute-done | bytes 1474592 | tf_op jit(solution)/shard_map/ppermute | solution.py:45
  96.3 2.6 %join.6 = (bf16[320,1152]{1,0:T(8,128)(2,1)}, bf16[320,1152]{1,0:T(8,128)(2,1)}, bf16[320,1152]{1,0:T(8,128)(2,1)}) custom-call(bf16[960,1152]{1,0:T(8,128)(2,1)} %get-tuple-element.49.refs_0_, bf16[960,1152]{1,0:T(8,128)(2,1)} %collective-permute-done.18.refs_1_), custom_call_target="tpu_custom_call" | custom-call | tf_op jit(solution)/shard_map/join/pallas_call | solution.py:406
  99.0 2.7 %collective-permute-start.26 = (bf16[320,1152]{1,0:T(8,128)(2,1)}, bf16[320,1152]{1,0:T(8,128)(2,1)}, u32[]{:S(2)}, u32[]{:S(2)}) collective-permute-start(bf16[320,1152]{1,0:T(8,128)(2,1)} %get-tuple-element.53), channel_id=1, source_target_pairs={{0,12},{1,97},{16,28},{17,113},{2,14},{3,99},{18,30},{19,115},{32,... | collective-permute-start | bytes 2211848 | tf_op jit(solution)/shard_map/ppermute | solution.py:45
  103.9 2.3 %join.5 = (bf16[320,1152]{1,0:T(8,128)(2,1)}, bf16[320,1152]{1,0:T(8,128)(2,1)}) custom-call(bf16[640,1152]{1,0:T(8,128)(2,1)} %get-tuple-element.46.refs_0_, bf16[640,1152]{1,0:T(8,128)(2,1)} %collective-permute-done.19.refs_1_), custom_call_target="tpu_custom_call" | custom-call | tf_op jit(solution)/shard_map/join/pallas_call | solution.py:406
  106.3 2.7 %collective-permute-start.22 = (bf16[320,1152]{1,0:T(8,128)(2,1)}, bf16[320,1152]{1,0:T(8,128)(2,1)}, u32[]{:S(2)}, u32[]{:S(2)}) collective-permute-start(bf16[320,1152]{1,0:T(8,128)(2,1)} %get-tuple-element.48), channel_id=1, source_target_pairs={{0,12},{1,97},{16,28},{17,113},{2,14},{3,99},{18,30},{19,115},{32,... | collective-permute-start | bytes 2211848 | tf_op jit(solution)/shard_map/ppermute | solution.py:45
  109.0 2.3 %join.4 = (bf16[320,1152]{1,0:T(8,128)(2,1)}, bf16[320,1152]{1,0:T(8,128)(2,1)}) custom-call(bf16[960,1152]{1,0:T(8,128)(2,1)} %get-tuple-element.39.refs_0_, bf16[960,1152]{1,0:T(8,128)(2,1)} %collective-permute-done.20.refs_1_), custom_call_target="tpu_custom_call" | custom-call | tf_op jit(solution)/shard_map/join/pallas_call | solution.py:406
  111.3 2.7 %add.1 = bf16[320,1152]{1,0:T(8,128)(2,1)} custom-call(bf16[320,1152]{1,0:T(8,128)(2,1)} %get-tuple-element.51.refs_0_, bf16[320,1152]{1,0:T(8,128)(2,1)} %collective-permute-done.25.refs_1_, bf16[320,1152]{1,0:T(8,128)(2,1)} %collective-permute-done.26.refs_2_), custom_call_target="tpu_custom_call" | custom-call | tf_op jit(solution)/shard_map/add/pallas_call | solution.py:436
  116.0 2.4 %join.7 = bf16[320,1152]{1,0:T(8,128)(2,1)} custom-call(bf16[960,1152]{1,0:T(8,128)(2,1)} %get-tuple-element.39.refs_0_, bf16[960,1152]{1,0:T(8,128)(2,1)} %collective-permute-done.20.refs_1_, bf16[320,1152]{1,0:T(8,128)(2,1)} %collective-permute-done.23.refs_2_), custom_call_target="tpu_custom_call" | custom-call | tf_op jit(solution)/shard_map/join/pallas_call | solution.py:406
  118.4 2.7 %collective-permute-start.24 = (bf16[320,1152]{1,0:T(8,128)(2,1)}, bf16[320,1152]{1,0:T(8,128)(2,1)}, u32[]{:S(2)}, u32[]{:S(2)}) collective-permute-start(bf16[320,1152]{1,0:T(8,128)(2,1)} %join.7), channel_id=1, source_target_pairs={{0,8},{1,65},{16,24},{17,81},{2,10},{3,67},{18,26},{19,83},{32,40}... | collective-permute-start | bytes 2211848 | tf_op jit(solution)/shard_map/ppermute | solution.py:45
  121.1 5.0 %collective-permute-done.27.refs_4_ = bf16[320,1152]{1,0:T(8,128)(2,1)} collective-permute-done((bf16[320,1152]{1,0:T(8,128)(2,1)}, bf16[320,1152]{1,0:T(8,128)(2,1)}, u32[]{:S(2)}, u32[]{:S(2)}) %collective-permute-start.27) | collective-permute-done | bytes 737312 | tf_op jit(solution)/shard_map/ppermute | solution.py:45
  126.1 4.8 %collective-permute-done.24.refs_3_ = bf16[320,1152]{1,0:T(8,128)(2,1)} collective-permute-done((bf16[320,1152]{1,0:T(8,128)(2,1)}, bf16[320,1152]{1,0:T(8,128)(2,1)}, u32[]{:S(2)}, u32[]{:S(2)}) %collective-permute-start.24) | collective-permute-done | bytes 737312 | tf_op jit(solution)/shard_map/ppermute | solution.py:45
  130.9 3.3 %split_total.1 = (f32[160,1152]{1,0:T(8,128)}, f32[160,1152]{1,0:T(8,128)}) custom-call(bf16[320,1152]{1,0:T(8,128)(2,1)} %get-tuple-element.45.refs_0_, bf16[320,1152]{1,0:T(8,128)(2,1)} %collective-permute-done.21.refs_1_, bf16[320,1152]{1,0:T(8,128)(2,1)} %collective-permute-done.22.refs_2_, bf16[320,1152]{1,0:T(8,128)(2,1)} %collective-permute-done.24.refs_3_, ...), custom_call_target="tpu_custom_call" | custom-call | tf_op jit(solution)/shard_map/split_total/pallas_call | solution.py:455
  134.2 2.4 %collective-permute-start.28 = (f32[160,1152]{1,0:T(8,128)}, f32[160,1152]{1,0:T(8,128)}, u32[]{:S(2)}, u32[]{:S(2)}) collective-permute-start(f32[160,1152]{1,0:T(8,128)} %get-tuple-element.55), channel_id=1, source_target_pairs={{0,1},{1,0},{16,17},{17,16},{2,3},{3,2},{18,19},{19,18},{32,33},{3... | collective-permute-start | bytes 2211848 | tf_op jit(solution)/shard_map/ppermute | solution.py:45
  138.8 3.2 %finish.1 = (f32[160,1152]{1,0:T(8,128)}, f32[160,1152]{1,0:T(8,128)}) custom-call(f32[1]{0:T(128)S(6)} %copy.7.sharpness.scale, bf16[160,1152]{1,0:T(8,128)(2,1)} %image.3, bf16[160,1152]{1,0:T(8,128)(2,1)} %text.3, f32[160,1152]{1,0:T(8,128)} %get-tuple-element.54.total, f32[160,1152]{1,0:T(8,128)} %collective-permute-done.28.got), custom_call_target="tpu_custom_call" | custom-call | tf_op jit(solution)/shard_map/finish/pallas_call | solution.py:487
  (54 shorter events, 26.3 us)
Async XLA Ops:
  0.6 3.7 %collective-permute-start = (bf16[160,1152]{1,0:T(8,128)(2,1)}, bf16[160,1152]{1,0:T(8,128)(2,1)}, u32[]{:S(2)}, u32[]{:S(2)}) collective-permute-start(bf16[160,1152]{1,0:T(8,128)(2,1)} %image.3), channel_id=1, source_target_pairs={{0,1},{1,0},{16,17},{17,16},{2,3},{3,2},{18,19},{19,18},{32,33},{3... | collective-permute-start | bytes 1105928 | tf_op jit(solution)/shard_map/ppermute | solution.py:45
  6.8 13.7 %collective-permute-start.6 = (bf16[336,1152]{1,0:T(8,128)(2,1)}, bf16[336,1152]{1,0:T(8,128)(2,1)}, u32[]{:S(2)}, u32[]{:S(2)}) collective-permute-start(bf16[336,1152]{1,0:T(8,128)(2,1)} %prepare.1.refs_0_), channel_id=1, source_target_pairs={{0,16},{1,19},{16,0},{17,3},{2,18},{3,17},{18,2},{19,1},{32,48},{3... | collective-permute-start | bytes 2322440 | tf_op jit(solution)/shard_map/ppermute | solution.py:45
  10.6 12.7 %collective-permute-start.5 = (bf16[336,1152]{1,0:T(8,128)(2,1)}, bf16[336,1152]{1,0:T(8,128)(2,1)}, u32[]{:S(2)}, u32[]{:S(2)}) collective-permute-start(bf16[336,1152]{1,0:T(8,128)(2,1)} %prepare.1.refs_0_), channel_id=1, source_target_pairs={{0,8},{1,65},{16,24},{17,81},{2,10},{3,67},{18,26},{19,83},{32,40}... | collective-permute-start | bytes 2322440 | tf_op jit(solution)/shard_map/ppermute | solution.py:45
  13.5 17.8 %collective-permute-start.4 = (bf16[336,1152]{1,0:T(8,128)(2,1)}, bf16[336,1152]{1,0:T(8,128)(2,1)S(1)}, u32[]{:S(2)}, u32[]{:S(2)}) collective-permute-start(bf16[336,1152]{1,0:T(8,128)(2,1)} %prepare.1.refs_0_), channel_id=1, source_target_pairs={{0,4},{1,33},{16,20},{17,49},{2,6},{3,35},{18,22},{19,51},{32,36},... | collective-permute-start | bytes 2322440 | tf_op jit(solution)/shard_map/ppermute | solution.py:45
  13.9 17.8 %collective-permute-start.3 = (bf16[336,1152]{1,0:T(8,128)(2,1)}, bf16[336,1152]{1,0:T(8,128)(2,1)S(1)}, u32[]{:S(2)}, u32[]{:S(2)}) collective-permute-start(bf16[336,1152]{1,0:T(8,128)(2,1)} %prepare.1.refs_0_), channel_id=1, source_target_pairs={{0,12},{1,97},{16,28},{17,113},{2,14},{3,99},{18,30},{19,115},{32,... | collective-permute-start | bytes 2322440 | tf_op jit(solution)/shard_map/ppermute | solution.py:45
  31.7 5.9 %collective-permute-start.11 = (bf16[336,1152]{1,0:T(8,128)(2,1)S(1)}, bf16[336,1152]{1,0:T(8,128)(2,1)S(1)}, u32[]{:S(2)}, u32[]{:S(2)}) collective-permute-start(bf16[336,1152]{1,0:T(8,128)(2,1)S(1)} %collective-permute-done.3.refs_1_), channel_id=1, source_target_pairs={{0,1},{1,0},{16,17},{17,16},{2,3},{3,2},{18,19},{19,18},{32,33},{3... | collective-permute-start | bytes 2322440 | tf_op jit(solution)/shard_map/ppermute | solution.py:45
  32.3 8.8 %collective-permute-start.12 = (bf16[336,1152]{1,0:T(8,128)(2,1)S(1)}, bf16[336,1152]{1,0:T(8,128)(2,1)S(1)}, u32[]{:S(2)}, u32[]{:S(2)}) collective-permute-start(bf16[336,1152]{1,0:T(8,128)(2,1)S(1)} %collective-permute-done.4.refs_2_), channel_id=1, source_target_pairs={{0,1},{1,0},{16,17},{17,16},{2,3},{3,2},{18,19},{19,18},{32,33},{3... | collective-permute-start | bytes 2322440 | tf_op jit(solution)/shard_map/ppermute | solution.py:45
  32.6 9.4 %collective-permute-start.13 = (bf16[336,1152]{1,0:T(8,128)(2,1)}, bf16[336,1152]{1,0:T(8,128)(2,1)}, u32[]{:S(2)}, u32[]{:S(2)}) collective-permute-start(bf16[336,1152]{1,0:T(8,128)(2,1)} %collective-permute-done.5.refs_3_), channel_id=1, source_target_pairs={{0,1},{1,0},{16,17},{17,16},{2,3},{3,2},{18,19},{19,18},{32,33},{3... | collective-permute-start | bytes 2322440 | tf_op jit(solution)/shard_map/ppermute | solution.py:45
  32.8 21.3 %collective-permute-start.8 = (bf16[336,1152]{1,0:T(8,128)(2,1)}, bf16[336,1152]{1,0:T(8,128)(2,1)}, u32[]{:S(2)}, u32[]{:S(2)}) collective-permute-start(bf16[336,1152]{1,0:T(8,128)(2,1)} %collective-permute-done.6.refs_4_), channel_id=1, source_target_pairs={{0,4},{1,33},{16,20},{17,49},{2,6},{3,35},{18,22},{19,51},{32,36},... | collective-permute-start | bytes 2322440 | tf_op jit(solution)/shard_map/ppermute | solution.py:45
  35.3 18.8 %collective-permute-start.7 = (bf16[336,1152]{1,0:T(8,128)(2,1)}, bf16[336,1152]{1,0:T(8,128)(2,1)}, u32[]{:S(2)}, u32[]{:S(2)}) collective-permute-start(bf16[336,1152]{1,0:T(8,128)(2,1)} %collective-permute-done.6.refs_4_), channel_id=1, source_target_pairs={{0,12},{1,97},{16,28},{17,113},{2,14},{3,99},{18,30},{19,115},{32,... | collective-permute-start | bytes 2322440 | tf_op jit(solution)/shard_map/ppermute | solution.py:45
  38.5 15.5 %collective-permute-start.9 = (bf16[336,1152]{1,0:T(8,128)(2,1)}, bf16[336,1152]{1,0:T(8,128)(2,1)}, u32[]{:S(2)}, u32[]{:S(2)}) collective-permute-start(bf16[336,1152]{1,0:T(8,128)(2,1)} %collective-permute-done.5.refs_3_), channel_id=1, source_target_pairs={{0,16},{1,19},{16,0},{17,3},{2,18},{3,17},{18,2},{19,1},{32,48},{3... | collective-permute-start | bytes 2322440 | tf_op jit(solution)/shard_map/ppermute | solution.py:45
  54.2 3.7 %collective-permute-start.15 = (bf16[336,1152]{1,0:T(8,128)(2,1)}, bf16[336,1152]{1,0:T(8,128)(2,1)}, u32[]{:S(2)}, u32[]{:S(2)}) collective-permute-start(bf16[336,1152]{1,0:T(8,128)(2,1)} %collective-permute-done.7.refs_5_), channel_id=1, source_target_pairs={{0,1},{1,0},{16,17},{17,16},{2,3},{3,2},{18,19},{19,18},{32,33},{3... | collective-permute-start | bytes 2322440 | tf_op jit(solution)/shard_map/ppermute | solution.py:45
  54.7 4.3 %collective-permute-start.16 = (bf16[336,1152]{1,0:T(8,128)(2,1)}, bf16[336,1152]{1,0:T(8,128)(2,1)}, u32[]{:S(2)}, u32[]{:S(2)}) collective-permute-start(bf16[336,1152]{1,0:T(8,128)(2,1)} %collective-permute-done.8.refs_6_), channel_id=1, source_target_pairs={{0,1},{1,0},{16,17},{17,16},{2,3},{3,2},{18,19},{19,18},{32,33},{3... | collective-permute-start | bytes 2322440 | tf_op jit(solution)/shard_map/ppermute | solution.py:45
  54.8 5.3 %collective-permute-start.17 = (bf16[336,1152]{1,0:T(8,128)(2,1)}, bf16[336,1152]{1,0:T(8,128)(2,1)}, u32[]{:S(2)}, u32[]{:S(2)}) collective-permute-start(bf16[336,1152]{1,0:T(8,128)(2,1)} %collective-permute-done.9.refs_7_), channel_id=1, source_target_pairs={{0,1},{1,0},{16,17},{17,16},{2,3},{3,2},{18,19},{19,18},{32,33},{3... | collective-permute-start | bytes 2322440 | tf_op jit(solution)/shard_map/ppermute | solution.py:45
  87.8 4.7 %collective-permute-start.18 = (bf16[960,1152]{1,0:T(8,128)(2,1)}, bf16[960,1152]{1,0:T(8,128)(2,1)}, u32[]{:S(2)}, u32[]{:S(2)}) collective-permute-start(bf16[960,1152]{1,0:T(8,128)(2,1)} %get-tuple-element.42), channel_id=1, source_target_pairs={{0,1},{1,0},{16,17},{17,16},{2,3},{3,2},{18,19},{19,18},{32,33},{3... | collective-permute-start | bytes 6635528 | tf_op jit(solution)/shard_map/ppermute | solution.py:45
  96.2 10.1 %collective-permute-start.20 = (bf16[960,1152]{1,0:T(8,128)(2,1)}, bf16[960,1152]{1,0:T(8,128)(2,1)}, u32[]{:S(2)}, u32[]{:S(2)}) collective-permute-start(bf16[960,1152]{1,0:T(8,128)(2,1)} %get-tuple-element.44), channel_id=1, source_target_pairs={{0,1},{1,0},{16,17},{17,16},{2,3},{3,2},{18,19},{19,18},{32,33},{3... | collective-permute-start | bytes 6635528 | tf_op jit(solution)/shard_map/ppermute | solution.py:45
  98.9 12.4 %collective-permute-start.25 = (bf16[320,1152]{1,0:T(8,128)(2,1)}, bf16[320,1152]{1,0:T(8,128)(2,1)}, u32[]{:S(2)}, u32[]{:S(2)}) collective-permute-start(bf16[320,1152]{1,0:T(8,128)(2,1)} %get-tuple-element.52), channel_id=1, source_target_pairs={{0,4},{1,33},{16,20},{17,49},{2,6},{3,35},{18,22},{19,51},{32,36},... | collective-permute-start | bytes 2211848 | tf_op jit(solution)/shard_map/ppermute | solution.py:45
  99.0 12.3 %collective-permute-start.26 = (bf16[320,1152]{1,0:T(8,128)(2,1)}, bf16[320,1152]{1,0:T(8,128)(2,1)}, u32[]{:S(2)}, u32[]{:S(2)}) collective-permute-start(bf16[320,1152]{1,0:T(8,128)(2,1)} %get-tuple-element.53), channel_id=1, source_target_pairs={{0,12},{1,97},{16,28},{17,113},{2,14},{3,99},{18,30},{19,115},{32,... | collective-permute-start | bytes 2211848 | tf_op jit(solution)/shard_map/ppermute | solution.py:45
  101.7 14.3 %collective-permute-start.23 = (bf16[320,1152]{1,0:T(8,128)(2,1)}, bf16[320,1152]{1,0:T(8,128)(2,1)}, u32[]{:S(2)}, u32[]{:S(2)}) collective-permute-start(bf16[320,1152]{1,0:T(8,128)(2,1)} %get-tuple-element.50), channel_id=1, source_target_pairs={{0,16},{1,19},{16,0},{17,3},{2,18},{3,17},{18,2},{19,1},{32,48},{3... | collective-permute-start | bytes 2211848 | tf_op jit(solution)/shard_map/ppermute | solution.py:45
  106.2 14.9 %collective-permute-start.21 = (bf16[320,1152]{1,0:T(8,128)(2,1)}, bf16[320,1152]{1,0:T(8,128)(2,1)}, u32[]{:S(2)}, u32[]{:S(2)}) collective-permute-start(bf16[320,1152]{1,0:T(8,128)(2,1)} %get-tuple-element.47), channel_id=1, source_target_pairs={{0,4},{1,33},{16,20},{17,49},{2,6},{3,35},{18,22},{19,51},{32,36},... | collective-permute-start | bytes 2211848 | tf_op jit(solution)/shard_map/ppermute | solution.py:45
  106.3 14.8 %collective-permute-start.22 = (bf16[320,1152]{1,0:T(8,128)(2,1)}, bf16[320,1152]{1,0:T(8,128)(2,1)}, u32[]{:S(2)}, u32[]{:S(2)}) collective-permute-start(bf16[320,1152]{1,0:T(8,128)(2,1)} %get-tuple-element.48), channel_id=1, source_target_pairs={{0,12},{1,97},{16,28},{17,113},{2,14},{3,99},{18,30},{19,115},{32,... | collective-permute-start | bytes 2211848 | tf_op jit(solution)/shard_map/ppermute | solution.py:45
  114.0 12.1 %collective-permute-start.27 = (bf16[320,1152]{1,0:T(8,128)(2,1)}, bf16[320,1152]{1,0:T(8,128)(2,1)}, u32[]{:S(2)}, u32[]{:S(2)}) collective-permute-start(bf16[320,1152]{1,0:T(8,128)(2,1)} %add.1), channel_id=1, source_target_pairs={{0,16},{1,19},{16,0},{17,3},{2,18},{3,17},{18,2},{19,1},{32,48},{3... | collective-permute-start | bytes 2211848 | tf_op jit(solution)/shard_map/ppermute | solution.py:45
  118.4 12.5 %collective-permute-start.24 = (bf16[320,1152]{1,0:T(8,128)(2,1)}, bf16[320,1152]{1,0:T(8,128)(2,1)}, u32[]{:S(2)}, u32[]{:S(2)}) collective-permute-start(bf16[320,1152]{1,0:T(8,128)(2,1)} %join.7), channel_id=1, source_target_pairs={{0,8},{1,65},{16,24},{17,81},{2,10},{3,67},{18,26},{19,83},{32,40}... | collective-permute-start | bytes 2211848 | tf_op jit(solution)/shard_map/ppermute | solution.py:45
  134.2 4.6 %collective-permute-start.28 = (f32[160,1152]{1,0:T(8,128)}, f32[160,1152]{1,0:T(8,128)}, u32[]{:S(2)}, u32[]{:S(2)}) collective-permute-start(f32[160,1152]{1,0:T(8,128)} %get-tuple-element.55), channel_id=1, source_target_pairs={{0,1},{1,0},{16,17},{17,16},{2,3},{3,2},{18,19},{19,18},{32,33},{3... | collective-permute-start | bytes 2211848 | tf_op jit(solution)/shard_map/ppermute | solution.py:45
  (10 other events, 20.1 us)

commit v3 on v2

--- a/solution.py
+++ b/solution.py
@@ -39,6 +39,8 @@
 CORES = pairs(lambda x, y, z, k: (x, y, z, 1 - k))
 MATES = pairs(lambda x, y, z, k: (x, y, z_mate(z, k), k))
 STEPS = (0, 1, -1, 2)
+GROUPS = (((0, False), (1, False), (-1, False), (0, True)), ((2, False), (1, True), (-1, True), (2, True)))
+CHUNK = 32
 
 
 def send(value, perm):
@@ -137,16 +139,19 @@
                 self.labels[:, start : start + self.half] = jnp.broadcast_to(number, (8, self.half))
 
 
-def set_coefficient(scale, mate, texts, images, labels, out):
+def set_coefficient(scale, late, texts, images, labels, out):
     a, b = 0.5 * scale[0][0], 0.5 * scale[1][0]
     half = texts.shape[0] // 4
     x, y, z, core = whoami()
-    level = jnp.where(mate, jnp.where(z % 2 == 1, z + 1, z + 3) % 4, z)
+    mate_z = jnp.where(z % 2 == 1, z + 1, z + 3) % 4
     logits = lax.dot_general(texts[...], images[...], (((1,), (1,)), ((), ())), preferred_element_type=F32)
     label = labels[0:1, :]
     position = lax.broadcasted_iota(jnp.int32, (half, label.shape[1]), 0).astype(F32)
-    for p, step in enumerate(STEPS):
-        first = (device_at(x, y + step + 4, level, core) * half).astype(F32)
+    for p in range(4):
+        (near_step, near_mate), (far_step, far_mate) = GROUPS[0][p], GROUPS[1][p]
+        one = device_at(x, y + near_step + 4, mate_z if near_mate else z, core)
+        two = device_at(x, y + far_step + 4, mate_z if far_mate else z, core)
+        first = (jnp.where(late, two, one) * half).astype(F32)
         part = slice(p * half, (p + 1) * half)
         shift = jnp.where(position == label - first, -0.5, 0.5)
         out[part, :] = (0.5 * jnp.tanh(logits[part, :] * a + b) + shift).astype(BF16)
@@ -166,8 +171,8 @@
 
 def own_kernel(sharpness, shift, *refs):
     mine, other = refs[:4], refs[4:8]
-    image_sum, text_sum = refs[8:10]
-    images, digits, labels, texts, coefficient, sems = refs[10:]
+    image_to, text_to = refs[8:10]
+    images, digits, labels, texts, coefficient, image_sum, text_sum, sems, out_sem = refs[10:]
     core = lax.axis_index("col") % 2
     group = Blocks(mine, other, images, digits, texts, labels, sems)
     for wait in (False, True):
@@ -176,7 +181,16 @@
     group.set_labels()
     set_coefficient((sharpness, shift), False, texts, images, labels, coefficient)
     text_sum[...] = along_text(coefficient, images)
-    image_sum[...] = along_image(coefficient, texts)
+    copies = [pltpu.make_async_copy(text_sum, text_to, out_sem.at[0])]
+    copies[0].start()
+    part = images.shape[0] // 2
+    for i in range(2):
+        here = pl.ds(i * part, part)
+        image_sum[here, :] = along_image(coefficient.at[:, here], texts)
+        copies.append(pltpu.make_async_copy(image_sum.at[here], image_to.at[here], out_sem.at[1 + i]))
+        copies[-1].start()
+    for copy in copies:
+        copy.wait()
 
 
 def group_scratch(rows, width):
@@ -198,12 +212,15 @@
         own_kernel,
         out_shape=(jax.ShapeDtypeStruct((4 * rows, width), F32), jax.ShapeDtypeStruct((2 * rows, width), F32)),
         in_specs=[SMEM] * 2 + [HBM] * 8,
-        out_specs=(VMEM, VMEM),
+        out_specs=(HBM, HBM),
         scratch_shapes=group_scratch(rows, width)
         + [
             pltpu.VMEM((2 * rows, width), BF16),
             pltpu.VMEM((2 * rows, 4 * rows), BF16),
+            pltpu.VMEM((4 * rows, width), F32),
+            pltpu.VMEM((2 * rows, width), F32),
             pltpu.SemaphoreType.DMA((12,)),
+            pltpu.SemaphoreType.DMA((3,)),
         ],
         compiler_params=BIG,
         cost_estimate=cost(1, rows, width),
@@ -211,7 +228,7 @@
     )(*scale, *mine, *other)
 
 
-LEAVING = (((1, 1, 3),), ((0, 1, 2),), ((0, 0, 1), (0, 3, 1), (1, 0, 1)))
+LEAVING = (((1, 1, 3),), ((0, 1, 2),), ((0, 0, 1), (1, 0, 1), (0, 3, 1)))
 
 
 def rest_kernel(sharpness, shift, *refs):
@@ -300,14 +317,17 @@
         def _():
             before[0].wait()
 
+        @pl.when(q == 2)
+        def _():
+            text_out[1] = text_total[1].astype(BF16)
+            flush(False, ((1, 1),))
+
         image_total[i] += along_image(coefficient, texts.at[t])
         return 0
 
     lax.fori_loop(0, 3, block, 0)
     image_out[1] = image_total[1].astype(BF16)
     flush(False, ((0, 1),))
-    text_out[1] = text_total[1].astype(BF16)
-    flush(False, ((1, 1),))
     flush(True, ((0, 0), (0, 1), (1, 0), (1, 1)))
 
 
@@ -368,22 +388,29 @@
         for i, out in enumerate(outs):
             copies[2 * i].wait()
             copies[2 * i + 1].wait()
-            part = slice(i * rows, (i + 1) * rows)
-            first, second = slice(i * rows, i * rows + half), slice(i * rows + half, (i + 1) * rows)
-            if i == len(outs) - 1:
+            last = extras and i == len(outs) - 1
+            if last:
                 for copy in added:
                     copy.wait()
-            if size == rows:
-                total = kept[part, :].astype(F32) + came[part, :].astype(F32)
-                if extras and i == len(outs) - 1:
-                    total = total + more[0].astype(F32)
-                sent[part, :] = total.astype(BF16)
-            elif extras and i == len(outs) - 1:
-                sent[first, :] = (kept[first, :].astype(F32) + more[0, :half, :].astype(F32)).astype(BF16)
-                sent[second, :] = (came[first, :].astype(F32) + more[0, half:, :].astype(F32)).astype(BF16)
-            else:
-                sent[first, :] = kept[first, :]
-                sent[second, :] = came[first, :]
+
+            def chunk(c, _):
+                here = pl.ds(pl.multiple_of(i * rows + c * CHUNK, CHUNK), CHUNK)
+                there = pl.ds(pl.multiple_of(i * rows + half + c * CHUNK, CHUNK), CHUNK)
+                if size == rows:
+                    total = kept[here, :].astype(F32) + came[here, :].astype(F32)
+                    if last:
+                        total = total + more[0, pl.ds(pl.multiple_of(c * CHUNK, CHUNK), CHUNK), :].astype(F32)
+                    sent[here, :] = total.astype(BF16)
+                    return 0
+                for source, target, offset in ((kept, here, 0), (came, there, half)):
+                    value = source[here, :]
+                    if last:
+                        extra_rows = pl.ds(pl.multiple_of(offset + c * CHUNK, CHUNK), CHUNK)
+                        value = (value.astype(F32) + more[0, extra_rows, :].astype(F32)).astype(BF16)
+                    sent[target, :] = value
+                return 0
+
+            lax.fori_loop(0, size // CHUNK, chunk, 0)
             store = pltpu.make_async_copy(sent.at[pl.ds(i * rows, rows)], out, out_sems.at[i])
             store.start()
             stores.append(store)
@@ -421,15 +448,26 @@
     )(keep, got, *extra)
 
 
-def total_of(refs):
-    total = refs[0][...].astype(F32)
+def each_chunk(rows, step):
+    def run(c, _):
+        step(pl.ds(pl.multiple_of(c * CHUNK, CHUNK), CHUNK), c)
+        return 0
+
+    lax.fori_loop(0, rows // CHUNK, run, 0)
+
+
+def total_of(refs, part):
+    total = refs[0][part, :].astype(F32)
     for ref in refs[1:]:
-        total = total + ref[...].astype(F32)
+        total = total + ref[part, :].astype(F32)
     return total
 
 
 def add_kernel(*refs):
-    refs[-1][...] = total_of(refs[:-1]).astype(refs[-1].dtype)
+    def step(part, c):
+        refs[-1][part, :] = total_of(refs[:-1], part).astype(refs[-1].dtype)
+
+    each_chunk(refs[-1].shape[0], step)
 
 
 def add(*values):
@@ -444,10 +482,14 @@
 
 
 def split_kernel(*refs):
-    total = total_of(refs[:-2])
-    half = total.shape[0] // 2
-    refs[-2][...] = total[:half, :]
-    refs[-1][...] = total[half:, :]
+    half = refs[-1].shape[0]
+
+    def step(part, c):
+        refs[-2][part, :] = total_of(refs[:-2], part)
+        other = pl.ds(pl.multiple_of(half + c * CHUNK, CHUNK), CHUNK)
+        refs[-1][part, :] = total_of(refs[:-2], other)
+
+    each_chunk(half, step)
 
 
 def split_total(*values):
@@ -462,36 +504,40 @@
     )(*values)
 
 
-def finish_kernel(scale, image, text, total, got, image_grad, text_grad):
+def finish_kernel(scale, image, text, kept, got, far, last, got_far, got_last, image_grad, text_grad):
     core = lax.axis_index("col") % 2
 
-    def backward(raw, unit_grad):
+    def backward(raw, parts):
         unit, inverse = normalize(raw[...])
-        unit_grad = scale[0] * unit_grad[...]
+        unit_grad = scale[0] * (parts[0][...] + parts[1][...].astype(F32) + parts[2][...].astype(F32))
         along = jnp.sum(unit * unit_grad, axis=1, keepdims=True)
         return inverse * (unit_grad - unit * along)
 
     @pl.when(core == 0)
     def _():
-        image_grad[...] = backward(image, total)
-        text_grad[...] = backward(text, got)
+        image_grad[...] = backward(image, (kept, far, last))
+        text_grad[...] = backward(text, (got, got_far, got_last))
 
     @pl.when(core == 1)
     def _():
-        image_grad[...] = backward(image, got)
-        text_grad[...] = backward(text, total)
-
-
-def finish(scale, image, text, total, got):
+        image_grad[...] = backward(image, (got, got_far, got_last))
+        text_grad[...] = backward(text, (kept, far, last))
+
+
+def finish(scale, image, text, kept, got, far, last):
+    rows, width = image.shape
     shape = jax.ShapeDtypeStruct(image.shape, F32)
+    block = pl.BlockSpec((rows // 2, width), lambda i: (i, 0))
+    other = pl.BlockSpec((rows // 2, width), lambda i: (2 + i, 0))
     return pl.pallas_call(
         finish_kernel,
+        grid=(2,),
         out_shape=(shape, shape),
-        in_specs=[SMEM] + [VMEM] * 4,
-        out_specs=(VMEM, VMEM),
+        in_specs=[SMEM] + [block] * 6 + [other] * 2,
+        out_specs=(block, block),
         compiler_params=BIG,
         name="finish",
-    )(scale, image, text, total, got)
+    )(scale, image, text, kept, got, far, last, send(far, CORES), send(last, CORES))
 
 
 def after(values, first):
@@ -507,29 +553,29 @@
     rows = 2 * image.shape[0]
     own0 = prepare(image, text, labels)
     mate0 = send(own0, MATES)
-    own = [own0] + [send(own0, ring(-d)) for d in STEPS[1:]]
-    own = after(own, mate0)
+    up, down, far = (send(own0, ring(-d)) for d in STEPS[1:])
+    own = [own0, up, down, mate0]
     own_other = [send(piece, CORES) for piece in own]
-    mate = [mate0] + [send(mate0, ring(-d)) for d in STEPS[1:3]] + [send(own[3], MATES)]
+    mate = [far] + [send(mate0, ring(-d)) for d in STEPS[1:3]] + [send(far, MATES)]
     before = own_sums(scale, own, own_other)
-    mate = after(mate, before)
+    mate = mate[:1] + after(mate[1:], before)
     mate_other = [send(piece, CORES) for piece in mate]
     keeps, aways = rest_sums(scale, own + mate, own_other + mate_other, before)
 
     gone = send(aways[0], CORES)
+    own_gone, last_gone = (send(away, CORES) for away in after(aways[1:], gone))
     mate_up, mate_down, far = join(keeps[0], gone, rows, (0, 1, 2))
     far = send(far, MATES)
     mate_up, mate_down = send(mate_up, ring(1)), send(mate_down, ring(-1))
-    gone = send(after(aways[1:2], gone)[0], CORES)
-    up, down = join(keeps[1], gone, rows, (0, 1))
+    up, down = join(keeps[1], own_gone, rows, (0, 1))
     up, down = send(up, ring(1)), send(down, ring(-1))
-    gone = send(after(aways[2:], gone)[0], CORES)
-    own_part, mate_part = join(keeps[2], gone, rows, (0, 2))
-    (far,) = join(keeps[2], gone, rows, (1,), (far,))
+    (far,) = join(keeps[2], last_gone, rows, (1,), (far,))
+    own_part, mate_part = join(keeps[2], last_gone, rows, (0, 2))
+    (mate_part,) = after((mate_part,), far)
     far = send(far, ring(2))
     mate_total = send(add(mate_part, mate_up, mate_down), MATES)
-    total, away = split_total(own_part, up, down, far, mate_total)
-    return finish(sharpness, image, text, total, send(away, CORES))
+    kept, away = split_total(own_part, up, down)
+    return finish(sharpness, image, text, kept, send(away, CORES), far, mate_total)
 
 
 def solution(mesh):

time: 142 us -> 130 us (0.915)
  waiting for transfers between devices: 43.2 us -> 25 us
  starting transfers between devices: 33.4 us -> 40.8 us
    ppermute x29 -> x31, waiting for transfers between devices: 43.2 us -> 25 us  [send(): return lax.ppermute(value, AXES, perm)]
    ppermute x29 -> x31, starting transfers between devices: 33.4 us -> 40.8 us  [send(): return lax.ppermute(value, AXES, perm)]
  transfers between devices with their start and end apart: 29 -> 31, of which waited for: 15 -> 10; matrix products, arithmetic and copies ran while one was open for 0% -> 0% of each run, Pallas kernels for 17% -> 21%
where the time goes in v3:
time: 130 us; the launch traced here: 129 us
  Pallas kernels  59.8 us (46%)
  starting transfers between devices  40.8 us (31%)
  waiting for transfers between devices  25 us (19%)
  between operations  2.1 us (2%)
  local copies, waits for them, and re-layouts  1.71 us (1%)
    ppermute x31, starting transfers between devices, send(): return lax.ppermute(value, AXES, perm)  40.8 us
    pallas_call x1, Pallas kernels, rest_sums(): pl.pallas_call(rest_kernel, out_shape=tuple(shapes * 2), in_specs=[SMEM]...  27.4 us
    ppermute x31, waiting for transfers between devices, send(): return lax.ppermute(value, AXES, perm)  25 us
    pallas_call x1, Pallas kernels, own_sums(): pl.pallas_call(own_kernel, out_shape=(jax.ShapeDtypeStruct((4 * rows, wid...  11.2 us
    pallas_call x4, Pallas kernels, join(): pl.pallas_call(lambda *refs: join_kernel(pieces, len(extra), *refs), out_...  9.74 us
    pallas_call x1, Pallas kernels, finish(): pl.pallas_call(finish_kernel, grid=(2,), out_shape=(shape, shape), in_spe...  3.25 us
    pallas_call x1, Pallas kernels, split_total(): pl.pallas_call(split_kernel, out_shape=(shape, shape), in_specs=[VMEM] *...  2.92 us
    pallas_call x1, Pallas kernels, add(): pl.pallas_call(add_kernel, out_shape=jax.ShapeDtypeStruct(values[0].shape...  2.78 us
  transfers between devices with their start and end apart: 31, of which 10 were waited for; matrix products, arithmetic and copies ran while one was open for 0% of the time, Pallas kernels for 21%

profile of v3, /device:TPU:1, one launch (start us, length us, event | category | flops | bytes accessed | tf_op | source)
XLA Modules:
  0.0 129.4 jit_solution(6180896654212091522)
XLA Ops:
  4.3 2.5 %prepare.1.refs_0_ = bf16[336,1152]{1,0:T(8,128)(2,1)} custom-call(bf16[160,1152]{1,0:T(8,128)(2,1)} %image.3, bf16[160,1152]{1,0:T(8,128)(2,1)} %text.3, bf16[160,1152]{1,0:T(8,128)(2,1)} %collective-permute-done.other_image, bf16[160,1152]{1,0:T(8,128)(2,1)} %collective-permute-done.1.other_text, s32[1,160]{1,0:T(1,128)} %bitcast.2, ...), custom_call_target="tpu_custom_call" | custom-call | tf_op jit(solution)/shard_map/prepare/pallas_call | solution.py:90
  6.8 3.8 %collective-permute-start.5 = (bf16[336,1152]{1,0:T(8,128)(2,1)}, bf16[336,1152]{1,0:T(8,128)(2,1)}, u32[]{:S(2)}, u32[]{:S(2)}) collective-permute-start(bf16[336,1152]{1,0:T(8,128)(2,1)} %prepare.1.refs_0_), channel_id=1, source_target_pairs={{0,16},{1,19},{16,0},{17,3},{2,18},{3,17},{18,2},{19,1},{32,48},{3... | collective-permute-start | bytes 2322440 | tf_op jit(solution)/shard_map/ppermute | solution.py:47
  15.3 5.1 %collective-permute-done.5.refs_3_ = bf16[336,1152]{1,0:T(8,128)(2,1)} collective-permute-done((bf16[336,1152]{1,0:T(8,128)(2,1)}, bf16[336,1152]{1,0:T(8,128)(2,1)}, u32[]{:S(2)}, u32[]{:S(2)}) %collective-permute-start.5) | collective-permute-done | bytes 774176 | tf_op jit(solution)/shard_map/ppermute | solution.py:47
  20.4 2.9 %collective-permute-done.4.refs_2_ = bf16[336,1152]{1,0:T(8,128)(2,1)S(1)} collective-permute-done((bf16[336,1152]{1,0:T(8,128)(2,1)}, bf16[336,1152]{1,0:T(8,128)(2,1)S(1)}, u32[]{:S(2)}, u32[]{:S(2)}) %collective-permute-start.4) | collective-permute-done | bytes 774176 | tf_op jit(solution)/shard_map/ppermute | solution.py:47
  24.2 6.3 %collective-permute-start.11 = (bf16[336,1152]{1,0:T(8,128)(2,1)S(1)}, bf16[336,1152]{1,0:T(8,128)(2,1)}, u32[]{:S(2)}, u32[]{:S(2)}) collective-permute-start(bf16[336,1152]{1,0:T(8,128)(2,1)S(1)} %collective-permute-done.3.refs_1_), channel_id=1, source_target_pairs={{0,1},{1,0},{16,17},{17,16},{2,3},{3,2},{18,19},{19,18},{32,33},{3... | collective-permute-start | bytes 2322440 | tf_op jit(solution)/shard_map/ppermute | solution.py:47
  37.7 11.2 %own_sums.1 = (f32[1280,1152]{1,0:T(8,128)}, f32[640,1152]{1,0:T(8,128)}) custom-call(f32[1]{0:T(128)S(6)} %copy.7.sharpness.scale, f32[1]{0:T(128)S(6)} %copy.8.shift, bf16[336,1152]{1,0:T(8,128)(2,1)} %prepare.1.refs_0_, bf16[336,1152]{1,0:T(8,128)(2,1)} %copy-done.1, bf16[336,1152]{1,0:T(8,128)(2,1)} %copy-done, ...), custom_call_target="tpu_custom_call" | custom-call | flops 5662310400 | bytes 7372800 | tf_op jit(solution)/shard_map/own_sums/pallas_call | solution.py:211
  49.6 2.0 %collective-permute-done.15.refs_13_ = bf16[336,1152]{1,0:T(8,128)(2,1)} collective-permute-done((bf16[336,1152]{1,0:T(8,128)(2,1)}, bf16[336,1152]{1,0:T(8,128)(2,1)}, u32[]{:S(2)}, u32[]{:S(2)}) %collective-permute-start.15) | collective-permute-done | bytes 774176 | tf_op jit(solution)/shard_map/ppermute | solution.py:47
  53.9 27.4 %rest_sums.1 = (bf16[960,1152]{1,0:T(8,128)(2,1)}, bf16[640,1152]{1,0:T(8,128)(2,1)}, bf16[960,1152]{1,0:T(8,128)(2,1)}, bf16[960,1152]{1,0:T(8,128)(2,1)}, bf16...) custom-call(f32[1]{0:T(128)S(6)} %copy.7.sharpness.scale, f32[1]{0:T(128)S(6)} %copy.8.shift, ...), custom_call_target="tpu_custom_call" | custom-call | flops 16986931200 | bytes 22118400 | tf_op jit(solution)/shard_map/rest_sums/pallas_call | solution.py:337
  81.5 4.6 %collective-permute-done.18.refs_1_ = bf16[960,1152]{1,0:T(8,128)(2,1)} collective-permute-done((bf16[960,1152]{1,0:T(8,128)(2,1)}, bf16[960,1152]{1,0:T(8,128)(2,1)}, u32[]{:S(2)}, u32[]{:S(2)}) %collective-permute-start.18) | collective-permute-done | bytes 2211872 | tf_op jit(solution)/shard_map/ppermute | solution.py:47
  86.6 2.6 %join.6 = (bf16[320,1152]{1,0:T(8,128)(2,1)}, bf16[320,1152]{1,0:T(8,128)(2,1)}, bf16[320,1152]{1,0:T(8,128)(2,1)}) custom-call(bf16[960,1152]{1,0:T(8,128)(2,1)} %get-tuple-element.42.refs_0_, bf16[960,1152]{1,0:T(8,128)(2,1)} %collective-permute-done.18.refs_1_), custom_call_target="tpu_custom_call" | custom-call | tf_op jit(solution)/shard_map/join/pallas_call | solution.py:433
  89.2 2.3 %collective-permute-start.24 = (bf16[320,1152]{1,0:T(8,128)(2,1)}, bf16[320,1152]{1,0:T(8,128)(2,1)}, u32[]{:S(2)}, u32[]{:S(2)}) collective-permute-start(bf16[320,1152]{1,0:T(8,128)(2,1)} %get-tuple-element.43), channel_id=1, source_target_pairs={{0,16},{1,19},{16,0},{17,3},{2,18},{3,17},{18,2},{19,1},{32,48},{3... | collective-permute-start | bytes 2211848 | tf_op jit(solution)/shard_map/ppermute | solution.py:47
  94.2 2.3 %join.5 = (bf16[320,1152]{1,0:T(8,128)(2,1)}, bf16[320,1152]{1,0:T(8,128)(2,1)}) custom-call(bf16[640,1152]{1,0:T(8,128)(2,1)} %get-tuple-element.36.refs_0_, bf16[640,1152]{1,0:T(8,128)(2,1)} %collective-permute-done.20.refs_1_), custom_call_target="tpu_custom_call" | custom-call | tf_op jit(solution)/shard_map/join/pallas_call | solution.py:433
  96.6 2.6 %collective-permute-start.22 = (bf16[320,1152]{1,0:T(8,128)(2,1)}, bf16[320,1152]{1,0:T(8,128)(2,1)}, u32[]{:S(2)}, u32[]{:S(2)}) collective-permute-start(bf16[320,1152]{1,0:T(8,128)(2,1)} %get-tuple-element.39), channel_id=1, source_target_pairs={{0,12},{1,97},{16,28},{17,113},{2,14},{3,99},{18,30},{19,115},{32,... | collective-permute-start | bytes 2211848 | tf_op jit(solution)/shard_map/ppermute | solution.py:47
  99.3 2.3 %join.4 = (bf16[320,1152]{1,0:T(8,128)(2,1)}, bf16[320,1152]{1,0:T(8,128)(2,1)}) custom-call(bf16[960,1152]{1,0:T(8,128)(2,1)} %get-tuple-element.30.refs_0_, bf16[960,1152]{1,0:T(8,128)(2,1)} %collective-permute-done.19.refs_1_), custom_call_target="tpu_custom_call" | custom-call | tf_op jit(solution)/shard_map/join/pallas_call | solution.py:433
  101.6 2.5 %join.7 = bf16[320,1152]{1,0:T(8,128)(2,1)} custom-call(bf16[960,1152]{1,0:T(8,128)(2,1)} %get-tuple-element.30.refs_0_, bf16[960,1152]{1,0:T(8,128)(2,1)} %collective-permute-done.19.refs_1_, bf16[320,1152]{1,0:T(8,128)(2,1)} %collective-permute-done.24.refs_2_), custom_call_target="tpu_custom_call" | custom-call | tf_op jit(solution)/shard_map/join/pallas_call | solution.py:433
  104.1 2.8 %add.1 = bf16[320,1152]{1,0:T(8,128)(2,1)} custom-call(bf16[320,1152]{1,0:T(8,128)(2,1)} %get-tuple-element.45.refs_0_, bf16[320,1152]{1,0:T(8,128)(2,1)} %collective-permute-done.26.refs_1_, bf16[320,1152]{1,0:T(8,128)(2,1)} %collective-permute-done.27.refs_2_), custom_call_target="tpu_custom_call" | custom-call | tf_op jit(solution)/shard_map/add/pallas_call | solution.py:474
  106.9 1.9 %collective-permute-start.28 = (bf16[320,1152]{1,0:T(8,128)(2,1)}, bf16[320,1152]{1,0:T(8,128)(2,1)}, u32[]{:S(2)}, u32[]{:S(2)}) collective-permute-start(bf16[320,1152]{1,0:T(8,128)(2,1)} %add.1), channel_id=1, source_target_pairs={{0,16},{1,19},{16,0},{17,3},{2,18},{3,17},{18,2},{19,1},{32,48},{3... | collective-permute-start | bytes 2211848 | tf_op jit(solution)/shard_map/ppermute | solution.py:47
  108.8 2.9 %collective-permute-start.25 = (bf16[320,1152]{1,0:T(8,128)(2,1)}, bf16[320,1152]{1,0:T(8,128)(2,1)}, u32[]{:S(2)}, u32[]{:S(2)}) collective-permute-start(bf16[320,1152]{1,0:T(8,128)(2,1)} %join.7), channel_id=1, source_target_pairs={{0,8},{1,65},{16,24},{17,81},{2,10},{3,67},{18,26},{19,83},{32,40}... | collective-permute-start | bytes 2211848 | tf_op jit(solution)/shard_map/ppermute | solution.py:47
  111.8 2.9 %split_total.1 = (f32[160,1152]{1,0:T(8,128)}, f32[160,1152]{1,0:T(8,128)}) custom-call(bf16[320,1152]{1,0:T(8,128)(2,1)} %get-tuple-element.35.refs_0_, bf16[320,1152]{1,0:T(8,128)(2,1)} %collective-permute-done.21.refs_1_, bf16[320,1152]{1,0:T(8,128)(2,1)} %collective-permute-done.22.refs_2_), custom_call_target="tpu_custom_call" | custom-call | tf_op jit(solution)/shard_map/split_total/pallas_call | solution.py:497
  115.4 3.6 %collective-permute-done.28.last = bf16[320,1152]{1,0:T(8,128)(2,1)} collective-permute-done((bf16[320,1152]{1,0:T(8,128)(2,1)}, bf16[320,1152]{1,0:T(8,128)(2,1)}, u32[]{:S(2)}, u32[]{:S(2)}) %collective-permute-start.28) | collective-permute-done | bytes 737312 | tf_op jit(solution)/shard_map/ppermute | solution.py:47
  119.0 2.4 %collective-permute-start.30 = (bf16[320,1152]{1,0:T(8,128)(2,1)}, bf16[320,1152]{1,0:T(8,128)(2,1)}, u32[]{:S(2)}, u32[]{:S(2)}) collective-permute-start(bf16[320,1152]{1,0:T(8,128)(2,1)} %collective-permute-done.28.last), channel_id=1, source_target_pairs={{0,1},{1,0},{16,17},{17,16},{2,3},{3,2},{18,19},{19,18},{32,33},{3... | collective-permute-start | bytes 2211848 | tf_op jit(solution)/shard_map/ppermute | solution.py:47
  121.4 2.5 %collective-permute-start.29 = (bf16[320,1152]{1,0:T(8,128)(2,1)}, bf16[320,1152]{1,0:T(8,128)(2,1)}, u32[]{:S(2)}, u32[]{:S(2)}) collective-permute-start(bf16[320,1152]{1,0:T(8,128)(2,1)} %collective-permute-done.25.far), channel_id=1, source_target_pairs={{0,1},{1,0},{16,17},{17,16},{2,3},{3,2},{18,19},{19,18},{32,33},{3... | collective-permute-start | bytes 2211848 | tf_op jit(solution)/shard_map/ppermute | solution.py:47
  123.9 2.2 %collective-permute-done.29.got_far = bf16[320,1152]{1,0:T(8,128)(2,1)} collective-permute-done((bf16[320,1152]{1,0:T(8,128)(2,1)}, bf16[320,1152]{1,0:T(8,128)(2,1)}, u32[]{:S(2)}, u32[]{:S(2)}) %collective-permute-start.29) | collective-permute-done | bytes 737312 | tf_op jit(solution)/shard_map/ppermute | solution.py:47
  126.1 3.3 %finish.1 = (f32[160,1152]{1,0:T(8,128)}, f32[160,1152]{1,0:T(8,128)}) custom-call(f32[1]{0:T(128)S(6)} %copy.7.sharpness.scale, bf16[160,1152]{1,0:T(8,128)(2,1)} %image.3, bf16[160,1152]{1,0:T(8,128)(2,1)} %text.3, f32[160,1152]{1,0:T(8,128)} %get-tuple-element.40.kept, f32[160,1152]{1,0:T(8,128)} %collective-permute-done.23.got, ...), custom_call_target="tpu_custom_call" | custom-call | tf_op jit(solution)/shard_map/finish/pallas_call | solution.py:532
  (54 shorter events, 22.4 us)
Async XLA Ops:
  6.8 13.6 %collective-permute-start.5 = (bf16[336,1152]{1,0:T(8,128)(2,1)}, bf16[336,1152]{1,0:T(8,128)(2,1)}, u32[]{:S(2)}, u32[]{:S(2)}) collective-permute-start(bf16[336,1152]{1,0:T(8,128)(2,1)} %prepare.1.refs_0_), channel_id=1, source_target_pairs={{0,16},{1,19},{16,0},{17,3},{2,18},{3,17},{18,2},{19,1},{32,48},{3... | collective-permute-start | bytes 2322440 | tf_op jit(solution)/shard_map/ppermute | solution.py:47
  10.6 12.6 %collective-permute-start.4 = (bf16[336,1152]{1,0:T(8,128)(2,1)}, bf16[336,1152]{1,0:T(8,128)(2,1)S(1)}, u32[]{:S(2)}, u32[]{:S(2)}) collective-permute-start(bf16[336,1152]{1,0:T(8,128)(2,1)} %prepare.1.refs_0_), channel_id=1, source_target_pairs={{0,4},{1,33},{16,20},{17,49},{2,6},{3,35},{18,22},{19,51},{32,36},... | collective-permute-start | bytes 2322440 | tf_op jit(solution)/shard_map/ppermute | solution.py:47
  11.9 12.2 %collective-permute-start.3 = (bf16[336,1152]{1,0:T(8,128)(2,1)}, bf16[336,1152]{1,0:T(8,128)(2,1)S(1)}, u32[]{:S(2)}, u32[]{:S(2)}) collective-permute-start(bf16[336,1152]{1,0:T(8,128)(2,1)} %prepare.1.refs_0_), channel_id=1, source_target_pairs={{0,12},{1,97},{16,28},{17,113},{2,14},{3,99},{18,30},{19,115},{32,... | collective-permute-start | bytes 2322440 | tf_op jit(solution)/shard_map/ppermute | solution.py:47
  13.4 17.1 %collective-permute-start.10 = (bf16[336,1152]{1,0:T(8,128)(2,1)}, bf16[336,1152]{1,0:T(8,128)(2,1)}, u32[]{:S(2)}, u32[]{:S(2)}) collective-permute-start(bf16[336,1152]{1,0:T(8,128)(2,1)} %prepare.1.refs_0_), channel_id=1, source_target_pairs={{0,1},{1,0},{16,17},{17,16},{2,3},{3,2},{18,19},{19,18},{32,33},{3... | collective-permute-start | bytes 2322440 | tf_op jit(solution)/shard_map/ppermute | solution.py:47
  13.4 19.0 %collective-permute-start.6 = (bf16[336,1152]{1,0:T(8,128)(2,1)}, bf16[336,1152]{1,0:T(8,128)(2,1)}, u32[]{:S(2)}, u32[]{:S(2)}) collective-permute-start(bf16[336,1152]{1,0:T(8,128)(2,1)} %prepare.1.refs_0_), channel_id=1, source_target_pairs={{0,8},{1,65},{16,24},{17,81},{2,10},{3,67},{18,26},{19,83},{32,40}... | collective-permute-start | bytes 2322440 | tf_op jit(solution)/shard_map/ppermute | solution.py:47
  20.4 13.6 %collective-permute-start.13 = (bf16[336,1152]{1,0:T(8,128)(2,1)}, bf16[336,1152]{1,0:T(8,128)(2,1)}, u32[]{:S(2)}, u32[]{:S(2)}) collective-permute-start(bf16[336,1152]{1,0:T(8,128)(2,1)} %collective-permute-done.5.refs_3_), channel_id=1, source_target_pairs={{0,1},{1,0},{16,17},{17,16},{2,3},{3,2},{18,19},{19,18},{32,33},{3... | collective-permute-start | bytes 2322440 | tf_op jit(solution)/shard_map/ppermute | solution.py:47
  24.2 12.6 %collective-permute-start.12 = (bf16[336,1152]{1,0:T(8,128)(2,1)S(1)}, bf16[336,1152]{1,0:T(8,128)(2,1)S(1)}, u32[]{:S(2)}, u32[]{:S(2)}) collective-permute-start(bf16[336,1152]{1,0:T(8,128)(2,1)S(1)} %collective-permute-done.4.refs_2_), channel_id=1, source_target_pairs={{0,1},{1,0},{16,17},{17,16},{2,3},{3,2},{18,19},{19,18},{32,33},{3... | collective-permute-start | bytes 2322440 | tf_op jit(solution)/shard_map/ppermute | solution.py:47
  24.2 13.6 %collective-permute-start.11 = (bf16[336,1152]{1,0:T(8,128)(2,1)S(1)}, bf16[336,1152]{1,0:T(8,128)(2,1)}, u32[]{:S(2)}, u32[]{:S(2)}) collective-permute-start(bf16[336,1152]{1,0:T(8,128)(2,1)S(1)} %collective-permute-done.3.refs_1_), channel_id=1, source_target_pairs={{0,1},{1,0},{16,17},{17,16},{2,3},{3,2},{18,19},{19,18},{32,33},{3... | collective-permute-start | bytes 2322440 | tf_op jit(solution)/shard_map/ppermute | solution.py:47
  30.4 18.5 %collective-permute-start.8 = (bf16[336,1152]{1,0:T(8,128)(2,1)}, bf16[336,1152]{1,0:T(8,128)(2,1)}, u32[]{:S(2)}, u32[]{:S(2)}) collective-permute-start(bf16[336,1152]{1,0:T(8,128)(2,1)} %collective-permute-done.5.refs_3_), channel_id=1, source_target_pairs={{0,4},{1,33},{16,20},{17,49},{2,6},{3,35},{18,22},{19,51},{32,36},... | collective-permute-start | bytes 2322440 | tf_op jit(solution)/shard_map/ppermute | solution.py:47
  32.4 16.5 %collective-permute-start.9 = (bf16[336,1152]{1,0:T(8,128)(2,1)}, bf16[336,1152]{1,0:T(8,128)(2,1)}, u32[]{:S(2)}, u32[]{:S(2)}) collective-permute-start(bf16[336,1152]{1,0:T(8,128)(2,1)} %collective-permute-done.6.refs_4_), channel_id=1, source_target_pairs={{0,16},{1,19},{16,0},{17,3},{2,18},{3,17},{18,2},{19,1},{32,48},{3... | collective-permute-start | bytes 2322440 | tf_op jit(solution)/shard_map/ppermute | solution.py:47
  34.0 15.0 %collective-permute-start.7 = (bf16[336,1152]{1,0:T(8,128)(2,1)}, bf16[336,1152]{1,0:T(8,128)(2,1)}, u32[]{:S(2)}, u32[]{:S(2)}) collective-permute-start(bf16[336,1152]{1,0:T(8,128)(2,1)} %collective-permute-done.5.refs_3_), channel_id=1, source_target_pairs={{0,12},{1,97},{16,28},{17,113},{2,14},{3,99},{18,30},{19,115},{32,... | collective-permute-start | bytes 2322440 | tf_op jit(solution)/shard_map/ppermute | solution.py:47
  36.8 12.8 %collective-permute-start.14 = (bf16[336,1152]{1,0:T(8,128)(2,1)}, bf16[336,1152]{1,0:T(8,128)(2,1)}, u32[]{:S(2)}, u32[]{:S(2)}) collective-permute-start(bf16[336,1152]{1,0:T(8,128)(2,1)} %collective-permute-done.6.refs_4_), channel_id=1, source_target_pairs={{0,1},{1,0},{16,17},{17,16},{2,3},{3,2},{18,19},{19,18},{32,33},{3... | collective-permute-start | bytes 2322440 | tf_op jit(solution)/shard_map/ppermute | solution.py:47
  81.3 4.7 %collective-permute-start.18 = (bf16[960,1152]{1,0:T(8,128)(2,1)}, bf16[960,1152]{1,0:T(8,128)(2,1)}, u32[]{:S(2)}, u32[]{:S(2)}) collective-permute-start(bf16[960,1152]{1,0:T(8,128)(2,1)} %get-tuple-element.33), channel_id=1, source_target_pairs={{0,1},{1,0},{16,17},{17,16},{2,3},{3,2},{18,19},{19,18},{32,33},{3... | collective-permute-start | bytes 6635528 | tf_op jit(solution)/shard_map/ppermute | solution.py:47
  86.1 10.6 %collective-permute-start.19 = (bf16[960,1152]{1,0:T(8,128)(2,1)}, bf16[960,1152]{1,0:T(8,128)(2,1)}, u32[]{:S(2)}, u32[]{:S(2)}) collective-permute-start(bf16[960,1152]{1,0:T(8,128)(2,1)} %get-tuple-element.34), channel_id=1, source_target_pairs={{0,1},{1,0},{16,17},{17,16},{2,3},{3,2},{18,19},{19,18},{32,33},{3... | collective-permute-start | bytes 6635528 | tf_op jit(solution)/shard_map/ppermute | solution.py:47
  86.2 8.0 %collective-permute-start.20 = (bf16[640,1152]{1,0:T(8,128)(2,1)}, bf16[640,1152]{1,0:T(8,128)(2,1)}, u32[]{:S(2)}, u32[]{:S(2)}) collective-permute-start(bf16[640,1152]{1,0:T(8,128)(2,1)} %get-tuple-element.37), channel_id=1, source_target_pairs={{0,1},{1,0},{16,17},{17,16},{2,3},{3,2},{18,19},{19,18},{32,33},{3... | collective-permute-start | bytes 4423688 | tf_op jit(solution)/shard_map/ppermute | solution.py:47
  89.2 12.4 %collective-permute-start.24 = (bf16[320,1152]{1,0:T(8,128)(2,1)}, bf16[320,1152]{1,0:T(8,128)(2,1)}, u32[]{:S(2)}, u32[]{:S(2)}) collective-permute-start(bf16[320,1152]{1,0:T(8,128)(2,1)} %get-tuple-element.43), channel_id=1, source_target_pairs={{0,16},{1,19},{16,0},{17,3},{2,18},{3,17},{18,2},{19,1},{32,48},{3... | collective-permute-start | bytes 2211848 | tf_op jit(solution)/shard_map/ppermute | solution.py:47
  91.4 12.7 %collective-permute-start.26 = (bf16[320,1152]{1,0:T(8,128)(2,1)}, bf16[320,1152]{1,0:T(8,128)(2,1)}, u32[]{:S(2)}, u32[]{:S(2)}) collective-permute-start(bf16[320,1152]{1,0:T(8,128)(2,1)} %get-tuple-element.46), channel_id=1, source_target_pairs={{0,4},{1,33},{16,20},{17,49},{2,6},{3,35},{18,22},{19,51},{32,36},... | collective-permute-start | bytes 2211848 | tf_op jit(solution)/shard_map/ppermute | solution.py:47
  92.7 11.4 %collective-permute-start.27 = (bf16[320,1152]{1,0:T(8,128)(2,1)}, bf16[320,1152]{1,0:T(8,128)(2,1)}, u32[]{:S(2)}, u32[]{:S(2)}) collective-permute-start(bf16[320,1152]{1,0:T(8,128)(2,1)} %get-tuple-element.47), channel_id=1, source_target_pairs={{0,12},{1,97},{16,28},{17,113},{2,14},{3,99},{18,30},{19,115},{32,... | collective-permute-start | bytes 2211848 | tf_op jit(solution)/shard_map/ppermute | solution.py:47
  96.5 15.2 %collective-permute-start.21 = (bf16[320,1152]{1,0:T(8,128)(2,1)}, bf16[320,1152]{1,0:T(8,128)(2,1)}, u32[]{:S(2)}, u32[]{:S(2)}) collective-permute-start(bf16[320,1152]{1,0:T(8,128)(2,1)} %get-tuple-element.38), channel_id=1, source_target_pairs={{0,4},{1,33},{16,20},{17,49},{2,6},{3,35},{18,22},{19,51},{32,36},... | collective-permute-start | bytes 2211848 | tf_op jit(solution)/shard_map/ppermute | solution.py:47
  96.6 15.1 %collective-permute-start.22 = (bf16[320,1152]{1,0:T(8,128)(2,1)}, bf16[320,1152]{1,0:T(8,128)(2,1)}, u32[]{:S(2)}, u32[]{:S(2)}) collective-permute-start(bf16[320,1152]{1,0:T(8,128)(2,1)} %get-tuple-element.39), channel_id=1, source_target_pairs={{0,12},{1,97},{16,28},{17,113},{2,14},{3,99},{18,30},{19,115},{32,... | collective-permute-start | bytes 2211848 | tf_op jit(solution)/shard_map/ppermute | solution.py:47
  106.9 12.1 %collective-permute-start.28 = (bf16[320,1152]{1,0:T(8,128)(2,1)}, bf16[320,1152]{1,0:T(8,128)(2,1)}, u32[]{:S(2)}, u32[]{:S(2)}) collective-permute-start(bf16[320,1152]{1,0:T(8,128)(2,1)} %add.1), channel_id=1, source_target_pairs={{0,16},{1,19},{16,0},{17,3},{2,18},{3,17},{18,2},{19,1},{32,48},{3... | collective-permute-start | bytes 2211848 | tf_op jit(solution)/shard_map/ppermute | solution.py:47
  108.8 12.6 %collective-permute-start.25 = (bf16[320,1152]{1,0:T(8,128)(2,1)}, bf16[320,1152]{1,0:T(8,128)(2,1)}, u32[]{:S(2)}, u32[]{:S(2)}) collective-permute-start(bf16[320,1152]{1,0:T(8,128)(2,1)} %join.7), channel_id=1, source_target_pairs={{0,8},{1,65},{16,24},{17,81},{2,10},{3,67},{18,26},{19,83},{32,40}... | collective-permute-start | bytes 2211848 | tf_op jit(solution)/shard_map/ppermute | solution.py:47
  114.7 9.2 %collective-permute-start.23 = (f32[160,1152]{1,0:T(8,128)}, f32[160,1152]{1,0:T(8,128)}, u32[]{:S(2)}, u32[]{:S(2)}) collective-permute-start(f32[160,1152]{1,0:T(8,128)} %get-tuple-element.41), channel_id=1, source_target_pairs={{0,1},{1,0},{16,17},{17,16},{2,3},{3,2},{18,19},{19,18},{32,33},{3... | collective-permute-start | bytes 2211848 | tf_op jit(solution)/shard_map/ppermute | solution.py:47
  119.0 4.9 %collective-permute-start.30 = (bf16[320,1152]{1,0:T(8,128)(2,1)}, bf16[320,1152]{1,0:T(8,128)(2,1)}, u32[]{:S(2)}, u32[]{:S(2)}) collective-permute-start(bf16[320,1152]{1,0:T(8,128)(2,1)} %collective-permute-done.28.last), channel_id=1, source_target_pairs={{0,1},{1,0},{16,17},{17,16},{2,3},{3,2},{18,19},{19,18},{32,33},{3... | collective-permute-start | bytes 2211848 | tf_op jit(solution)/shard_map/ppermute | solution.py:47
  (10 other events, 37.8 us)

commit v4 on v3

--- a/solution.py
+++ b/solution.py
@@ -228,7 +228,7 @@
     )(*scale, *mine, *other)
 
 
-LEAVING = (((1, 1, 3),), ((0, 1, 2),), ((0, 0, 1), (1, 0, 1), (0, 3, 1)))
+LEAVING = (((1, 1, 1), (1, 2, 2)), ((0, 1, 2),), ((0, 0, 1), (1, 0, 1), (0, 3, 1)))
 
 
 def rest_kernel(sharpness, shift, *refs):
@@ -249,14 +249,10 @@
     ]
     mate.each(core, False, "text")
     own.each(core, False, "image")
-    before[0].start()
-    own.each(core, False, "text")
-    mate.each(core, False, "image")
-    before[1].start()
     image_total[1] = jnp.zeros_like(image_total[1])
     text_total[1] = jnp.zeros_like(text_total[1])
 
-    def flush(wait, which):
+    def flush(wait, wanted):
         def act(image_to, text_to):
             sem = 0
             for g, spans in enumerate(LEAVING):
@@ -266,7 +262,7 @@
                         (0, image_out, image_to[g], rows),
                         (1, text_out, text_to[g], half),
                     ):
-                        if (kind, group) not in which:
+                        if not wanted(kind, group, first):
                             sem += 1
                             continue
                         copy = pltpu.make_async_copy(
@@ -294,6 +290,10 @@
         def _():
             mate.each(core, True, "text")
             own.each(core, True, "image")
+            before[0].start()
+            own.each(core, False, "text")
+            mate.each(core, False, "image")
+            before[1].start()
             own.set_labels()
 
         @pl.when(q == 1)
@@ -302,33 +302,45 @@
             mate.each(core, True, "image")
             mate.set_labels()
             before[1].wait()
-            image_out[0] = image_total[0].astype(BF16)
-            flush(False, ((0, 0),))
+
+        set_coefficient(scale, t == 1, texts.at[t], images.at[i], labels.at[i], coefficient)
+        text_sum = text_total[t] + along_text(coefficient, images.at[i])
+        text_total[t] = text_sum
+        text_out[t] = text_sum.astype(BF16)
+
+        @pl.when(q == 0)
+        def _():
+            before[0].wait()
+
+        @pl.when(q == 1)
+        def _():
+            flush(False, lambda kind, group, first: kind == 1 and group == 0)
 
         @pl.when(q == 2)
         def _():
-            text_out[0] = text_total[0].astype(BF16)
-            flush(False, ((1, 0),))
-
-        set_coefficient(scale, t == 1, texts.at[t], images.at[i], labels.at[i], coefficient)
-        text_total[t] += along_text(coefficient, images.at[i])
+            flush(False, lambda kind, group, first: kind == 1 and group == 1)
+
+        for h in range(2):
+            here = pl.ds(2 * h * rows, 2 * rows)
+            image_sum = image_total[i, here, :] + along_image(coefficient.at[:, here], texts.at[t])
+            image_total[i, here, :] = image_sum
+            image_out[i, here, :] = image_sum.astype(BF16)
+
+            if h == 0:
+
+                @pl.when(q == 2)
+                def _():
+                    flush(False, lambda kind, group, first: kind == 0 and group == 1 and first < 2)
 
         @pl.when(q == 0)
         def _():
-            before[0].wait()
-
-        @pl.when(q == 2)
-        def _():
-            text_out[1] = text_total[1].astype(BF16)
-            flush(False, ((1, 1),))
-
-        image_total[i] += along_image(coefficient, texts.at[t])
+            flush(False, lambda kind, group, first: kind == 0 and group == 0)
+
         return 0
 
     lax.fori_loop(0, 3, block, 0)
-    image_out[1] = image_total[1].astype(BF16)
-    flush(False, ((0, 1),))
-    flush(True, ((0, 0), (0, 1), (1, 0), (1, 1)))
+    flush(False, lambda kind, group, first: kind == 0 and group == 1 and first >= 2)
+    flush(True, lambda kind, group, first: True)
 
 
 def rest_sums(scale, mine, other, before):
@@ -351,7 +363,7 @@
             pltpu.VMEM((2, 2 * rows, width), BF16),
             pltpu.SemaphoreType.DMA((2, 12)),
             pltpu.SemaphoreType.DMA((2,)),
-            pltpu.SemaphoreType.DMA((10,)),
+            pltpu.SemaphoreType.DMA((12,)),
         ],
         compiler_params=BIG,
         cost_estimate=cost(3, rows, width),
@@ -397,16 +409,17 @@
                 here = pl.ds(pl.multiple_of(i * rows + c * CHUNK, CHUNK), CHUNK)
                 there = pl.ds(pl.multiple_of(i * rows + half + c * CHUNK, CHUNK), CHUNK)
                 if size == rows:
+                    if not last:
+                        sent[here, :] = kept[here, :] + came[here, :]
+                        return 0
                     total = kept[here, :].astype(F32) + came[here, :].astype(F32)
-                    if last:
-                        total = total + more[0, pl.ds(pl.multiple_of(c * CHUNK, CHUNK), CHUNK), :].astype(F32)
+                    total = total + more[0, pl.ds(pl.multiple_of(c * CHUNK, CHUNK), CHUNK), :].astype(F32)
                     sent[here, :] = total.astype(BF16)
                     return 0
                 for source, target, offset in ((kept, here, 0), (came, there, half)):
                     value = source[here, :]
                     if last:
-                        extra_rows = pl.ds(pl.multiple_of(offset + c * CHUNK, CHUNK), CHUNK)
-                        value = (value.astype(F32) + more[0, extra_rows, :].astype(F32)).astype(BF16)
+                        value = value + more[0, pl.ds(pl.multiple_of(offset + c * CHUNK, CHUNK), CHUNK), :]
                     sent[target, :] = value
                 return 0
 
@@ -471,11 +484,14 @@
 
 
 def add(*values):
+    rows, width = values[0].shape
+    block = pl.BlockSpec((rows // 2, width), lambda i: (i, 0))
     return pl.pallas_call(
         add_kernel,
-        out_shape=jax.ShapeDtypeStruct(values[0].shape, BF16),
-        in_specs=[VMEM] * len(values),
-        out_specs=VMEM,
+        grid=(2,),
+        out_shape=jax.ShapeDtypeStruct((rows, width), BF16),
+        in_specs=[block] * len(values),
+        out_specs=block,
         compiler_params=BIG,
         name="add",
     )(*values)

time: 130 us -> 128 us (0.985)
  Pallas kernels: 59.8 us -> 58 us
    pallas_call x1, Pallas kernels: 27.4 us -> 26 us  [rest_sums(): pl.pallas_call(rest_kernel, out_shape=tuple(shapes * 2), in_specs=[SMEM]...]
  transfers between devices with their start and end apart: 31 -> 31, of which waited for: 10 -> 12; matrix products, arithmetic and copies ran while one was open for 0% -> 0% of each run, Pallas kernels for 21% -> 21%
where the time goes in v4:
time: 128 us; the launch traced here: 127 us
  Pallas kernels  58 us (45%)
  starting transfers between devices  40.6 us (32%)
  waiting for transfers between devices  24.9 us (19%)
  between operations  2.1 us (2%)
  local copies, waits for them, and re-layouts  1.71 us (1%)
    ppermute x31, starting transfers between devices, send(): return lax.ppermute(value, AXES, perm)  40.6 us
    pallas_call x1, Pallas kernels, rest_sums(): pl.pallas_call(rest_kernel, out_shape=tuple(shapes * 2), in_specs=[SMEM]...  26 us
    ppermute x31, waiting for transfers between devices, send(): return lax.ppermute(value, AXES, perm)  24.9 us
    pallas_call x1, Pallas kernels, own_sums(): pl.pallas_call(own_kernel, out_shape=(jax.ShapeDtypeStruct((4 * rows, wid...  11.2 us
    pallas_call x4, Pallas kernels, join(): pl.pallas_call(lambda *refs: join_kernel(pieces, len(extra), *refs), out_...  9.67 us
    pallas_call x1, Pallas kernels, finish(): pl.pallas_call(finish_kernel, grid=(2,), out_shape=(shape, shape), in_spe...  3.25 us
    pallas_call x1, Pallas kernels, split_total(): pl.pallas_call(split_kernel, out_shape=(shape, shape), in_specs=[VMEM] *...  2.92 us
  transfers between devices with their start and end apart: 31, of which 12 were waited for; matrix products, arithmetic and copies ran while one was open for 0% of the time, Pallas kernels for 21%

profile of v4, /device:TPU:1, one launch (start us, length us, event | category | flops | bytes accessed | tf_op | source)
XLA Modules:
  0.0 127.3 jit_solution(5192587480896462522)
XLA Ops:
  4.3 2.5 %prepare.1.refs_0_ = bf16[336,1152]{1,0:T(8,128)(2,1)} custom-call(bf16[160,1152]{1,0:T(8,128)(2,1)} %image.3, bf16[160,1152]{1,0:T(8,128)(2,1)} %text.3, bf16[160,1152]{1,0:T(8,128)(2,1)} %collective-permute-done.other_image, bf16[160,1152]{1,0:T(8,128)(2,1)} %collective-permute-done.1.other_text, s32[1,160]{1,0:T(1,128)} %bitcast.2, ...), custom_call_target="tpu_custom_call" | custom-call | tf_op jit(solution)/shard_map/prepare/pallas_call | solution.py:90
  6.8 3.8 %collective-permute-start.5 = (bf16[336,1152]{1,0:T(8,128)(2,1)}, bf16[336,1152]{1,0:T(8,128)(2,1)}, u32[]{:S(2)}, u32[]{:S(2)}) collective-permute-start(bf16[336,1152]{1,0:T(8,128)(2,1)} %prepare.1.refs_0_), channel_id=1, source_target_pairs={{0,16},{1,19},{16,0},{17,3},{2,18},{3,17},{18,2},{19,1},{32,48},{3... | collective-permute-start | bytes 2322440 | tf_op jit(solution)/shard_map/ppermute | solution.py:47
  15.3 5.1 %collective-permute-done.5.refs_3_ = bf16[336,1152]{1,0:T(8,128)(2,1)} collective-permute-done((bf16[336,1152]{1,0:T(8,128)(2,1)}, bf16[336,1152]{1,0:T(8,128)(2,1)}, u32[]{:S(2)}, u32[]{:S(2)}) %collective-permute-start.5) | collective-permute-done | bytes 774176 | tf_op jit(solution)/shard_map/ppermute | solution.py:47
  20.4 2.9 %collective-permute-done.4.refs_2_ = bf16[336,1152]{1,0:T(8,128)(2,1)S(1)} collective-permute-done((bf16[336,1152]{1,0:T(8,128)(2,1)}, bf16[336,1152]{1,0:T(8,128)(2,1)S(1)}, u32[]{:S(2)}, u32[]{:S(2)}) %collective-permute-start.4) | collective-permute-done | bytes 774176 | tf_op jit(solution)/shard_map/ppermute | solution.py:47
  24.2 6.3 %collective-permute-start.11 = (bf16[336,1152]{1,0:T(8,128)(2,1)S(1)}, bf16[336,1152]{1,0:T(8,128)(2,1)}, u32[]{:S(2)}, u32[]{:S(2)}) collective-permute-start(bf16[336,1152]{1,0:T(8,128)(2,1)S(1)} %collective-permute-done.3.refs_1_), channel_id=1, source_target_pairs={{0,1},{1,0},{16,17},{17,16},{2,3},{3,2},{18,19},{19,18},{32,33},{3... | collective-permute-start | bytes 2322440 | tf_op jit(solution)/shard_map/ppermute | solution.py:47
  37.7 11.2 %own_sums.1 = (f32[1280,1152]{1,0:T(8,128)}, f32[640,1152]{1,0:T(8,128)}) custom-call(f32[1]{0:T(128)S(6)} %copy.7.sharpness.scale, f32[1]{0:T(128)S(6)} %copy.8.shift, bf16[336,1152]{1,0:T(8,128)(2,1)} %prepare.1.refs_0_, bf16[336,1152]{1,0:T(8,128)(2,1)} %copy-done.1, bf16[336,1152]{1,0:T(8,128)(2,1)} %copy-done, ...), custom_call_target="tpu_custom_call" | custom-call | flops 5662310400 | bytes 7372800 | tf_op jit(solution)/shard_map/own_sums/pallas_call | solution.py:211
  49.6 2.0 %collective-permute-done.15.refs_13_ = bf16[336,1152]{1,0:T(8,128)(2,1)} collective-permute-done((bf16[336,1152]{1,0:T(8,128)(2,1)}, bf16[336,1152]{1,0:T(8,128)(2,1)}, u32[]{:S(2)}, u32[]{:S(2)}) %collective-permute-start.15) | collective-permute-done | bytes 774176 | tf_op jit(solution)/shard_map/ppermute | solution.py:47
  53.9 26.0 %rest_sums.1 = (bf16[960,1152]{1,0:T(8,128)(2,1)}, bf16[640,1152]{1,0:T(8,128)(2,1)}, bf16[960,1152]{1,0:T(8,128)(2,1)}, bf16[960,1152]{1,0:T(8,128)(2,1)}, bf16...) custom-call(f32[1]{0:T(128)S(6)} %copy.7.sharpness.scale, f32[1]{0:T(128)S(6)} %copy.8.shift, ...), custom_call_target="tpu_custom_call" | custom-call | flops 16986931200 | bytes 22118400 | tf_op jit(solution)/shard_map/rest_sums/pallas_call | solution.py:349
  80.1 4.5 %collective-permute-done.18.refs_1_ = bf16[960,1152]{1,0:T(8,128)(2,1)} collective-permute-done((bf16[960,1152]{1,0:T(8,128)(2,1)}, bf16[960,1152]{1,0:T(8,128)(2,1)}, u32[]{:S(2)}, u32[]{:S(2)}) %collective-permute-start.18) | collective-permute-done | bytes 2211872 | tf_op jit(solution)/shard_map/ppermute | solution.py:47
  85.1 2.6 %join.6 = (bf16[320,1152]{1,0:T(8,128)(2,1)}, bf16[320,1152]{1,0:T(8,128)(2,1)}, bf16[320,1152]{1,0:T(8,128)(2,1)}) custom-call(bf16[960,1152]{1,0:T(8,128)(2,1)} %get-tuple-element.42.refs_0_, bf16[960,1152]{1,0:T(8,128)(2,1)} %collective-permute-done.18.refs_1_), custom_call_target="tpu_custom_call" | custom-call | tf_op jit(solution)/shard_map/join/pallas_call | solution.py:446
  87.8 2.3 %collective-permute-start.24 = (bf16[320,1152]{1,0:T(8,128)(2,1)}, bf16[320,1152]{1,0:T(8,128)(2,1)}, u32[]{:S(2)}, u32[]{:S(2)}) collective-permute-start(bf16[320,1152]{1,0:T(8,128)(2,1)} %get-tuple-element.43), channel_id=1, source_target_pairs={{0,16},{1,19},{16,0},{17,3},{2,18},{3,17},{18,2},{19,1},{32,48},{3... | collective-permute-start | bytes 2211848 | tf_op jit(solution)/shard_map/ppermute | solution.py:47
  92.7 2.3 %join.5 = (bf16[320,1152]{1,0:T(8,128)(2,1)}, bf16[320,1152]{1,0:T(8,128)(2,1)}) custom-call(bf16[640,1152]{1,0:T(8,128)(2,1)} %get-tuple-element.36.refs_0_, bf16[640,1152]{1,0:T(8,128)(2,1)} %collective-permute-done.20.refs_1_), custom_call_target="tpu_custom_call" | custom-call | tf_op jit(solution)/shard_map/join/pallas_call | solution.py:446
  95.2 2.6 %collective-permute-start.22 = (bf16[320,1152]{1,0:T(8,128)(2,1)}, bf16[320,1152]{1,0:T(8,128)(2,1)}, u32[]{:S(2)}, u32[]{:S(2)}) collective-permute-start(bf16[320,1152]{1,0:T(8,128)(2,1)} %get-tuple-element.39), channel_id=1, source_target_pairs={{0,12},{1,97},{16,28},{17,113},{2,14},{3,99},{18,30},{19,115},{32,... | collective-permute-start | bytes 2211848 | tf_op jit(solution)/shard_map/ppermute | solution.py:47
  97.8 2.3 %join.4 = (bf16[320,1152]{1,0:T(8,128)(2,1)}, bf16[320,1152]{1,0:T(8,128)(2,1)}) custom-call(bf16[960,1152]{1,0:T(8,128)(2,1)} %get-tuple-element.30.refs_0_, bf16[960,1152]{1,0:T(8,128)(2,1)} %collective-permute-done.19.refs_1_), custom_call_target="tpu_custom_call" | custom-call | tf_op jit(solution)/shard_map/join/pallas_call | solution.py:446
  100.2 2.4 %join.7 = bf16[320,1152]{1,0:T(8,128)(2,1)} custom-call(bf16[960,1152]{1,0:T(8,128)(2,1)} %get-tuple-element.30.refs_0_, bf16[960,1152]{1,0:T(8,128)(2,1)} %collective-permute-done.19.refs_1_, bf16[320,1152]{1,0:T(8,128)(2,1)} %collective-permute-done.24.refs_2_), custom_call_target="tpu_custom_call" | custom-call | tf_op jit(solution)/shard_map/join/pallas_call | solution.py:446
  102.6 2.5 %add.1 = bf16[320,1152]{1,0:T(8,128)(2,1)} custom-call(bf16[320,1152]{1,0:T(8,128)(2,1)} %get-tuple-element.45.refs_0_, bf16[320,1152]{1,0:T(8,128)(2,1)} %collective-permute-done.26.refs_1_, bf16[320,1152]{1,0:T(8,128)(2,1)} %collective-permute-done.27.refs_2_), custom_call_target="tpu_custom_call" | custom-call | tf_op jit(solution)/shard_map/add/pallas_call | solution.py:489
  105.1 2.0 %collective-permute-start.28 = (bf16[320,1152]{1,0:T(8,128)(2,1)}, bf16[320,1152]{1,0:T(8,128)(2,1)}, u32[]{:S(2)}, u32[]{:S(2)}) collective-permute-start(bf16[320,1152]{1,0:T(8,128)(2,1)} %add.1), channel_id=1, source_target_pairs={{0,16},{1,19},{16,0},{17,3},{2,18},{3,17},{18,2},{19,1},{32,48},{3... | collective-permute-start | bytes 2211848 | tf_op jit(solution)/shard_map/ppermute | solution.py:47
  107.0 2.9 %collective-permute-start.25 = (bf16[320,1152]{1,0:T(8,128)(2,1)}, bf16[320,1152]{1,0:T(8,128)(2,1)}, u32[]{:S(2)}, u32[]{:S(2)}) collective-permute-start(bf16[320,1152]{1,0:T(8,128)(2,1)} %join.7), channel_id=1, source_target_pairs={{0,8},{1,65},{16,24},{17,81},{2,10},{3,67},{18,26},{19,83},{32,40}... | collective-permute-start | bytes 2211848 | tf_op jit(solution)/shard_map/ppermute | solution.py:47
  110.1 2.9 %split_total.1 = (f32[160,1152]{1,0:T(8,128)}, f32[160,1152]{1,0:T(8,128)}) custom-call(bf16[320,1152]{1,0:T(8,128)(2,1)} %get-tuple-element.35.refs_0_, bf16[320,1152]{1,0:T(8,128)(2,1)} %collective-permute-done.21.refs_1_, bf16[320,1152]{1,0:T(8,128)(2,1)} %collective-permute-done.22.refs_2_), custom_call_target="tpu_custom_call" | custom-call | tf_op jit(solution)/shard_map/split_total/pallas_call | solution.py:513
  113.8 3.3 %collective-permute-done.28.last = bf16[320,1152]{1,0:T(8,128)(2,1)} collective-permute-done((bf16[320,1152]{1,0:T(8,128)(2,1)}, bf16[320,1152]{1,0:T(8,128)(2,1)}, u32[]{:S(2)}, u32[]{:S(2)}) %collective-permute-start.28) | collective-permute-done | bytes 737312 | tf_op jit(solution)/shard_map/ppermute | solution.py:47
  117.2 2.2 %collective-permute-start.30 = (bf16[320,1152]{1,0:T(8,128)(2,1)}, bf16[320,1152]{1,0:T(8,128)(2,1)}, u32[]{:S(2)}, u32[]{:S(2)}) collective-permute-start(bf16[320,1152]{1,0:T(8,128)(2,1)} %collective-permute-done.28.last), channel_id=1, source_target_pairs={{0,1},{1,0},{16,17},{17,16},{2,3},{3,2},{18,19},{19,18},{32,33},{3... | collective-permute-start | bytes 2211848 | tf_op jit(solution)/shard_map/ppermute | solution.py:47
  119.4 2.4 %collective-permute-start.29 = (bf16[320,1152]{1,0:T(8,128)(2,1)}, bf16[320,1152]{1,0:T(8,128)(2,1)}, u32[]{:S(2)}, u32[]{:S(2)}) collective-permute-start(bf16[320,1152]{1,0:T(8,128)(2,1)} %collective-permute-done.25.far), channel_id=1, source_target_pairs={{0,1},{1,0},{16,17},{17,16},{2,3},{3,2},{18,19},{19,18},{32,33},{3... | collective-permute-start | bytes 2211848 | tf_op jit(solution)/shard_map/ppermute | solution.py:47
  121.9 2.2 %collective-permute-done.29.got_far = bf16[320,1152]{1,0:T(8,128)(2,1)} collective-permute-done((bf16[320,1152]{1,0:T(8,128)(2,1)}, bf16[320,1152]{1,0:T(8,128)(2,1)}, u32[]{:S(2)}, u32[]{:S(2)}) %collective-permute-start.29) | collective-permute-done | bytes 737312 | tf_op jit(solution)/shard_map/ppermute | solution.py:47
  124.0 3.3 %finish.1 = (f32[160,1152]{1,0:T(8,128)}, f32[160,1152]{1,0:T(8,128)}) custom-call(f32[1]{0:T(128)S(6)} %copy.7.sharpness.scale, bf16[160,1152]{1,0:T(8,128)(2,1)} %image.3, bf16[160,1152]{1,0:T(8,128)(2,1)} %text.3, f32[160,1152]{1,0:T(8,128)} %get-tuple-element.40.kept, f32[160,1152]{1,0:T(8,128)} %collective-permute-done.23.got, ...), custom_call_target="tpu_custom_call" | custom-call | tf_op jit(solution)/shard_map/finish/pallas_call | solution.py:548
  (54 shorter events, 22.8 us)
Async XLA Ops:
  6.8 13.6 %collective-permute-start.5 = (bf16[336,1152]{1,0:T(8,128)(2,1)}, bf16[336,1152]{1,0:T(8,128)(2,1)}, u32[]{:S(2)}, u32[]{:S(2)}) collective-permute-start(bf16[336,1152]{1,0:T(8,128)(2,1)} %prepare.1.refs_0_), channel_id=1, source_target_pairs={{0,16},{1,19},{16,0},{17,3},{2,18},{3,17},{18,2},{19,1},{32,48},{3... | collective-permute-start | bytes 2322440 | tf_op jit(solution)/shard_map/ppermute | solution.py:47
  10.6 12.6 %collective-permute-start.4 = (bf16[336,1152]{1,0:T(8,128)(2,1)}, bf16[336,1152]{1,0:T(8,128)(2,1)S(1)}, u32[]{:S(2)}, u32[]{:S(2)}) collective-permute-start(bf16[336,1152]{1,0:T(8,128)(2,1)} %prepare.1.refs_0_), channel_id=1, source_target_pairs={{0,4},{1,33},{16,20},{17,49},{2,6},{3,35},{18,22},{19,51},{32,36},... | collective-permute-start | bytes 2322440 | tf_op jit(solution)/shard_map/ppermute | solution.py:47
  11.9 12.2 %collective-permute-start.3 = (bf16[336,1152]{1,0:T(8,128)(2,1)}, bf16[336,1152]{1,0:T(8,128)(2,1)S(1)}, u32[]{:S(2)}, u32[]{:S(2)}) collective-permute-start(bf16[336,1152]{1,0:T(8,128)(2,1)} %prepare.1.refs_0_), channel_id=1, source_target_pairs={{0,12},{1,97},{16,28},{17,113},{2,14},{3,99},{18,30},{19,115},{32,... | collective-permute-start | bytes 2322440 | tf_op jit(solution)/shard_map/ppermute | solution.py:47
  13.4 17.1 %collective-permute-start.10 = (bf16[336,1152]{1,0:T(8,128)(2,1)}, bf16[336,1152]{1,0:T(8,128)(2,1)}, u32[]{:S(2)}, u32[]{:S(2)}) collective-permute-start(bf16[336,1152]{1,0:T(8,128)(2,1)} %prepare.1.refs_0_), channel_id=1, source_target_pairs={{0,1},{1,0},{16,17},{17,16},{2,3},{3,2},{18,19},{19,18},{32,33},{3... | collective-permute-start | bytes 2322440 | tf_op jit(solution)/shard_map/ppermute | solution.py:47
  13.4 19.0 %collective-permute-start.6 = (bf16[336,1152]{1,0:T(8,128)(2,1)}, bf16[336,1152]{1,0:T(8,128)(2,1)}, u32[]{:S(2)}, u32[]{:S(2)}) collective-permute-start(bf16[336,1152]{1,0:T(8,128)(2,1)} %prepare.1.refs_0_), channel_id=1, source_target_pairs={{0,8},{1,65},{16,24},{17,81},{2,10},{3,67},{18,26},{19,83},{32,40}... | collective-permute-start | bytes 2322440 | tf_op jit(solution)/shard_map/ppermute | solution.py:47
  20.4 13.6 %collective-permute-start.13 = (bf16[336,1152]{1,0:T(8,128)(2,1)}, bf16[336,1152]{1,0:T(8,128)(2,1)}, u32[]{:S(2)}, u32[]{:S(2)}) collective-permute-start(bf16[336,1152]{1,0:T(8,128)(2,1)} %collective-permute-done.5.refs_3_), channel_id=1, source_target_pairs={{0,1},{1,0},{16,17},{17,16},{2,3},{3,2},{18,19},{19,18},{32,33},{3... | collective-permute-start | bytes 2322440 | tf_op jit(solution)/shard_map/ppermute | solution.py:47
  24.2 12.6 %collective-permute-start.12 = (bf16[336,1152]{1,0:T(8,128)(2,1)S(1)}, bf16[336,1152]{1,0:T(8,128)(2,1)S(1)}, u32[]{:S(2)}, u32[]{:S(2)}) collective-permute-start(bf16[336,1152]{1,0:T(8,128)(2,1)S(1)} %collective-permute-done.4.refs_2_), channel_id=1, source_target_pairs={{0,1},{1,0},{16,17},{17,16},{2,3},{3,2},{18,19},{19,18},{32,33},{3... | collective-permute-start | bytes 2322440 | tf_op jit(solution)/shard_map/ppermute | solution.py:47
  24.2 13.6 %collective-permute-start.11 = (bf16[336,1152]{1,0:T(8,128)(2,1)S(1)}, bf16[336,1152]{1,0:T(8,128)(2,1)}, u32[]{:S(2)}, u32[]{:S(2)}) collective-permute-start(bf16[336,1152]{1,0:T(8,128)(2,1)S(1)} %collective-permute-done.3.refs_1_), channel_id=1, source_target_pairs={{0,1},{1,0},{16,17},{17,16},{2,3},{3,2},{18,19},{19,18},{32,33},{3... | collective-permute-start | bytes 2322440 | tf_op jit(solution)/shard_map/ppermute | solution.py:47
  30.4 18.5 %collective-permute-start.8 = (bf16[336,1152]{1,0:T(8,128)(2,1)}, bf16[336,1152]{1,0:T(8,128)(2,1)}, u32[]{:S(2)}, u32[]{:S(2)}) collective-permute-start(bf16[336,1152]{1,0:T(8,128)(2,1)} %collective-permute-done.5.refs_3_), channel_id=1, source_target_pairs={{0,4},{1,33},{16,20},{17,49},{2,6},{3,35},{18,22},{19,51},{32,36},... | collective-permute-start | bytes 2322440 | tf_op jit(solution)/shard_map/ppermute | solution.py:47
  32.4 16.5 %collective-permute-start.9 = (bf16[336,1152]{1,0:T(8,128)(2,1)}, bf16[336,1152]{1,0:T(8,128)(2,1)}, u32[]{:S(2)}, u32[]{:S(2)}) collective-permute-start(bf16[336,1152]{1,0:T(8,128)(2,1)} %collective-permute-done.6.refs_4_), channel_id=1, source_target_pairs={{0,16},{1,19},{16,0},{17,3},{2,18},{3,17},{18,2},{19,1},{32,48},{3... | collective-permute-start | bytes 2322440 | tf_op jit(solution)/shard_map/ppermute | solution.py:47
  34.0 15.0 %collective-permute-start.7 = (bf16[336,1152]{1,0:T(8,128)(2,1)}, bf16[336,1152]{1,0:T(8,128)(2,1)}, u32[]{:S(2)}, u32[]{:S(2)}) collective-permute-start(bf16[336,1152]{1,0:T(8,128)(2,1)} %collective-permute-done.5.refs_3_), channel_id=1, source_target_pairs={{0,12},{1,97},{16,28},{17,113},{2,14},{3,99},{18,30},{19,115},{32,... | collective-permute-start | bytes 2322440 | tf_op jit(solution)/shard_map/ppermute | solution.py:47
  36.8 12.8 %collective-permute-start.14 = (bf16[336,1152]{1,0:T(8,128)(2,1)}, bf16[336,1152]{1,0:T(8,128)(2,1)}, u32[]{:S(2)}, u32[]{:S(2)}) collective-permute-start(bf16[336,1152]{1,0:T(8,128)(2,1)} %collective-permute-done.6.refs_4_), channel_id=1, source_target_pairs={{0,1},{1,0},{16,17},{17,16},{2,3},{3,2},{18,19},{19,18},{32,33},{3... | collective-permute-start | bytes 2322440 | tf_op jit(solution)/shard_map/ppermute | solution.py:47
  79.9 4.7 %collective-permute-start.18 = (bf16[960,1152]{1,0:T(8,128)(2,1)}, bf16[960,1152]{1,0:T(8,128)(2,1)}, u32[]{:S(2)}, u32[]{:S(2)}) collective-permute-start(bf16[960,1152]{1,0:T(8,128)(2,1)} %get-tuple-element.33), channel_id=1, source_target_pairs={{0,1},{1,0},{16,17},{17,16},{2,3},{3,2},{18,19},{19,18},{32,33},{3... | collective-permute-start | bytes 6635528 | tf_op jit(solution)/shard_map/ppermute | solution.py:47
  84.6 10.6 %collective-permute-start.19 = (bf16[960,1152]{1,0:T(8,128)(2,1)}, bf16[960,1152]{1,0:T(8,128)(2,1)}, u32[]{:S(2)}, u32[]{:S(2)}) collective-permute-start(bf16[960,1152]{1,0:T(8,128)(2,1)} %get-tuple-element.34), channel_id=1, source_target_pairs={{0,1},{1,0},{16,17},{17,16},{2,3},{3,2},{18,19},{19,18},{32,33},{3... | collective-permute-start | bytes 6635528 | tf_op jit(solution)/shard_map/ppermute | solution.py:47
  84.8 8.0 %collective-permute-start.20 = (bf16[640,1152]{1,0:T(8,128)(2,1)}, bf16[640,1152]{1,0:T(8,128)(2,1)}, u32[]{:S(2)}, u32[]{:S(2)}) collective-permute-start(bf16[640,1152]{1,0:T(8,128)(2,1)} %get-tuple-element.37), channel_id=1, source_target_pairs={{0,1},{1,0},{16,17},{17,16},{2,3},{3,2},{18,19},{19,18},{32,33},{3... | collective-permute-start | bytes 4423688 | tf_op jit(solution)/shard_map/ppermute | solution.py:47
  87.8 12.4 %collective-permute-start.24 = (bf16[320,1152]{1,0:T(8,128)(2,1)}, bf16[320,1152]{1,0:T(8,128)(2,1)}, u32[]{:S(2)}, u32[]{:S(2)}) collective-permute-start(bf16[320,1152]{1,0:T(8,128)(2,1)} %get-tuple-element.43), channel_id=1, source_target_pairs={{0,16},{1,19},{16,0},{17,3},{2,18},{3,17},{18,2},{19,1},{32,48},{3... | collective-permute-start | bytes 2211848 | tf_op jit(solution)/shard_map/ppermute | solution.py:47
  90.0 12.6 %collective-permute-start.26 = (bf16[320,1152]{1,0:T(8,128)(2,1)}, bf16[320,1152]{1,0:T(8,128)(2,1)}, u32[]{:S(2)}, u32[]{:S(2)}) collective-permute-start(bf16[320,1152]{1,0:T(8,128)(2,1)} %get-tuple-element.46), channel_id=1, source_target_pairs={{0,4},{1,33},{16,20},{17,49},{2,6},{3,35},{18,22},{19,51},{32,36},... | collective-permute-start | bytes 2211848 | tf_op jit(solution)/shard_map/ppermute | solution.py:47
  91.3 11.3 %collective-permute-start.27 = (bf16[320,1152]{1,0:T(8,128)(2,1)}, bf16[320,1152]{1,0:T(8,128)(2,1)}, u32[]{:S(2)}, u32[]{:S(2)}) collective-permute-start(bf16[320,1152]{1,0:T(8,128)(2,1)} %get-tuple-element.47), channel_id=1, source_target_pairs={{0,12},{1,97},{16,28},{17,113},{2,14},{3,99},{18,30},{19,115},{32,... | collective-permute-start | bytes 2211848 | tf_op jit(solution)/shard_map/ppermute | solution.py:47
  95.1 15.0 %collective-permute-start.21 = (bf16[320,1152]{1,0:T(8,128)(2,1)}, bf16[320,1152]{1,0:T(8,128)(2,1)}, u32[]{:S(2)}, u32[]{:S(2)}) collective-permute-start(bf16[320,1152]{1,0:T(8,128)(2,1)} %get-tuple-element.38), channel_id=1, source_target_pairs={{0,4},{1,33},{16,20},{17,49},{2,6},{3,35},{18,22},{19,51},{32,36},... | collective-permute-start | bytes 2211848 | tf_op jit(solution)/shard_map/ppermute | solution.py:47
  95.2 14.9 %collective-permute-start.22 = (bf16[320,1152]{1,0:T(8,128)(2,1)}, bf16[320,1152]{1,0:T(8,128)(2,1)}, u32[]{:S(2)}, u32[]{:S(2)}) collective-permute-start(bf16[320,1152]{1,0:T(8,128)(2,1)} %get-tuple-element.39), channel_id=1, source_target_pairs={{0,12},{1,97},{16,28},{17,113},{2,14},{3,99},{18,30},{19,115},{32,... | collective-permute-start | bytes 2211848 | tf_op jit(solution)/shard_map/ppermute | solution.py:47
  105.1 12.1 %collective-permute-start.28 = (bf16[320,1152]{1,0:T(8,128)(2,1)}, bf16[320,1152]{1,0:T(8,128)(2,1)}, u32[]{:S(2)}, u32[]{:S(2)}) collective-permute-start(bf16[320,1152]{1,0:T(8,128)(2,1)} %add.1), channel_id=1, source_target_pairs={{0,16},{1,19},{16,0},{17,3},{2,18},{3,17},{18,2},{19,1},{32,48},{3... | collective-permute-start | bytes 2211848 | tf_op jit(solution)/shard_map/ppermute | solution.py:47
  107.0 12.4 %collective-permute-start.25 = (bf16[320,1152]{1,0:T(8,128)(2,1)}, bf16[320,1152]{1,0:T(8,128)(2,1)}, u32[]{:S(2)}, u32[]{:S(2)}) collective-permute-start(bf16[320,1152]{1,0:T(8,128)(2,1)} %join.7), channel_id=1, source_target_pairs={{0,8},{1,65},{16,24},{17,81},{2,10},{3,67},{18,26},{19,83},{32,40}... | collective-permute-start | bytes 2211848 | tf_op jit(solution)/shard_map/ppermute | solution.py:47
  113.0 8.8 %collective-permute-start.23 = (f32[160,1152]{1,0:T(8,128)}, f32[160,1152]{1,0:T(8,128)}, u32[]{:S(2)}, u32[]{:S(2)}) collective-permute-start(f32[160,1152]{1,0:T(8,128)} %get-tuple-element.41), channel_id=1, source_target_pairs={{0,1},{1,0},{16,17},{17,16},{2,3},{3,2},{18,19},{19,18},{32,33},{3... | collective-permute-start | bytes 2211848 | tf_op jit(solution)/shard_map/ppermute | solution.py:47
  117.2 4.7 %collective-permute-start.30 = (bf16[320,1152]{1,0:T(8,128)(2,1)}, bf16[320,1152]{1,0:T(8,128)(2,1)}, u32[]{:S(2)}, u32[]{:S(2)}) collective-permute-start(bf16[320,1152]{1,0:T(8,128)(2,1)} %collective-permute-done.28.last), channel_id=1, source_target_pairs={{0,1},{1,0},{16,17},{17,16},{2,3},{3,2},{18,19},{19,18},{32,33},{3... | collective-permute-start | bytes 2211848 | tf_op jit(solution)/shard_map/ppermute | solution.py:47
  (10 other events, 37.7 us)

commit v5 on v4

--- a/solution.py
+++ b/solution.py
@@ -63,8 +63,11 @@
     rows = image.shape[0]
 
     def fill(mine, other):
-        own[:rows, :] = normalize(mine[...])[0].astype(BF16)
-        own[rows : 2 * rows, :] = normalize(other[...])[0].astype(BF16)
+        def step(part, c):
+            own[part, :] = normalize(mine[part, :])[0].astype(BF16)
+            own[pl.ds(pl.multiple_of(rows + c * CHUNK, CHUNK), CHUNK), :] = normalize(other[part, :])[0].astype(BF16)
+
+        each_chunk(rows, step)
 
     @pl.when(core == 0)
     def _():
@@ -461,12 +464,12 @@
     )(keep, got, *extra)
 
 
-def each_chunk(rows, step):
+def each_chunk(rows, step, size=CHUNK):
     def run(c, _):
-        step(pl.ds(pl.multiple_of(c * CHUNK, CHUNK), CHUNK), c)
+        step(pl.ds(pl.multiple_of(c * size, size), size), c)
         return 0
 
-    lax.fori_loop(0, rows // CHUNK, run, 0)
+    lax.fori_loop(0, rows // size, run, 0)
 
 
 def total_of(refs, part):
@@ -523,21 +526,25 @@
 def finish_kernel(scale, image, text, kept, got, far, last, got_far, got_last, image_grad, text_grad):
     core = lax.axis_index("col") % 2
 
-    def backward(raw, parts):
-        unit, inverse = normalize(raw[...])
-        unit_grad = scale[0] * (parts[0][...] + parts[1][...].astype(F32) + parts[2][...].astype(F32))
-        along = jnp.sum(unit * unit_grad, axis=1, keepdims=True)
-        return inverse * (unit_grad - unit * along)
+    def backward(raw, parts, out):
+        def step(part, c):
+            unit, inverse = normalize(raw[part, :])
+            total = parts[0][part, :] + parts[1][part, :].astype(F32) + parts[2][part, :].astype(F32)
+            unit_grad = scale[0] * total
+            along = jnp.sum(unit * unit_grad, axis=1, keepdims=True)
+            out[part, :] = inverse * (unit_grad - unit * along)
+
+        each_chunk(out.shape[0], step, 16)
 
     @pl.when(core == 0)
     def _():
-        image_grad[...] = backward(image, (kept, far, last))
-        text_grad[...] = backward(text, (got, got_far, got_last))
+        backward(image, (kept, far, last), image_grad)
+        backward(text, (got, got_far, got_last), text_grad)
 
     @pl.when(core == 1)
     def _():
-        image_grad[...] = backward(image, (got, got_far, got_last))
-        text_grad[...] = backward(text, (kept, far, last))
+        backward(image, (got, got_far, got_last), image_grad)
+        backward(text, (kept, far, last), text_grad)
 
 
 def finish(scale, image, text, kept, got, far, last):

time: 128 us -> 131 us (1.023)
  Pallas kernels: 58 us -> 61.3 us
    pallas_call x1, Pallas kernels: 3.25 us -> 6.21 us  [finish(): pl.pallas_call(finish_kernel, grid=(2,), out_shape=(shape, shape), in_spe...]
  transfers between devices with their start and end apart: 31 -> 31, of which waited for: 12 -> 12; matrix products, arithmetic and copies ran while one was open for 0% -> 0% of each run, Pallas kernels for 21% -> 20%
where the time goes in v5:
time: 131 us
  Pallas kernels  61.3 us (47%)
  starting transfers between devices  40.6 us (31%)
  waiting for transfers between devices  24.9 us (19%)
  between operations  2.1 us (2%)
  local copies, waits for them, and re-layouts  1.71 us (1%)
    ppermute x31, starting transfers between devices, send(): return lax.ppermute(value, AXES, perm)  40.6 us
    pallas_call x1, Pallas kernels, rest_sums(): pl.pallas_call(rest_kernel, out_shape=tuple(shapes * 2), in_specs=[SMEM]...  26 us
    ppermute x31, waiting for transfers between devices, send(): return lax.ppermute(value, AXES, perm)  24.9 us
    pallas_call x1, Pallas kernels, own_sums(): pl.pallas_call(own_kernel, out_shape=(jax.ShapeDtypeStruct((4 * rows, wid...  11.2 us
    pallas_call x4, Pallas kernels, join(): pl.pallas_call(lambda *refs: join_kernel(pieces, len(extra), *refs), out_...  9.67 us
    pallas_call x1, Pallas kernels, finish(): pl.pallas_call(finish_kernel, grid=(2,), out_shape=(shape, shape), in_spe...  6.21 us
    pallas_call x1, Pallas kernels, split_total(): pl.pallas_call(split_kernel, out_shape=(shape, shape), in_specs=[VMEM] *...  2.92 us
    pallas_call x1, Pallas kernels, prepare(): pl.pallas_call(prepare_kernel, out_shape=jax.ShapeDtypeStruct((2 * rows +...  2.83 us
  transfers between devices with their start and end apart: 31, of which 12 were waited for; matrix products, arithmetic and copies ran while one was open for 0% of the time, Pallas kernels for 20%

profile of v5, /device:TPU:1, one launch (start us, length us, event | category | flops | bytes accessed | tf_op | source)
XLA Modules:
  0.0 130.6 jit_solution(2710968023909632494)
XLA Ops:
  4.3 2.8 %prepare.1.refs_0_ = bf16[336,1152]{1,0:T(8,128)(2,1)} custom-call(bf16[160,1152]{1,0:T(8,128)(2,1)} %image.3, bf16[160,1152]{1,0:T(8,128)(2,1)} %text.3, bf16[160,1152]{1,0:T(8,128)(2,1)} %collective-permute-done.other_image, bf16[160,1152]{1,0:T(8,128)(2,1)} %collective-permute-done.1.other_text, s32[1,160]{1,0:T(1,128)} %bitcast.2, ...), custom_call_target="tpu_custom_call" | custom-call | tf_op jit(solution)/shard_map/prepare/pallas_call | solution.py:93
  7.2 3.8 %collective-permute-start.5 = (bf16[336,1152]{1,0:T(8,128)(2,1)}, bf16[336,1152]{1,0:T(8,128)(2,1)}, u32[]{:S(2)}, u32[]{:S(2)}) collective-permute-start(bf16[336,1152]{1,0:T(8,128)(2,1)} %prepare.1.refs_0_), channel_id=1, source_target_pairs={{0,16},{1,19},{16,0},{17,3},{2,18},{3,17},{18,2},{19,1},{32,48},{3... | collective-permute-start | bytes 2322440 | tf_op jit(solution)/shard_map/ppermute | solution.py:47
  15.7 5.1 %collective-permute-done.5.refs_3_ = bf16[336,1152]{1,0:T(8,128)(2,1)} collective-permute-done((bf16[336,1152]{1,0:T(8,128)(2,1)}, bf16[336,1152]{1,0:T(8,128)(2,1)}, u32[]{:S(2)}, u32[]{:S(2)}) %collective-permute-start.5) | collective-permute-done | bytes 774176 | tf_op jit(solution)/shard_map/ppermute | solution.py:47
  20.7 2.9 %collective-permute-done.4.refs_2_ = bf16[336,1152]{1,0:T(8,128)(2,1)S(1)} collective-permute-done((bf16[336,1152]{1,0:T(8,128)(2,1)}, bf16[336,1152]{1,0:T(8,128)(2,1)S(1)}, u32[]{:S(2)}, u32[]{:S(2)}) %collective-permute-start.4) | collective-permute-done | bytes 774176 | tf_op jit(solution)/shard_map/ppermute | solution.py:47
  24.5 6.3 %collective-permute-start.11 = (bf16[336,1152]{1,0:T(8,128)(2,1)S(1)}, bf16[336,1152]{1,0:T(8,128)(2,1)}, u32[]{:S(2)}, u32[]{:S(2)}) collective-permute-start(bf16[336,1152]{1,0:T(8,128)(2,1)S(1)} %collective-permute-done.3.refs_1_), channel_id=1, source_target_pairs={{0,1},{1,0},{16,17},{17,16},{2,3},{3,2},{18,19},{19,18},{32,33},{3... | collective-permute-start | bytes 2322440 | tf_op jit(solution)/shard_map/ppermute | solution.py:47
  38.1 11.2 %own_sums.1 = (f32[1280,1152]{1,0:T(8,128)}, f32[640,1152]{1,0:T(8,128)}) custom-call(f32[1]{0:T(128)S(6)} %copy.7.sharpness.scale, f32[1]{0:T(128)S(6)} %copy.8.shift, bf16[336,1152]{1,0:T(8,128)(2,1)} %prepare.1.refs_0_, bf16[336,1152]{1,0:T(8,128)(2,1)} %copy-done.1, bf16[336,1152]{1,0:T(8,128)(2,1)} %copy-done, ...), custom_call_target="tpu_custom_call" | custom-call | flops 5662310400 | bytes 7372800 | tf_op jit(solution)/shard_map/own_sums/pallas_call | solution.py:214
  50.0 2.0 %collective-permute-done.15.refs_13_ = bf16[336,1152]{1,0:T(8,128)(2,1)} collective-permute-done((bf16[336,1152]{1,0:T(8,128)(2,1)}, bf16[336,1152]{1,0:T(8,128)(2,1)}, u32[]{:S(2)}, u32[]{:S(2)}) %collective-permute-start.15) | collective-permute-done | bytes 774176 | tf_op jit(solution)/shard_map/ppermute | solution.py:47
  54.2 26.0 %rest_sums.1 = (bf16[960,1152]{1,0:T(8,128)(2,1)}, bf16[640,1152]{1,0:T(8,128)(2,1)}, bf16[960,1152]{1,0:T(8,128)(2,1)}, bf16[960,1152]{1,0:T(8,128)(2,1)}, bf16...) custom-call(f32[1]{0:T(128)S(6)} %copy.7.sharpness.scale, f32[1]{0:T(128)S(6)} %copy.8.shift, ...), custom_call_target="tpu_custom_call" | custom-call | flops 16986931200 | bytes 22118400 | tf_op jit(solution)/shard_map/rest_sums/pallas_call | solution.py:352
  80.5 4.5 %collective-permute-done.18.refs_1_ = bf16[960,1152]{1,0:T(8,128)(2,1)} collective-permute-done((bf16[960,1152]{1,0:T(8,128)(2,1)}, bf16[960,1152]{1,0:T(8,128)(2,1)}, u32[]{:S(2)}, u32[]{:S(2)}) %collective-permute-start.18) | collective-permute-done | bytes 2211872 | tf_op jit(solution)/shard_map/ppermute | solution.py:47
  85.5 2.6 %join.6 = (bf16[320,1152]{1,0:T(8,128)(2,1)}, bf16[320,1152]{1,0:T(8,128)(2,1)}, bf16[320,1152]{1,0:T(8,128)(2,1)}) custom-call(bf16[960,1152]{1,0:T(8,128)(2,1)} %get-tuple-element.42.refs_0_, bf16[960,1152]{1,0:T(8,128)(2,1)} %collective-permute-done.18.refs_1_), custom_call_target="tpu_custom_call" | custom-call | tf_op jit(solution)/shard_map/join/pallas_call | solution.py:449
  88.1 2.3 %collective-permute-start.24 = (bf16[320,1152]{1,0:T(8,128)(2,1)}, bf16[320,1152]{1,0:T(8,128)(2,1)}, u32[]{:S(2)}, u32[]{:S(2)}) collective-permute-start(bf16[320,1152]{1,0:T(8,128)(2,1)} %get-tuple-element.43), channel_id=1, source_target_pairs={{0,16},{1,19},{16,0},{17,3},{2,18},{3,17},{18,2},{19,1},{32,48},{3... | collective-permute-start | bytes 2211848 | tf_op jit(solution)/shard_map/ppermute | solution.py:47
  93.1 2.3 %join.5 = (bf16[320,1152]{1,0:T(8,128)(2,1)}, bf16[320,1152]{1,0:T(8,128)(2,1)}) custom-call(bf16[640,1152]{1,0:T(8,128)(2,1)} %get-tuple-element.36.refs_0_, bf16[640,1152]{1,0:T(8,128)(2,1)} %collective-permute-done.20.refs_1_), custom_call_target="tpu_custom_call" | custom-call | tf_op jit(solution)/shard_map/join/pallas_call | solution.py:449
  95.5 2.7 %collective-permute-start.22 = (bf16[320,1152]{1,0:T(8,128)(2,1)}, bf16[320,1152]{1,0:T(8,128)(2,1)}, u32[]{:S(2)}, u32[]{:S(2)}) collective-permute-start(bf16[320,1152]{1,0:T(8,128)(2,1)} %get-tuple-element.39), channel_id=1, source_target_pairs={{0,12},{1,97},{16,28},{17,113},{2,14},{3,99},{18,30},{19,115},{32,... | collective-permute-start | bytes 2211848 | tf_op jit(solution)/shard_map/ppermute | solution.py:47
  98.2 2.3 %join.4 = (bf16[320,1152]{1,0:T(8,128)(2,1)}, bf16[320,1152]{1,0:T(8,128)(2,1)}) custom-call(bf16[960,1152]{1,0:T(8,128)(2,1)} %get-tuple-element.30.refs_0_, bf16[960,1152]{1,0:T(8,128)(2,1)} %collective-permute-done.19.refs_1_), custom_call_target="tpu_custom_call" | custom-call | tf_op jit(solution)/shard_map/join/pallas_call | solution.py:449
  100.5 2.4 %join.7 = bf16[320,1152]{1,0:T(8,128)(2,1)} custom-call(bf16[960,1152]{1,0:T(8,128)(2,1)} %get-tuple-element.30.refs_0_, bf16[960,1152]{1,0:T(8,128)(2,1)} %collective-permute-done.19.refs_1_, bf16[320,1152]{1,0:T(8,128)(2,1)} %collective-permute-done.24.refs_2_), custom_call_target="tpu_custom_call" | custom-call | tf_op jit(solution)/shard_map/join/pallas_call | solution.py:449
  103.0 2.5 %add.1 = bf16[320,1152]{1,0:T(8,128)(2,1)} custom-call(bf16[320,1152]{1,0:T(8,128)(2,1)} %get-tuple-element.45.refs_0_, bf16[320,1152]{1,0:T(8,128)(2,1)} %collective-permute-done.26.refs_1_, bf16[320,1152]{1,0:T(8,128)(2,1)} %collective-permute-done.27.refs_2_), custom_call_target="tpu_custom_call" | custom-call | tf_op jit(solution)/shard_map/add/pallas_call | solution.py:492
  105.4 2.0 %collective-permute-start.28 = (bf16[320,1152]{1,0:T(8,128)(2,1)}, bf16[320,1152]{1,0:T(8,128)(2,1)}, u32[]{:S(2)}, u32[]{:S(2)}) collective-permute-start(bf16[320,1152]{1,0:T(8,128)(2,1)} %add.1), channel_id=1, source_target_pairs={{0,16},{1,19},{16,0},{17,3},{2,18},{3,17},{18,2},{19,1},{32,48},{3... | collective-permute-start | bytes 2211848 | tf_op jit(solution)/shard_map/ppermute | solution.py:47
  107.4 2.9 %collective-permute-start.25 = (bf16[320,1152]{1,0:T(8,128)(2,1)}, bf16[320,1152]{1,0:T(8,128)(2,1)}, u32[]{:S(2)}, u32[]{:S(2)}) collective-permute-start(bf16[320,1152]{1,0:T(8,128)(2,1)} %join.7), channel_id=1, source_target_pairs={{0,8},{1,65},{16,24},{17,81},{2,10},{3,67},{18,26},{19,83},{32,40}... | collective-permute-start | bytes 2211848 | tf_op jit(solution)/shard_map/ppermute | solution.py:47
  110.5 2.9 %split_total.1 = (f32[160,1152]{1,0:T(8,128)}, f32[160,1152]{1,0:T(8,128)}) custom-call(bf16[320,1152]{1,0:T(8,128)(2,1)} %get-tuple-element.35.refs_0_, bf16[320,1152]{1,0:T(8,128)(2,1)} %collective-permute-done.21.refs_1_, bf16[320,1152]{1,0:T(8,128)(2,1)} %collective-permute-done.22.refs_2_), custom_call_target="tpu_custom_call" | custom-call | tf_op jit(solution)/shard_map/split_total/pallas_call | solution.py:516
  114.2 3.4 %collective-permute-done.28.last = bf16[320,1152]{1,0:T(8,128)(2,1)} collective-permute-done((bf16[320,1152]{1,0:T(8,128)(2,1)}, bf16[320,1152]{1,0:T(8,128)(2,1)}, u32[]{:S(2)}, u32[]{:S(2)}) %collective-permute-start.28) | collective-permute-done | bytes 737312 | tf_op jit(solution)/shard_map/ppermute | solution.py:47
  117.6 2.2 %collective-permute-start.30 = (bf16[320,1152]{1,0:T(8,128)(2,1)}, bf16[320,1152]{1,0:T(8,128)(2,1)}, u32[]{:S(2)}, u32[]{:S(2)}) collective-permute-start(bf16[320,1152]{1,0:T(8,128)(2,1)} %collective-permute-done.28.last), channel_id=1, source_target_pairs={{0,1},{1,0},{16,17},{17,16},{2,3},{3,2},{18,19},{19,18},{32,33},{3... | collective-permute-start | bytes 2211848 | tf_op jit(solution)/shard_map/ppermute | solution.py:47
  119.8 2.4 %collective-permute-start.29 = (bf16[320,1152]{1,0:T(8,128)(2,1)}, bf16[320,1152]{1,0:T(8,128)(2,1)}, u32[]{:S(2)}, u32[]{:S(2)}) collective-permute-start(bf16[320,1152]{1,0:T(8,128)(2,1)} %collective-permute-done.25.far), channel_id=1, source_target_pairs={{0,1},{1,0},{16,17},{17,16},{2,3},{3,2},{18,19},{19,18},{32,33},{3... | collective-permute-start | bytes 2211848 | tf_op jit(solution)/shard_map/ppermute | solution.py:47
  122.2 2.2 %collective-permute-done.29.got_far = bf16[320,1152]{1,0:T(8,128)(2,1)} collective-permute-done((bf16[320,1152]{1,0:T(8,128)(2,1)}, bf16[320,1152]{1,0:T(8,128)(2,1)}, u32[]{:S(2)}, u32[]{:S(2)}) %collective-permute-start.29) | collective-permute-done | bytes 737312 | tf_op jit(solution)/shard_map/ppermute | solution.py:47
  124.4 6.2 %finish.1 = (f32[160,1152]{1,0:T(8,128)}, f32[160,1152]{1,0:T(8,128)}) custom-call(f32[1]{0:T(128)S(6)} %copy.7.sharpness.scale, bf16[160,1152]{1,0:T(8,128)(2,1)} %image.3, bf16[160,1152]{1,0:T(8,128)(2,1)} %text.3, f32[160,1152]{1,0:T(8,128)} %get-tuple-element.40.kept, f32[160,1152]{1,0:T(8,128)} %collective-permute-done.23.got, ...), custom_call_target="tpu_custom_call" | custom-call | tf_op jit(solution)/shard_map/finish/pallas_call | solution.py:555
  (54 shorter events, 22.8 us)
Async XLA Ops:
  7.2 13.6 %collective-permute-start.5 = (bf16[336,1152]{1,0:T(8,128)(2,1)}, bf16[336,1152]{1,0:T(8,128)(2,1)}, u32[]{:S(2)}, u32[]{:S(2)}) collective-permute-start(bf16[336,1152]{1,0:T(8,128)(2,1)} %prepare.1.refs_0_), channel_id=1, source_target_pairs={{0,16},{1,19},{16,0},{17,3},{2,18},{3,17},{18,2},{19,1},{32,48},{3... | collective-permute-start | bytes 2322440 | tf_op jit(solution)/shard_map/ppermute | solution.py:47
  11.0 12.6 %collective-permute-start.4 = (bf16[336,1152]{1,0:T(8,128)(2,1)}, bf16[336,1152]{1,0:T(8,128)(2,1)S(1)}, u32[]{:S(2)}, u32[]{:S(2)}) collective-permute-start(bf16[336,1152]{1,0:T(8,128)(2,1)} %prepare.1.refs_0_), channel_id=1, source_target_pairs={{0,4},{1,33},{16,20},{17,49},{2,6},{3,35},{18,22},{19,51},{32,36},... | collective-permute-start | bytes 2322440 | tf_op jit(solution)/shard_map/ppermute | solution.py:47
  12.3 12.2 %collective-permute-start.3 = (bf16[336,1152]{1,0:T(8,128)(2,1)}, bf16[336,1152]{1,0:T(8,128)(2,1)S(1)}, u32[]{:S(2)}, u32[]{:S(2)}) collective-permute-start(bf16[336,1152]{1,0:T(8,128)(2,1)} %prepare.1.refs_0_), channel_id=1, source_target_pairs={{0,12},{1,97},{16,28},{17,113},{2,14},{3,99},{18,30},{19,115},{32,... | collective-permute-start | bytes 2322440 | tf_op jit(solution)/shard_map/ppermute | solution.py:47
  13.7 17.1 %collective-permute-start.10 = (bf16[336,1152]{1,0:T(8,128)(2,1)}, bf16[336,1152]{1,0:T(8,128)(2,1)}, u32[]{:S(2)}, u32[]{:S(2)}) collective-permute-start(bf16[336,1152]{1,0:T(8,128)(2,1)} %prepare.1.refs_0_), channel_id=1, source_target_pairs={{0,1},{1,0},{16,17},{17,16},{2,3},{3,2},{18,19},{19,18},{32,33},{3... | collective-permute-start | bytes 2322440 | tf_op jit(solution)/shard_map/ppermute | solution.py:47
  13.7 19.0 %collective-permute-start.6 = (bf16[336,1152]{1,0:T(8,128)(2,1)}, bf16[336,1152]{1,0:T(8,128)(2,1)}, u32[]{:S(2)}, u32[]{:S(2)}) collective-permute-start(bf16[336,1152]{1,0:T(8,128)(2,1)} %prepare.1.refs_0_), channel_id=1, source_target_pairs={{0,8},{1,65},{16,24},{17,81},{2,10},{3,67},{18,26},{19,83},{32,40}... | collective-permute-start | bytes 2322440 | tf_op jit(solution)/shard_map/ppermute | solution.py:47
  20.7 13.6 %collective-permute-start.13 = (bf16[336,1152]{1,0:T(8,128)(2,1)}, bf16[336,1152]{1,0:T(8,128)(2,1)}, u32[]{:S(2)}, u32[]{:S(2)}) collective-permute-start(bf16[336,1152]{1,0:T(8,128)(2,1)} %collective-permute-done.5.refs_3_), channel_id=1, source_target_pairs={{0,1},{1,0},{16,17},{17,16},{2,3},{3,2},{18,19},{19,18},{32,33},{3... | collective-permute-start | bytes 2322440 | tf_op jit(solution)/shard_map/ppermute | solution.py:47
  24.5 12.6 %collective-permute-start.12 = (bf16[336,1152]{1,0:T(8,128)(2,1)S(1)}, bf16[336,1152]{1,0:T(8,128)(2,1)S(1)}, u32[]{:S(2)}, u32[]{:S(2)}) collective-permute-start(bf16[336,1152]{1,0:T(8,128)(2,1)S(1)} %collective-permute-done.4.refs_2_), channel_id=1, source_target_pairs={{0,1},{1,0},{16,17},{17,16},{2,3},{3,2},{18,19},{19,18},{32,33},{3... | collective-permute-start | bytes 2322440 | tf_op jit(solution)/shard_map/ppermute | solution.py:47
  24.5 13.6 %collective-permute-start.11 = (bf16[336,1152]{1,0:T(8,128)(2,1)S(1)}, bf16[336,1152]{1,0:T(8,128)(2,1)}, u32[]{:S(2)}, u32[]{:S(2)}) collective-permute-start(bf16[336,1152]{1,0:T(8,128)(2,1)S(1)} %collective-permute-done.3.refs_1_), channel_id=1, source_target_pairs={{0,1},{1,0},{16,17},{17,16},{2,3},{3,2},{18,19},{19,18},{32,33},{3... | collective-permute-start | bytes 2322440 | tf_op jit(solution)/shard_map/ppermute | solution.py:47
  30.8 18.5 %collective-permute-start.8 = (bf16[336,1152]{1,0:T(8,128)(2,1)}, bf16[336,1152]{1,0:T(8,128)(2,1)}, u32[]{:S(2)}, u32[]{:S(2)}) collective-permute-start(bf16[336,1152]{1,0:T(8,128)(2,1)} %collective-permute-done.5.refs_3_), channel_id=1, source_target_pairs={{0,4},{1,33},{16,20},{17,49},{2,6},{3,35},{18,22},{19,51},{32,36},... | collective-permute-start | bytes 2322440 | tf_op jit(solution)/shard_map/ppermute | solution.py:47
  32.8 16.5 %collective-permute-start.9 = (bf16[336,1152]{1,0:T(8,128)(2,1)}, bf16[336,1152]{1,0:T(8,128)(2,1)}, u32[]{:S(2)}, u32[]{:S(2)}) collective-permute-start(bf16[336,1152]{1,0:T(8,128)(2,1)} %collective-permute-done.6.refs_4_), channel_id=1, source_target_pairs={{0,16},{1,19},{16,0},{17,3},{2,18},{3,17},{18,2},{19,1},{32,48},{3... | collective-permute-start | bytes 2322440 | tf_op jit(solution)/shard_map/ppermute | solution.py:47
  34.3 15.0 %collective-permute-start.7 = (bf16[336,1152]{1,0:T(8,128)(2,1)}, bf16[336,1152]{1,0:T(8,128)(2,1)}, u32[]{:S(2)}, u32[]{:S(2)}) collective-permute-start(bf16[336,1152]{1,0:T(8,128)(2,1)} %collective-permute-done.5.refs_3_), channel_id=1, source_target_pairs={{0,12},{1,97},{16,28},{17,113},{2,14},{3,99},{18,30},{19,115},{32,... | collective-permute-start | bytes 2322440 | tf_op jit(solution)/shard_map/ppermute | solution.py:47
  37.2 12.8 %collective-permute-start.14 = (bf16[336,1152]{1,0:T(8,128)(2,1)}, bf16[336,1152]{1,0:T(8,128)(2,1)}, u32[]{:S(2)}, u32[]{:S(2)}) collective-permute-start(bf16[336,1152]{1,0:T(8,128)(2,1)} %collective-permute-done.6.refs_4_), channel_id=1, source_target_pairs={{0,1},{1,0},{16,17},{17,16},{2,3},{3,2},{18,19},{19,18},{32,33},{3... | collective-permute-start | bytes 2322440 | tf_op jit(solution)/shard_map/ppermute | solution.py:47
  80.2 4.7 %collective-permute-start.18 = (bf16[960,1152]{1,0:T(8,128)(2,1)}, bf16[960,1152]{1,0:T(8,128)(2,1)}, u32[]{:S(2)}, u32[]{:S(2)}) collective-permute-start(bf16[960,1152]{1,0:T(8,128)(2,1)} %get-tuple-element.33), channel_id=1, source_target_pairs={{0,1},{1,0},{16,17},{17,16},{2,3},{3,2},{18,19},{19,18},{32,33},{3... | collective-permute-start | bytes 6635528 | tf_op jit(solution)/shard_map/ppermute | solution.py:47
  85.0 10.6 %collective-permute-start.19 = (bf16[960,1152]{1,0:T(8,128)(2,1)}, bf16[960,1152]{1,0:T(8,128)(2,1)}, u32[]{:S(2)}, u32[]{:S(2)}) collective-permute-start(bf16[960,1152]{1,0:T(8,128)(2,1)} %get-tuple-element.34), channel_id=1, source_target_pairs={{0,1},{1,0},{16,17},{17,16},{2,3},{3,2},{18,19},{19,18},{32,33},{3... | collective-permute-start | bytes 6635528 | tf_op jit(solution)/shard_map/ppermute | solution.py:47
  85.1 8.0 %collective-permute-start.20 = (bf16[640,1152]{1,0:T(8,128)(2,1)}, bf16[640,1152]{1,0:T(8,128)(2,1)}, u32[]{:S(2)}, u32[]{:S(2)}) collective-permute-start(bf16[640,1152]{1,0:T(8,128)(2,1)} %get-tuple-element.37), channel_id=1, source_target_pairs={{0,1},{1,0},{16,17},{17,16},{2,3},{3,2},{18,19},{19,18},{32,33},{3... | collective-permute-start | bytes 4423688 | tf_op jit(solution)/shard_map/ppermute | solution.py:47
  88.1 12.4 %collective-permute-start.24 = (bf16[320,1152]{1,0:T(8,128)(2,1)}, bf16[320,1152]{1,0:T(8,128)(2,1)}, u32[]{:S(2)}, u32[]{:S(2)}) collective-permute-start(bf16[320,1152]{1,0:T(8,128)(2,1)} %get-tuple-element.43), channel_id=1, source_target_pairs={{0,16},{1,19},{16,0},{17,3},{2,18},{3,17},{18,2},{19,1},{32,48},{3... | collective-permute-start | bytes 2211848 | tf_op jit(solution)/shard_map/ppermute | solution.py:47
  90.4 12.6 %collective-permute-start.26 = (bf16[320,1152]{1,0:T(8,128)(2,1)}, bf16[320,1152]{1,0:T(8,128)(2,1)}, u32[]{:S(2)}, u32[]{:S(2)}) collective-permute-start(bf16[320,1152]{1,0:T(8,128)(2,1)} %get-tuple-element.46), channel_id=1, source_target_pairs={{0,4},{1,33},{16,20},{17,49},{2,6},{3,35},{18,22},{19,51},{32,36},... | collective-permute-start | bytes 2211848 | tf_op jit(solution)/shard_map/ppermute | solution.py:47
  91.7 11.3 %collective-permute-start.27 = (bf16[320,1152]{1,0:T(8,128)(2,1)}, bf16[320,1152]{1,0:T(8,128)(2,1)}, u32[]{:S(2)}, u32[]{:S(2)}) collective-permute-start(bf16[320,1152]{1,0:T(8,128)(2,1)} %get-tuple-element.47), channel_id=1, source_target_pairs={{0,12},{1,97},{16,28},{17,113},{2,14},{3,99},{18,30},{19,115},{32,... | collective-permute-start | bytes 2211848 | tf_op jit(solution)/shard_map/ppermute | solution.py:47
  95.4 15.0 %collective-permute-start.21 = (bf16[320,1152]{1,0:T(8,128)(2,1)}, bf16[320,1152]{1,0:T(8,128)(2,1)}, u32[]{:S(2)}, u32[]{:S(2)}) collective-permute-start(bf16[320,1152]{1,0:T(8,128)(2,1)} %get-tuple-element.38), channel_id=1, source_target_pairs={{0,4},{1,33},{16,20},{17,49},{2,6},{3,35},{18,22},{19,51},{32,36},... | collective-permute-start | bytes 2211848 | tf_op jit(solution)/shard_map/ppermute | solution.py:47
  95.5 14.9 %collective-permute-start.22 = (bf16[320,1152]{1,0:T(8,128)(2,1)}, bf16[320,1152]{1,0:T(8,128)(2,1)}, u32[]{:S(2)}, u32[]{:S(2)}) collective-permute-start(bf16[320,1152]{1,0:T(8,128)(2,1)} %get-tuple-element.39), channel_id=1, source_target_pairs={{0,12},{1,97},{16,28},{17,113},{2,14},{3,99},{18,30},{19,115},{32,... | collective-permute-start | bytes 2211848 | tf_op jit(solution)/shard_map/ppermute | solution.py:47
  105.4 12.1 %collective-permute-start.28 = (bf16[320,1152]{1,0:T(8,128)(2,1)}, bf16[320,1152]{1,0:T(8,128)(2,1)}, u32[]{:S(2)}, u32[]{:S(2)}) collective-permute-start(bf16[320,1152]{1,0:T(8,128)(2,1)} %add.1), channel_id=1, source_target_pairs={{0,16},{1,19},{16,0},{17,3},{2,18},{3,17},{18,2},{19,1},{32,48},{3... | collective-permute-start | bytes 2211848 | tf_op jit(solution)/shard_map/ppermute | solution.py:47
  107.4 12.4 %collective-permute-start.25 = (bf16[320,1152]{1,0:T(8,128)(2,1)}, bf16[320,1152]{1,0:T(8,128)(2,1)}, u32[]{:S(2)}, u32[]{:S(2)}) collective-permute-start(bf16[320,1152]{1,0:T(8,128)(2,1)} %join.7), channel_id=1, source_target_pairs={{0,8},{1,65},{16,24},{17,81},{2,10},{3,67},{18,26},{19,83},{32,40}... | collective-permute-start | bytes 2211848 | tf_op jit(solution)/shard_map/ppermute | solution.py:47
  113.4 8.8 %collective-permute-start.23 = (f32[160,1152]{1,0:T(8,128)}, f32[160,1152]{1,0:T(8,128)}, u32[]{:S(2)}, u32[]{:S(2)}) collective-permute-start(f32[160,1152]{1,0:T(8,128)} %get-tuple-element.41), channel_id=1, source_target_pairs={{0,1},{1,0},{16,17},{17,16},{2,3},{3,2},{18,19},{19,18},{32,33},{3... | collective-permute-start | bytes 2211848 | tf_op jit(solution)/shard_map/ppermute | solution.py:47
  117.6 4.7 %collective-permute-start.30 = (bf16[320,1152]{1,0:T(8,128)(2,1)}, bf16[320,1152]{1,0:T(8,128)(2,1)}, u32[]{:S(2)}, u32[]{:S(2)}) collective-permute-start(bf16[320,1152]{1,0:T(8,128)(2,1)} %collective-permute-done.28.last), channel_id=1, source_target_pairs={{0,1},{1,0},{16,17},{17,16},{2,3},{3,2},{18,19},{19,18},{32,33},{3... | collective-permute-start | bytes 2211848 | tf_op jit(solution)/shard_map/ppermute | solution.py:47
  (10 other events, 37.7 us)

commit v6 on v4

--- a/solution.py
+++ b/solution.py
@@ -183,9 +183,8 @@
     text_sum[...] = along_text(coefficient, images)
     copies = [pltpu.make_async_copy(text_sum, text_to, out_sem.at[0])]
     copies[0].start()
-    part = images.shape[0] // 2
-    for i in range(2):
-        here = pl.ds(i * part, part)
+    part = images.shape[0] * 7 // 10
+    for i, here in enumerate((pl.ds(0, part), pl.ds(part, images.shape[0] - part))):
         image_sum[here, :] = along_image(coefficient.at[:, here], texts)
         copies.append(pltpu.make_async_copy(image_sum.at[here], image_to.at[here], out_sem.at[1 + i]))
         copies[-1].start()

time: 128 us -> 128 us (level)
  no operation moved by 1% of the time
where the time goes in v6:
time: 128 us
  Pallas kernels  58.2 us (45%)
  starting transfers between devices  40.7 us (32%)
  waiting for transfers between devices  24.9 us (19%)
  between operations  2.1 us (2%)
  local copies, waits for them, and re-layouts  1.71 us (1%)
    ppermute x31, starting transfers between devices, send(): return lax.ppermute(value, AXES, perm)  40.7 us
    pallas_call x1, Pallas kernels, rest_sums(): pl.pallas_call(rest_kernel, out_shape=tuple(shapes * 2), in_specs=[SMEM]...  26 us
    ppermute x31, waiting for transfers between devices, send(): return lax.ppermute(value, AXES, perm)  24.9 us
    pallas_call x1, Pallas kernels, own_sums(): pl.pallas_call(own_kernel, out_shape=(jax.ShapeDtypeStruct((4 * rows, wid...  11.4 us
    pallas_call x4, Pallas kernels, join(): pl.pallas_call(lambda *refs: join_kernel(pieces, len(extra), *refs), out_...  9.67 us
    pallas_call x1, Pallas kernels, finish(): pl.pallas_call(finish_kernel, grid=(2,), out_shape=(shape, shape), in_spe...  3.25 us
    pallas_call x1, Pallas kernels, split_total(): pl.pallas_call(split_kernel, out_shape=(shape, shape), in_specs=[VMEM] *...  2.92 us
  transfers between devices with their start and end apart: 31, of which 12 were waited for; matrix products, arithmetic and copies ran while one was open for 0% of the time, Pallas kernels for 21%

profile of v6, /device:TPU:1, one launch (start us, length us, event | category | flops | bytes accessed | tf_op | source)
XLA Modules:
  0.0 127.5 jit_solution(7170475530103971300)
XLA Ops:
  4.3 2.5 %prepare.1.refs_0_ = bf16[336,1152]{1,0:T(8,128)(2,1)} custom-call(bf16[160,1152]{1,0:T(8,128)(2,1)} %image.3, bf16[160,1152]{1,0:T(8,128)(2,1)} %text.3, bf16[160,1152]{1,0:T(8,128)(2,1)} %collective-permute-done.other_image, bf16[160,1152]{1,0:T(8,128)(2,1)} %collective-permute-done.1.other_text, s32[1,160]{1,0:T(1,128)} %bitcast.2, ...), custom_call_target="tpu_custom_call" | custom-call | tf_op jit(solution)/shard_map/prepare/pallas_call | solution.py:90
  6.8 3.8 %collective-permute-start.5 = (bf16[336,1152]{1,0:T(8,128)(2,1)}, bf16[336,1152]{1,0:T(8,128)(2,1)}, u32[]{:S(2)}, u32[]{:S(2)}) collective-permute-start(bf16[336,1152]{1,0:T(8,128)(2,1)} %prepare.1.refs_0_), channel_id=1, source_target_pairs={{0,16},{1,19},{16,0},{17,3},{2,18},{3,17},{18,2},{19,1},{32,48},{3... | collective-permute-start | bytes 2322440 | tf_op jit(solution)/shard_map/ppermute | solution.py:47
  13.4 1.9 %collective-permute-start.6 = (bf16[336,1152]{1,0:T(8,128)(2,1)}, bf16[336,1152]{1,0:T(8,128)(2,1)}, u32[]{:S(2)}, u32[]{:S(2)}) collective-permute-start(bf16[336,1152]{1,0:T(8,128)(2,1)} %prepare.1.refs_0_), channel_id=1, source_target_pairs={{0,8},{1,65},{16,24},{17,81},{2,10},{3,67},{18,26},{19,83},{32,40}... | collective-permute-start | bytes 2322440 | tf_op jit(solution)/shard_map/ppermute | solution.py:47
  15.3 5.1 %collective-permute-done.5.refs_3_ = bf16[336,1152]{1,0:T(8,128)(2,1)} collective-permute-done((bf16[336,1152]{1,0:T(8,128)(2,1)}, bf16[336,1152]{1,0:T(8,128)(2,1)}, u32[]{:S(2)}, u32[]{:S(2)}) %collective-permute-start.5) | collective-permute-done | bytes 774176 | tf_op jit(solution)/shard_map/ppermute | solution.py:47
  20.4 2.9 %collective-permute-done.4.refs_2_ = bf16[336,1152]{1,0:T(8,128)(2,1)S(1)} collective-permute-done((bf16[336,1152]{1,0:T(8,128)(2,1)}, bf16[336,1152]{1,0:T(8,128)(2,1)S(1)}, u32[]{:S(2)}, u32[]{:S(2)}) %collective-permute-start.4) | collective-permute-done | bytes 774176 | tf_op jit(solution)/shard_map/ppermute | solution.py:47
  24.2 6.3 %collective-permute-start.11 = (bf16[336,1152]{1,0:T(8,128)(2,1)S(1)}, bf16[336,1152]{1,0:T(8,128)(2,1)}, u32[]{:S(2)}, u32[]{:S(2)}) collective-permute-start(bf16[336,1152]{1,0:T(8,128)(2,1)S(1)} %collective-permute-done.3.refs_1_), channel_id=1, source_target_pairs={{0,1},{1,0},{16,17},{17,16},{2,3},{3,2},{18,19},{19,18},{32,33},{3... | collective-permute-start | bytes 2322440 | tf_op jit(solution)/shard_map/ppermute | solution.py:47
  37.7 11.4 %own_sums.1 = (f32[1280,1152]{1,0:T(8,128)}, f32[640,1152]{1,0:T(8,128)}) custom-call(f32[1]{0:T(128)S(6)} %copy.7.sharpness.scale, f32[1]{0:T(128)S(6)} %copy.8.shift, bf16[336,1152]{1,0:T(8,128)(2,1)} %prepare.1.refs_0_, bf16[336,1152]{1,0:T(8,128)(2,1)} %copy-done.1, bf16[336,1152]{1,0:T(8,128)(2,1)} %copy-done, ...), custom_call_target="tpu_custom_call" | custom-call | flops 5662310400 | bytes 7372800 | tf_op jit(solution)/shard_map/own_sums/pallas_call | solution.py:210
  49.9 2.0 %collective-permute-done.15.refs_13_ = bf16[336,1152]{1,0:T(8,128)(2,1)} collective-permute-done((bf16[336,1152]{1,0:T(8,128)(2,1)}, bf16[336,1152]{1,0:T(8,128)(2,1)}, u32[]{:S(2)}, u32[]{:S(2)}) %collective-permute-start.15) | collective-permute-done | bytes 774176 | tf_op jit(solution)/shard_map/ppermute | solution.py:47
  54.1 26.0 %rest_sums.1 = (bf16[960,1152]{1,0:T(8,128)(2,1)}, bf16[640,1152]{1,0:T(8,128)(2,1)}, bf16[960,1152]{1,0:T(8,128)(2,1)}, bf16[960,1152]{1,0:T(8,128)(2,1)}, bf16...) custom-call(f32[1]{0:T(128)S(6)} %copy.7.sharpness.scale, f32[1]{0:T(128)S(6)} %copy.8.shift, ...), custom_call_target="tpu_custom_call" | custom-call | flops 16986931200 | bytes 22118400 | tf_op jit(solution)/shard_map/rest_sums/pallas_call | solution.py:348
  80.3 4.5 %collective-permute-done.18.refs_1_ = bf16[960,1152]{1,0:T(8,128)(2,1)} collective-permute-done((bf16[960,1152]{1,0:T(8,128)(2,1)}, bf16[960,1152]{1,0:T(8,128)(2,1)}, u32[]{:S(2)}, u32[]{:S(2)}) %collective-permute-start.18) | collective-permute-done | bytes 2211872 | tf_op jit(solution)/shard_map/ppermute | solution.py:47
  85.3 2.6 %join.6 = (bf16[320,1152]{1,0:T(8,128)(2,1)}, bf16[320,1152]{1,0:T(8,128)(2,1)}, bf16[320,1152]{1,0:T(8,128)(2,1)}) custom-call(bf16[960,1152]{1,0:T(8,128)(2,1)} %get-tuple-element.42.refs_0_, bf16[960,1152]{1,0:T(8,128)(2,1)} %collective-permute-done.18.refs_1_), custom_call_target="tpu_custom_call" | custom-call | tf_op jit(solution)/shard_map/join/pallas_call | solution.py:445
  88.0 2.2 %collective-permute-start.24 = (bf16[320,1152]{1,0:T(8,128)(2,1)}, bf16[320,1152]{1,0:T(8,128)(2,1)}, u32[]{:S(2)}, u32[]{:S(2)}) collective-permute-start(bf16[320,1152]{1,0:T(8,128)(2,1)} %get-tuple-element.43), channel_id=1, source_target_pairs={{0,16},{1,19},{16,0},{17,3},{2,18},{3,17},{18,2},{19,1},{32,48},{3... | collective-permute-start | bytes 2211848 | tf_op jit(solution)/shard_map/ppermute | solution.py:47
  92.9 2.3 %join.5 = (bf16[320,1152]{1,0:T(8,128)(2,1)}, bf16[320,1152]{1,0:T(8,128)(2,1)}) custom-call(bf16[640,1152]{1,0:T(8,128)(2,1)} %get-tuple-element.36.refs_0_, bf16[640,1152]{1,0:T(8,128)(2,1)} %collective-permute-done.20.refs_1_), custom_call_target="tpu_custom_call" | custom-call | tf_op jit(solution)/shard_map/join/pallas_call | solution.py:445
  95.4 2.7 %collective-permute-start.22 = (bf16[320,1152]{1,0:T(8,128)(2,1)}, bf16[320,1152]{1,0:T(8,128)(2,1)}, u32[]{:S(2)}, u32[]{:S(2)}) collective-permute-start(bf16[320,1152]{1,0:T(8,128)(2,1)} %get-tuple-element.39), channel_id=1, source_target_pairs={{0,12},{1,97},{16,28},{17,113},{2,14},{3,99},{18,30},{19,115},{32,... | collective-permute-start | bytes 2211848 | tf_op jit(solution)/shard_map/ppermute | solution.py:47
  98.0 2.3 %join.4 = (bf16[320,1152]{1,0:T(8,128)(2,1)}, bf16[320,1152]{1,0:T(8,128)(2,1)}) custom-call(bf16[960,1152]{1,0:T(8,128)(2,1)} %get-tuple-element.30.refs_0_, bf16[960,1152]{1,0:T(8,128)(2,1)} %collective-permute-done.19.refs_1_), custom_call_target="tpu_custom_call" | custom-call | tf_op jit(solution)/shard_map/join/pallas_call | solution.py:445
  100.4 2.4 %join.7 = bf16[320,1152]{1,0:T(8,128)(2,1)} custom-call(bf16[960,1152]{1,0:T(8,128)(2,1)} %get-tuple-element.30.refs_0_, bf16[960,1152]{1,0:T(8,128)(2,1)} %collective-permute-done.19.refs_1_, bf16[320,1152]{1,0:T(8,128)(2,1)} %collective-permute-done.24.refs_2_), custom_call_target="tpu_custom_call" | custom-call | tf_op jit(solution)/shard_map/join/pallas_call | solution.py:445
  102.8 2.5 %add.1 = bf16[320,1152]{1,0:T(8,128)(2,1)} custom-call(bf16[320,1152]{1,0:T(8,128)(2,1)} %get-tuple-element.45.refs_0_, bf16[320,1152]{1,0:T(8,128)(2,1)} %collective-permute-done.26.refs_1_, bf16[320,1152]{1,0:T(8,128)(2,1)} %collective-permute-done.27.refs_2_), custom_call_target="tpu_custom_call" | custom-call | tf_op jit(solution)/shard_map/add/pallas_call | solution.py:488
  107.2 2.9 %collective-permute-start.25 = (bf16[320,1152]{1,0:T(8,128)(2,1)}, bf16[320,1152]{1,0:T(8,128)(2,1)}, u32[]{:S(2)}, u32[]{:S(2)}) collective-permute-start(bf16[320,1152]{1,0:T(8,128)(2,1)} %join.7), channel_id=1, source_target_pairs={{0,8},{1,65},{16,24},{17,81},{2,10},{3,67},{18,26},{19,83},{32,40}... | collective-permute-start | bytes 2211848 | tf_op jit(solution)/shard_map/ppermute | solution.py:47
  110.3 2.9 %split_total.1 = (f32[160,1152]{1,0:T(8,128)}, f32[160,1152]{1,0:T(8,128)}) custom-call(bf16[320,1152]{1,0:T(8,128)(2,1)} %get-tuple-element.35.refs_0_, bf16[320,1152]{1,0:T(8,128)(2,1)} %collective-permute-done.21.refs_1_, bf16[320,1152]{1,0:T(8,128)(2,1)} %collective-permute-done.22.refs_2_), custom_call_target="tpu_custom_call" | custom-call | tf_op jit(solution)/shard_map/split_total/pallas_call | solution.py:512
  114.1 3.4 %collective-permute-done.28.last = bf16[320,1152]{1,0:T(8,128)(2,1)} collective-permute-done((bf16[320,1152]{1,0:T(8,128)(2,1)}, bf16[320,1152]{1,0:T(8,128)(2,1)}, u32[]{:S(2)}, u32[]{:S(2)}) %collective-permute-start.28) | collective-permute-done | bytes 737312 | tf_op jit(solution)/shard_map/ppermute | solution.py:47
  117.4 2.2 %collective-permute-start.30 = (bf16[320,1152]{1,0:T(8,128)(2,1)}, bf16[320,1152]{1,0:T(8,128)(2,1)}, u32[]{:S(2)}, u32[]{:S(2)}) collective-permute-start(bf16[320,1152]{1,0:T(8,128)(2,1)} %collective-permute-done.28.last), channel_id=1, source_target_pairs={{0,1},{1,0},{16,17},{17,16},{2,3},{3,2},{18,19},{19,18},{32,33},{3... | collective-permute-start | bytes 2211848 | tf_op jit(solution)/shard_map/ppermute | solution.py:47
  119.6 2.4 %collective-permute-start.29 = (bf16[320,1152]{1,0:T(8,128)(2,1)}, bf16[320,1152]{1,0:T(8,128)(2,1)}, u32[]{:S(2)}, u32[]{:S(2)}) collective-permute-start(bf16[320,1152]{1,0:T(8,128)(2,1)} %collective-permute-done.25.far), channel_id=1, source_target_pairs={{0,1},{1,0},{16,17},{17,16},{2,3},{3,2},{18,19},{19,18},{32,33},{3... | collective-permute-start | bytes 2211848 | tf_op jit(solution)/shard_map/ppermute | solution.py:47
  122.1 2.2 %collective-permute-done.29.got_far = bf16[320,1152]{1,0:T(8,128)(2,1)} collective-permute-done((bf16[320,1152]{1,0:T(8,128)(2,1)}, bf16[320,1152]{1,0:T(8,128)(2,1)}, u32[]{:S(2)}, u32[]{:S(2)}) %collective-permute-start.29) | collective-permute-done | bytes 737312 | tf_op jit(solution)/shard_map/ppermute | solution.py:47
  124.3 3.3 %finish.1 = (f32[160,1152]{1,0:T(8,128)}, f32[160,1152]{1,0:T(8,128)}) custom-call(f32[1]{0:T(128)S(6)} %copy.7.sharpness.scale, bf16[160,1152]{1,0:T(8,128)(2,1)} %image.3, bf16[160,1152]{1,0:T(8,128)(2,1)} %text.3, f32[160,1152]{1,0:T(8,128)} %get-tuple-element.40.kept, f32[160,1152]{1,0:T(8,128)} %collective-permute-done.23.got, ...), custom_call_target="tpu_custom_call" | custom-call | tf_op jit(solution)/shard_map/finish/pallas_call | solution.py:547
  (54 shorter events, 22.8 us)
Async XLA Ops:
  6.8 13.6 %collective-permute-start.5 = (bf16[336,1152]{1,0:T(8,128)(2,1)}, bf16[336,1152]{1,0:T(8,128)(2,1)}, u32[]{:S(2)}, u32[]{:S(2)}) collective-permute-start(bf16[336,1152]{1,0:T(8,128)(2,1)} %prepare.1.refs_0_), channel_id=1, source_target_pairs={{0,16},{1,19},{16,0},{17,3},{2,18},{3,17},{18,2},{19,1},{32,48},{3... | collective-permute-start | bytes 2322440 | tf_op jit(solution)/shard_map/ppermute | solution.py:47
  10.6 12.6 %collective-permute-start.4 = (bf16[336,1152]{1,0:T(8,128)(2,1)}, bf16[336,1152]{1,0:T(8,128)(2,1)S(1)}, u32[]{:S(2)}, u32[]{:S(2)}) collective-permute-start(bf16[336,1152]{1,0:T(8,128)(2,1)} %prepare.1.refs_0_), channel_id=1, source_target_pairs={{0,4},{1,33},{16,20},{17,49},{2,6},{3,35},{18,22},{19,51},{32,36},... | collective-permute-start | bytes 2322440 | tf_op jit(solution)/shard_map/ppermute | solution.py:47
  11.9 12.2 %collective-permute-start.3 = (bf16[336,1152]{1,0:T(8,128)(2,1)}, bf16[336,1152]{1,0:T(8,128)(2,1)S(1)}, u32[]{:S(2)}, u32[]{:S(2)}) collective-permute-start(bf16[336,1152]{1,0:T(8,128)(2,1)} %prepare.1.refs_0_), channel_id=1, source_target_pairs={{0,12},{1,97},{16,28},{17,113},{2,14},{3,99},{18,30},{19,115},{32,... | collective-permute-start | bytes 2322440 | tf_op jit(solution)/shard_map/ppermute | solution.py:47
  13.4 17.1 %collective-permute-start.10 = (bf16[336,1152]{1,0:T(8,128)(2,1)}, bf16[336,1152]{1,0:T(8,128)(2,1)}, u32[]{:S(2)}, u32[]{:S(2)}) collective-permute-start(bf16[336,1152]{1,0:T(8,128)(2,1)} %prepare.1.refs_0_), channel_id=1, source_target_pairs={{0,1},{1,0},{16,17},{17,16},{2,3},{3,2},{18,19},{19,18},{32,33},{3... | collective-permute-start | bytes 2322440 | tf_op jit(solution)/shard_map/ppermute | solution.py:47
  13.4 19.0 %collective-permute-start.6 = (bf16[336,1152]{1,0:T(8,128)(2,1)}, bf16[336,1152]{1,0:T(8,128)(2,1)}, u32[]{:S(2)}, u32[]{:S(2)}) collective-permute-start(bf16[336,1152]{1,0:T(8,128)(2,1)} %prepare.1.refs_0_), channel_id=1, source_target_pairs={{0,8},{1,65},{16,24},{17,81},{2,10},{3,67},{18,26},{19,83},{32,40}... | collective-permute-start | bytes 2322440 | tf_op jit(solution)/shard_map/ppermute | solution.py:47
  20.4 13.6 %collective-permute-start.13 = (bf16[336,1152]{1,0:T(8,128)(2,1)}, bf16[336,1152]{1,0:T(8,128)(2,1)}, u32[]{:S(2)}, u32[]{:S(2)}) collective-permute-start(bf16[336,1152]{1,0:T(8,128)(2,1)} %collective-permute-done.5.refs_3_), channel_id=1, source_target_pairs={{0,1},{1,0},{16,17},{17,16},{2,3},{3,2},{18,19},{19,18},{32,33},{3... | collective-permute-start | bytes 2322440 | tf_op jit(solution)/shard_map/ppermute | solution.py:47
  24.2 12.6 %collective-permute-start.12 = (bf16[336,1152]{1,0:T(8,128)(2,1)S(1)}, bf16[336,1152]{1,0:T(8,128)(2,1)S(1)}, u32[]{:S(2)}, u32[]{:S(2)}) collective-permute-start(bf16[336,1152]{1,0:T(8,128)(2,1)S(1)} %collective-permute-done.4.refs_2_), channel_id=1, source_target_pairs={{0,1},{1,0},{16,17},{17,16},{2,3},{3,2},{18,19},{19,18},{32,33},{3... | collective-permute-start | bytes 2322440 | tf_op jit(solution)/shard_map/ppermute | solution.py:47
  24.2 13.6 %collective-permute-start.11 = (bf16[336,1152]{1,0:T(8,128)(2,1)S(1)}, bf16[336,1152]{1,0:T(8,128)(2,1)}, u32[]{:S(2)}, u32[]{:S(2)}) collective-permute-start(bf16[336,1152]{1,0:T(8,128)(2,1)S(1)} %collective-permute-done.3.refs_1_), channel_id=1, source_target_pairs={{0,1},{1,0},{16,17},{17,16},{2,3},{3,2},{18,19},{19,18},{32,33},{3... | collective-permute-start | bytes 2322440 | tf_op jit(solution)/shard_map/ppermute | solution.py:47
  30.4 18.7 %collective-permute-start.8 = (bf16[336,1152]{1,0:T(8,128)(2,1)}, bf16[336,1152]{1,0:T(8,128)(2,1)}, u32[]{:S(2)}, u32[]{:S(2)}) collective-permute-start(bf16[336,1152]{1,0:T(8,128)(2,1)} %collective-permute-done.5.refs_3_), channel_id=1, source_target_pairs={{0,4},{1,33},{16,20},{17,49},{2,6},{3,35},{18,22},{19,51},{32,36},... | collective-permute-start | bytes 2322440 | tf_op jit(solution)/shard_map/ppermute | solution.py:47
  32.4 16.7 %collective-permute-start.9 = (bf16[336,1152]{1,0:T(8,128)(2,1)}, bf16[336,1152]{1,0:T(8,128)(2,1)}, u32[]{:S(2)}, u32[]{:S(2)}) collective-permute-start(bf16[336,1152]{1,0:T(8,128)(2,1)} %collective-permute-done.6.refs_4_), channel_id=1, source_target_pairs={{0,16},{1,19},{16,0},{17,3},{2,18},{3,17},{18,2},{19,1},{32,48},{3... | collective-permute-start | bytes 2322440 | tf_op jit(solution)/shard_map/ppermute | solution.py:47
  34.0 15.2 %collective-permute-start.7 = (bf16[336,1152]{1,0:T(8,128)(2,1)}, bf16[336,1152]{1,0:T(8,128)(2,1)}, u32[]{:S(2)}, u32[]{:S(2)}) collective-permute-start(bf16[336,1152]{1,0:T(8,128)(2,1)} %collective-permute-done.5.refs_3_), channel_id=1, source_target_pairs={{0,12},{1,97},{16,28},{17,113},{2,14},{3,99},{18,30},{19,115},{32,... | collective-permute-start | bytes 2322440 | tf_op jit(solution)/shard_map/ppermute | solution.py:47
  36.8 13.0 %collective-permute-start.14 = (bf16[336,1152]{1,0:T(8,128)(2,1)}, bf16[336,1152]{1,0:T(8,128)(2,1)}, u32[]{:S(2)}, u32[]{:S(2)}) collective-permute-start(bf16[336,1152]{1,0:T(8,128)(2,1)} %collective-permute-done.6.refs_4_), channel_id=1, source_target_pairs={{0,1},{1,0},{16,17},{17,16},{2,3},{3,2},{18,19},{19,18},{32,33},{3... | collective-permute-start | bytes 2322440 | tf_op jit(solution)/shard_map/ppermute | solution.py:47
  80.1 4.7 %collective-permute-start.18 = (bf16[960,1152]{1,0:T(8,128)(2,1)}, bf16[960,1152]{1,0:T(8,128)(2,1)}, u32[]{:S(2)}, u32[]{:S(2)}) collective-permute-start(bf16[960,1152]{1,0:T(8,128)(2,1)} %get-tuple-element.33), channel_id=1, source_target_pairs={{0,1},{1,0},{16,17},{17,16},{2,3},{3,2},{18,19},{19,18},{32,33},{3... | collective-permute-start | bytes 6635528 | tf_op jit(solution)/shard_map/ppermute | solution.py:47
  84.8 10.6 %collective-permute-start.19 = (bf16[960,1152]{1,0:T(8,128)(2,1)}, bf16[960,1152]{1,0:T(8,128)(2,1)}, u32[]{:S(2)}, u32[]{:S(2)}) collective-permute-start(bf16[960,1152]{1,0:T(8,128)(2,1)} %get-tuple-element.34), channel_id=1, source_target_pairs={{0,1},{1,0},{16,17},{17,16},{2,3},{3,2},{18,19},{19,18},{32,33},{3... | collective-permute-start | bytes 6635528 | tf_op jit(solution)/shard_map/ppermute | solution.py:47
  85.0 8.0 %collective-permute-start.20 = (bf16[640,1152]{1,0:T(8,128)(2,1)}, bf16[640,1152]{1,0:T(8,128)(2,1)}, u32[]{:S(2)}, u32[]{:S(2)}) collective-permute-start(bf16[640,1152]{1,0:T(8,128)(2,1)} %get-tuple-element.37), channel_id=1, source_target_pairs={{0,1},{1,0},{16,17},{17,16},{2,3},{3,2},{18,19},{19,18},{32,33},{3... | collective-permute-start | bytes 4423688 | tf_op jit(solution)/shard_map/ppermute | solution.py:47
  88.0 12.4 %collective-permute-start.24 = (bf16[320,1152]{1,0:T(8,128)(2,1)}, bf16[320,1152]{1,0:T(8,128)(2,1)}, u32[]{:S(2)}, u32[]{:S(2)}) collective-permute-start(bf16[320,1152]{1,0:T(8,128)(2,1)} %get-tuple-element.43), channel_id=1, source_target_pairs={{0,16},{1,19},{16,0},{17,3},{2,18},{3,17},{18,2},{19,1},{32,48},{3... | collective-permute-start | bytes 2211848 | tf_op jit(solution)/shard_map/ppermute | solution.py:47
  90.2 12.6 %collective-permute-start.26 = (bf16[320,1152]{1,0:T(8,128)(2,1)}, bf16[320,1152]{1,0:T(8,128)(2,1)}, u32[]{:S(2)}, u32[]{:S(2)}) collective-permute-start(bf16[320,1152]{1,0:T(8,128)(2,1)} %get-tuple-element.46), channel_id=1, source_target_pairs={{0,4},{1,33},{16,20},{17,49},{2,6},{3,35},{18,22},{19,51},{32,36},... | collective-permute-start | bytes 2211848 | tf_op jit(solution)/shard_map/ppermute | solution.py:47
  91.5 11.3 %collective-permute-start.27 = (bf16[320,1152]{1,0:T(8,128)(2,1)}, bf16[320,1152]{1,0:T(8,128)(2,1)}, u32[]{:S(2)}, u32[]{:S(2)}) collective-permute-start(bf16[320,1152]{1,0:T(8,128)(2,1)} %get-tuple-element.47), channel_id=1, source_target_pairs={{0,12},{1,97},{16,28},{17,113},{2,14},{3,99},{18,30},{19,115},{32,... | collective-permute-start | bytes 2211848 | tf_op jit(solution)/shard_map/ppermute | solution.py:47
  95.3 15.0 %collective-permute-start.21 = (bf16[320,1152]{1,0:T(8,128)(2,1)}, bf16[320,1152]{1,0:T(8,128)(2,1)}, u32[]{:S(2)}, u32[]{:S(2)}) collective-permute-start(bf16[320,1152]{1,0:T(8,128)(2,1)} %get-tuple-element.38), channel_id=1, source_target_pairs={{0,4},{1,33},{16,20},{17,49},{2,6},{3,35},{18,22},{19,51},{32,36},... | collective-permute-start | bytes 2211848 | tf_op jit(solution)/shard_map/ppermute | solution.py:47
  95.4 14.9 %collective-permute-start.22 = (bf16[320,1152]{1,0:T(8,128)(2,1)}, bf16[320,1152]{1,0:T(8,128)(2,1)}, u32[]{:S(2)}, u32[]{:S(2)}) collective-permute-start(bf16[320,1152]{1,0:T(8,128)(2,1)} %get-tuple-element.39), channel_id=1, source_target_pairs={{0,12},{1,97},{16,28},{17,113},{2,14},{3,99},{18,30},{19,115},{32,... | collective-permute-start | bytes 2211848 | tf_op jit(solution)/shard_map/ppermute | solution.py:47
  105.3 12.1 %collective-permute-start.28 = (bf16[320,1152]{1,0:T(8,128)(2,1)}, bf16[320,1152]{1,0:T(8,128)(2,1)}, u32[]{:S(2)}, u32[]{:S(2)}) collective-permute-start(bf16[320,1152]{1,0:T(8,128)(2,1)} %add.1), channel_id=1, source_target_pairs={{0,16},{1,19},{16,0},{17,3},{2,18},{3,17},{18,2},{19,1},{32,48},{3... | collective-permute-start | bytes 2211848 | tf_op jit(solution)/shard_map/ppermute | solution.py:47
  107.2 12.4 %collective-permute-start.25 = (bf16[320,1152]{1,0:T(8,128)(2,1)}, bf16[320,1152]{1,0:T(8,128)(2,1)}, u32[]{:S(2)}, u32[]{:S(2)}) collective-permute-start(bf16[320,1152]{1,0:T(8,128)(2,1)} %join.7), channel_id=1, source_target_pairs={{0,8},{1,65},{16,24},{17,81},{2,10},{3,67},{18,26},{19,83},{32,40}... | collective-permute-start | bytes 2211848 | tf_op jit(solution)/shard_map/ppermute | solution.py:47
  113.2 8.8 %collective-permute-start.23 = (f32[160,1152]{1,0:T(8,128)}, f32[160,1152]{1,0:T(8,128)}, u32[]{:S(2)}, u32[]{:S(2)}) collective-permute-start(f32[160,1152]{1,0:T(8,128)} %get-tuple-element.41), channel_id=1, source_target_pairs={{0,1},{1,0},{16,17},{17,16},{2,3},{3,2},{18,19},{19,18},{32,33},{3... | collective-permute-start | bytes 2211848 | tf_op jit(solution)/shard_map/ppermute | solution.py:47
  117.4 4.7 %collective-permute-start.30 = (bf16[320,1152]{1,0:T(8,128)(2,1)}, bf16[320,1152]{1,0:T(8,128)(2,1)}, u32[]{:S(2)}, u32[]{:S(2)}) collective-permute-start(bf16[320,1152]{1,0:T(8,128)(2,1)} %collective-permute-done.28.last), channel_id=1, source_target_pairs={{0,1},{1,0},{16,17},{17,16},{2,3},{3,2},{18,19},{19,18},{32,33},{3... | collective-permute-start | bytes 2211848 | tf_op jit(solution)/shard_map/ppermute | solution.py:47
  (10 other events, 37.7 us)
